TPU v7x, 128 devices: a whole 4x4x4 slice. The times are simulated.
128 devices in a mesh: ma: 32 (over z, x, core), col: 4 (over y).
Axes of the slice: x: 4, y: 4, z: 4, core: 2. Of those that a mesh axis runs over, the one named last changes fastest.
Arguments:
- pred_four: bfloat16 [40, 2, 2, 1024, 1024], P('col', None, None, 'ma'), may hold values from -6 to 6
- target_four: bfloat16 [40, 2, 2, 1024, 1024], P('col', None, None, 'ma'), may hold values from -6 to 6
- legendre: bfloat16 [512, 1025, 1024], P(('ma', 'col')), may hold values from -0.1875 to 0.1875
- pair_order: int32 [512], replicated, may hold values from 0 to 511, each once
Outputs:
- grad_four: bfloat16 [40, 2, 2, 1024, 1024], P('col', None, None, 'ma')
Inputs may be any that keep to these rules, and one draw needn't show every extreme that they name: Each of 0 to 511 appears once; pair slot p holds the orders pair_order[p] and 1023 - pair_order[p].
All inputs are finite; a program needn't handle non-finite values.
Results may differ from a plain program's by a relative error of at most 0.0015.
The roundings to bfloat16 on the way count: a program that leaves them out, or rounds other values in their place, can miss the bound.
Values may be sent and summed in bfloat16 or wider, within the bound.
No kernel may reach another device: no remote copies, remote signals or barrier semaphores. Data moves between devices by JAX's collectives and lax.ppermute only.
A program may use at most 192 MiB of HBM per device.

v0:
```python
import jax
import jax.numpy as jnp
from jax import lax
from jax.sharding import PartitionSpec as P

DEGREES = 1024


POWER_FLOOR = 0.5


def degree_loss(power_pred, power_true, cross_power):
    pred_floor = jnp.maximum(power_pred, POWER_FLOOR)
    true_floor = jnp.maximum(power_true, POWER_FLOOR)
    root_pred = jnp.sqrt(pred_floor)
    root_true = jnp.sqrt(true_floor)
    upper_mean = (pred_floor * pred_floor + true_floor * true_floor) / (pred_floor + true_floor)
    coherence = cross_power / (root_pred * root_true)
    spread = root_pred - root_true
    return jnp.sum(spread * spread + 2.0 * upper_mean * (1.0 - coherence))


def loss_factors(moments):
    dpower, dcross = jax.grad(degree_loss, argnums=(0, 2))(
        moments[:, 0], moments[:, 1], moments[:, 2]
    )
    return jnp.stack([2.0 * dpower, dcross], axis=1)


def coeff_moments(coeffs, group_count):
    shaped = coeffs.reshape(coeffs.shape[:-1] + (2, group_count, 2))
    predicted = shaped[..., 0, :, :]
    observed = shaped[..., 1, :, :]
    return jnp.stack(
        [
            jnp.sum(predicted * predicted, -1),
            jnp.sum(observed * observed, -1),
            jnp.sum(predicted * observed, -1),
        ],
        axis=-2,
    )


def place_degrees(values, lower_order):
    upper_order = DEGREES - 1 - lower_order
    tail = values.shape[1:]
    padded = jnp.concatenate([jnp.zeros((DEGREES,) + tail, jnp.float32), values[:DEGREES]], axis=0)
    lower_part = lax.dynamic_slice_in_dim(padded, DEGREES - lower_order, DEGREES, 0)
    degree_index = jnp.arange(DEGREES, dtype=jnp.int32)
    upper_mask = (degree_index >= upper_order).reshape((DEGREES,) + (1,) * len(tail))
    upper_part = jnp.where(upper_mask, values[1:], jnp.zeros_like(values[1:]))
    lower_weight = jnp.where(lower_order == 0, 1.0, 2.0)
    return lower_weight * lower_part + 2.0 * upper_part


def spread_factors(factors, lower_order):
    tail = factors.shape[1:]
    padded = jnp.concatenate([factors, jnp.zeros((DEGREES + 1,) + tail, jnp.float32)], axis=0)
    lower_part = lax.dynamic_slice_in_dim(padded, lower_order, DEGREES + 1, 0)
    upper_part = jnp.concatenate([jnp.zeros((1,) + tail, jnp.float32), factors], axis=0)
    row_index = jnp.arange(DEGREES + 1, dtype=jnp.int32)
    lower_rows = (row_index < DEGREES - lower_order).reshape((DEGREES + 1,) + (1,) * len(tail))
    lower_weight = jnp.where(lower_order == 0, 1.0, 2.0)
    return jnp.where(lower_rows, lower_weight * lower_part, 2.0 * upper_part)


def grad_from(coeffs, row_factors, group_count):
    shaped = coeffs.reshape(coeffs.shape[:-1] + (2, group_count, 2))
    predicted = shaped[..., 0, :, :]
    observed = shaped[..., 1, :, :]
    combined = row_factors[..., 0, :, None] * predicted + row_factors[..., 1, :, None] * observed
    combined = combined.astype(jnp.bfloat16)
    return combined.reshape(combined.shape[:-2] + (2 * group_count,))


def per_device(pred_four, target_four, legendre, pair_order):
    channels_dev, samples, complex_parts, lat_dev, degrees = pred_four.shape
    pairs_dev, row_count, lat_count = legendre.shape
    slot_count = 2 * pairs_dev
    slot_orders = jnp.stack([pair_order, degrees - 1 - pair_order], axis=1).reshape(degrees)
    order_index = jnp.arange(degrees, dtype=jnp.int32)
    permuter = (slot_orders[:, None] == order_index[None, :]).astype(jnp.bfloat16)
    both_fields = jnp.stack([pred_four, target_four])
    outgoing = jnp.einsum(
        "fcsqkm,nm->nfcsqk", both_fields, permuter, preferred_element_type=jnp.float32
    ).astype(jnp.bfloat16)
    arrived = lax.all_to_all(
        lax.all_to_all(outgoing, "ma", split_axis=0, concat_axis=5, tiled=True),
        "col",
        split_axis=0,
        concat_axis=2,
        tiled=True,
    )
    channels = arrived.shape[2]
    group_count = channels * samples
    field_rows = 4 * group_count
    by_pair = arrived.reshape(pairs_dev, 2, field_rows, lat_count)
    device = lax.axis_index(("ma", "col"))
    lower_order = lax.dynamic_slice_in_dim(pair_order, device * pairs_dev, pairs_dev)
    boundary = degrees - lower_order
    row_index = jnp.arange(row_count, dtype=jnp.int32)
    products = jnp.einsum("pjk,pork->pojr", legendre, by_pair, preferred_element_type=jnp.float32)
    coeffs = jnp.where(
        row_index[None, :, None] < boundary[:, None, None], products[:, 0], products[:, 1]
    )
    moments = coeff_moments(coeffs, group_count)
    partial_sums = jnp.sum(jax.vmap(place_degrees)(moments, lower_order), axis=0)
    totals = lax.psum(partial_sums, ("ma", "col"))
    factors = loss_factors(totals)
    row_factors = jax.vmap(spread_factors, in_axes=(None, 0))(factors, lower_order)
    grad_rows = grad_from(coeffs, row_factors, group_count)
    lower_rows = (row_index[None, :] < boundary[:, None])[:, :, None]
    blank = jnp.zeros_like(grad_rows)
    split_grad = jnp.stack(
        [jnp.where(lower_rows, grad_rows, blank), jnp.where(lower_rows, blank, grad_rows)], axis=1
    )
    synthesis = jnp.einsum(
        "pjk,pojr->pork", legendre, split_grad, preferred_element_type=jnp.float32
    )
    going_home = synthesis.astype(jnp.bfloat16).reshape(slot_count, channels, samples, 2, lat_count)
    returned = lax.all_to_all(
        lax.all_to_all(going_home, "col", split_axis=1, concat_axis=0, tiled=True),
        "ma",
        split_axis=4,
        concat_axis=0,
        tiled=True,
    )
    ordered = jnp.einsum("ncsqk,nm->csqkm", returned, permuter, preferred_element_type=jnp.float32)
    return ordered.astype(jnp.bfloat16)


def solution(mesh):
    placed = (
        P("col", None, None, "ma", None),
        P("col", None, None, "ma", None),
        P(("ma", "col"), None, None),
        P(),
    )
    return jax.shard_map(
        per_device,
        mesh=mesh,
        in_specs=placed,
        out_specs=P("col", None, None, "ma", None),
        check_vma=False,
    )
```

profile of v0, /device:TPU:1, one launch (start us, length us, event | category | flops | bytes accessed | tf_op | source)
XLA Modules:
  0.0 821.2 jit_solution(627821815072670636)
XLA Ops:
  8.2 10.5 %fusion.19 = bf16[1024,2,10,2,2,32]{0,5,4,3,2,1:T(8,128)(2,1)} fusion(bf16[1,10,2,2,32,1024]{5,4,3,2,1,0:T(8,128)(2,1)} %bitcast.120, bf16[1,10,2,2,32,1024]{5,4,3,2,1,0:T(8,128)(2,1)} %bitcast.121, s32[1024]{0:T(1024)S(1)} %eq.24), kind=kOutput, calls=%fused_computation.27 | convolution fusion | flops 5382864896 | bytes 10489856 | tf_op jit(solution)/shard_map/fcsqkm,nm->nfcsqk/dot_general | solution.py:84
  18.7 41.2 %copy.40 = bf16[1024,2,10,2,2,32]{5,4,3,2,1,0:T(2,128)(2,1)} copy(bf16[1024,2,10,2,2,32]{0,5,4,3,2,1:T(8,128)(2,1)} %fusion.19) | data formatting | bytes 10485760 | tf_op jit(solution)/shard_map/convert_element_type | solution.py:86
  59.9 30.9 %reshape.218 = bf16[32,2,40960]{2,1,0:T(2,128)(2,1)} reshape(bf16[1024,2,10,2,2,32]{5,4,3,2,1,0:T(2,128)(2,1)} %copy.40) | data formatting | bytes 10485760
  90.8 72.1 %all_to_all.69 = bf16[32,2,40960]{2,1,0:T(2,128)(2,1)} all-to-all(bf16[32,2,40960]{2,1,0:T(2,128)(2,1)} %reshape.218), channel_id=1, replica_groups=mesh['ma'=32,'col'=4] {'ma'}, dimensions={0} | all-to-all | bytes 10485760 | tf_op jit(solution)/shard_map/all_to_all | solution.py:88
  162.9 26.4 %reshape.219 = bf16[1024,2,10,2,2,32]{5,4,3,2,1,0:T(2,128)(2,1)} reshape(bf16[32,2,40960]{2,1,0:T(2,128)(2,1)} %all_to_all.69) | data formatting | bytes 10485760
  189.3 22.8 %copy.95 = bf16[32,32,2,10,2,2,32]{6,0,1,5,4,3,2:T(8,128)(2,1)} copy(bf16[32,32,2,10,2,2,32]{6,5,4,3,2,1,0:T(2,128)(2,1)} %bitcast.104) | data formatting | bytes 10485760 | tf_op jit(solution)/shard_map/all_to_all | solution.py:88
  212.2 28.7 %all_to_all.53 = bf16[32,2,10,2,2,1024]{5,0,4,3,2,1:T(8,128)(2,1)} reshape(bf16[32,2,10,2,2,32,32]{6,5,0,4,3,2,1:T(8,128)(2,1)} %bitcast.105) | data formatting | bytes 10485760 | tf_op jit(solution)/shard_map/all_to_all | solution.py:88
  240.9 10.2 %copy.42 = bf16[32,2,10,2,2,1024]{5,4,3,2,1,0:T(2,128)(2,1)} copy(bf16[32,2,10,2,2,1024]{5,0,4,3,2,1:T(8,128)(2,1)} %all_to_all.53) | data formatting | bytes 10485760 | tf_op jit(solution)/shard_map/all_to_all | solution.py:88
  257.5 58.5 %all-to-all-done.1 = bf16[32,2,10,2,2,1024]{5,4,3,2,1,0:T(2,128)(2,1)} async-done(((bf16[32,2,10,2,2,1024]{5,4,3,2,1,0:T(2,128)(2,1)}), bf16[32,2,10,2,2,1024]{5,4,3,2,1,0:T(2,128)(2,1)}, u32[]{:S(2)}, u32[]{:S(2)}) %all-to-all-start.1) | async-done | bytes 5242912 | tf_op jit(solution)/shard_map/all_to_all | solution.py:87
  316.0 10.4 %copy.97 = bf16[32,2,10,2,2,1024]{5,0,4,3,2,1:T(8,128)(2,1)} copy(bf16[32,2,10,2,2,1024]{5,4,3,2,1,0:T(2,128)(2,1)} %all-to-all-done.1) | data formatting | bytes 10485760 | tf_op jit(solution)/shard_map/all_to_all | solution.py:87
  326.4 10.2 %copy.44 = bf16[8,2,4,10,2,2,1024]{6,5,4,3,2,1,0:T(2,128)(2,1)} copy(bf16[8,2,4,10,2,2,1024]{6,0,2,5,4,3,1:T(8,128)(2,1)} %bitcast.109) | data formatting | bytes 10485760 | tf_op jit(solution)/shard_map/all_to_all | solution.py:87
  336.6 8.9 %reshape.162 = bf16[4,2,320,1024]{3,2,1,0:T(8,128)(2,1)} reshape(bf16[8,2,4,10,2,2,1024]{6,5,4,3,2,1,0:T(2,128)(2,1)} %copy.44) | data formatting | bytes 10485760 | tf_op jit(solution)/shard_map/reshape | solution.py:97
  345.5 18.6 %fusion.4 = f32[4,2,1025,320]{2,3,1,0:T(8,128)} fusion(bf16[4,2,320,1024]{3,2,1,0:T(8,128)(2,1)} %reshape.162, bf16[4,1025,1024,1]{2,0,1,3:T(4,128)(2,1)} %bitcast.118), kind=kOutput, calls=%fused_computation.11 | convolution fusion | flops 5373952000 | bytes 24135680 | tf_op jit(solution)/shard_map/pjk,pork->pojr/dot_general | solution.py:102
  364.1 9.6 %fusion.45 = (f32[4,1,1025,320]{2,3,1,0:T(8,128)}, f32[4,1,1025,320]{2,3,1,0:T(8,128)}) fusion(f32[4,2,1025,320]{2,3,1,0:T(8,128)} %fusion.4), kind=kLoop, calls=%fused_computation.71 | loop fusion | bytes 20992000 | tf_op jit(solution)/shard_map/slice | solution.py:104
  373.7 7.8 squeeze.18
  381.4 8.1 squeeze.8
  389.6 10.0 %broadcast_select_fusion = f32[4,1025,2,80,2]{1,4,3,2,0:T(2,128)} fusion(f32[4,1025,2,80,2]{1,4,3,2,0:T(2,128)} %squeeze.8, f32[4,1025,2,80,2]{1,4,3,2,0:T(2,128)} %squeeze.18, pred[4,1025]{1,0:T(4,128)(4,1)S(1)} %iota_compare_fusion.1), kind=kLoop, calls=%fused_computation.12 | loop fusion | flops 1312000 | bytes 15748100 | tf_op jit(solution)/shard_map/jit(_where)/select_n | solution.py:103
  399.6 16.2 %multiply_reduce_fusion.2 = (f32[4,1025,80]{1,2,0:T(8,128)S(1)}, f32[4,1025,80]{1,2,0:T(8,128)S(1)}, f32[4,1025,80]{1,2,0:T(8,128)S(1)}, f32[4,1025,1,80,2]{1,4,3,2,0:T(2,128)}, f32[4,1025,1,80,2]{1,4,3,2,0:T(2,128)S(1)}) fusion(f32[4,1025,2,80,2]{1,4,3,2,0:T(2,128)} %broadcast_select_fusion), kind=kLoop, calls=%fused_computation.35 | loop fusion | flops 2952000 | bytes 14432000 | tf_op jit(solution)/shard_map/reduce_sum | solution.py:36
  422.6 18.1 %while.4 = (s32[]{:T(128)}, f32[4,2048,3,80]{1,3,2,0:T(8,128)}, s32[4,4]{1,0:T(4,128)S(1)}, f32[4,1024,3,80]{1,3,2,0:T(8,128)}) while((s32[]{:T(128)}, f32[4,2048,3,80]{1,3,2,0:T(8,128)}, s32[4,4]{1,0:T(4,128)S(1)}, f32[4,1024,3,80]{1,3,2,0:T(8,128)}) %tuple.56), condition=%wide.while_cond.clone, body=%wide.while_body.sunk.clone | while | flops 2 | bytes 1967721 | solution.py:48
  440.6 5.6 fusion.18
  446.3 5.1 squeeze.19
  454.6 135.0 %all-reduce.7.cloned.1.call-done = f32[1024,3,80]{0,2,1:T(8,128)} async-done(((f32[1024,3,80]{0,2,1:T(8,128)}), f32[1024,3,80]{0,2,1:T(8,128)}) %all-reduce.7.cloned.1.call-update) | async-done | bytes 983056 | tf_op jit(solution)/shard_map/psum | solution.py:108
  592.7 13.6 %while.5 = (s32[]{:T(128)}, f32[2049,2,80]{0,2,1:T(8,128)S(1)}, s32[4,3]{1,0:T(4,128)S(1)}, f32[4,1025,2,80]{1,3,2,0:T(8,128)}) while((s32[]{:T(128)}, f32[2049,2,80]{0,2,1:T(8,128)S(1)}, s32[4,3]{1,0:T(4,128)S(1)}, f32[4,1025,2,80]{1,3,2,0:T(8,128)}) %tuple.59), condition=%wide.while_cond.1.clone, body=%wide.while_body.1.sunk.clone | while | flops 2 | bytes 5329877 | solution.py:59
  618.2 5.5 mul.198
  628.1 11.1 %fusion.29 = bf16[4,2,160,1024]{3,2,1,0:T(8,128)(2,1)} fusion(bf16[4,1025,1024,1]{2,0,1,3:T(4,128)(2,1)} %bitcast.119, bf16[4,1,1025,160]{2,3,1,0:T(8,128)(2,1)S(1)} %broadcast_select_fusion.1, bf16[4,1,1025,160]{2,3,1,0:T(8,128)(2,1)S(1)} %get-tuple-element.72), kind=kOutput, calls=%fused_computation.39 | convolution fusion | flops 2689598720 | bytes 13642240 | tf_op jit(solution)/shard_map/pjk,pojr->pork/dot_general | solution.py:117
  645.8 33.1 %all_to_all.70 = bf16[8,40,2,2,1024]{4,0,3,2,1:T(8,128)(2,1)S(1)} all-to-all(bf16[8,40,2,2,1024]{4,0,3,2,1:T(8,128)(2,1)S(1)} %copy.54), channel_id=1, replica_groups=mesh['ma'=32,'col'=4] {'col'}, dimensions={1} | all-to-all | bytes 5242880 | tf_op jit(solution)/shard_map/all_to_all | solution.py:122
  679.2 16.2 %copy.56 = bf16[32,10,2,2,1024]{0,3,2,1,4:T(2,128)(2,1)} copy(bf16[32,10,2,2,1024]{4,0,3,2,1:T(8,128)(2,1)S(1)} %bitcast.111) | data formatting | bytes 5242880 | tf_op jit(solution)/shard_map/all_to_all | solution.py:122
  695.4 21.0 %reshape.220 = bf16[32,2,20480]{2,1,0:T(2,128)(2,1)S(1)} reshape(bf16[1024,10,2,2,32]{4,3,2,1,0:T(2,128)(2,1)} %bitcast.106) | data formatting | bytes 5242880
  716.4 42.2 %all_to_all.71 = bf16[32,2,20480]{2,1,0:T(2,128)(2,1)} all-to-all(bf16[32,2,20480]{2,1,0:T(2,128)(2,1)S(1)} %reshape.220), channel_id=1, replica_groups=mesh['ma'=32,'col'=4] {'ma'}, dimensions={0} | all-to-all | bytes 5242880 | tf_op jit(solution)/shard_map/all_to_all | solution.py:121
  758.6 22.7 %reshape.221 = bf16[1024,10,2,2,32]{4,3,2,1,0:T(2,128)(2,1)} reshape(bf16[32,2,20480]{2,1,0:T(2,128)(2,1)} %all_to_all.71) | data formatting | bytes 5242880
  781.3 14.5 %copy.96 = bf16[32,10,2,2,32,32]{0,4,5,3,2,1:T(8,128)(2,1)} copy(bf16[32,10,2,2,32,32]{0,3,2,1,5,4:T(2,128)(2,1)} %bitcast.107) | data formatting | bytes 5242880 | tf_op jit(solution)/shard_map/all_to_all | solution.py:121
  795.8 13.9 %all_to_all.64 = bf16[1024,10,2,2,32]{0,4,3,2,1:T(8,128)(2,1)S(1)} reshape(bf16[32,32,10,2,2,32]{1,0,5,4,3,2:T(8,128)(2,1)} %bitcast.108) | data formatting | bytes 5242880 | tf_op jit(solution)/shard_map/all_to_all | solution.py:121
  (78 shorter events, 80.1 us)
Async XLA Ops:
  8.2 10.5 %copy-start.2 = (s32[1024]{0:T(1024)}, s32[1024]{0:T(1024)S(1)}, u32[]{:S(2)}) copy-start(s32[1024]{0:T(1024)S(1)} %eq.24) | copy-start | bytes 12292
  251.1 64.9 %all-to-all-start.1 = ((bf16[32,2,10,2,2,1024]{5,4,3,2,1,0:T(2,128)(2,1)}), bf16[32,2,10,2,2,1024]{5,4,3,2,1,0:T(2,128)(2,1)}, u32[]{:S(2)}, u32[]{:S(2)}) async-start(bf16[32,2,10,2,2,1024]{5,4,3,2,1,0:T(2,128)(2,1)} %copy.42), calls=%async_computation.1 | async-start | bytes 10485760 | tf_op jit(solution)/shard_map/all_to_all | solution.py:87
  256.2 333.4 %all-reduce.7.cloned.1.call-start = ((), (), s32[]{:S(2)}) async-start(), calls=%async_computation.4 | async-start | bytes 1966080 | tf_op jit(solution)/shard_map/psum | solution.py:108
  416.1 2.1 copy-start
  618.2 5.5 copy-start.1
  795.8 13.9 %copy-start.3 = (s32[1024]{0:T(1024)S(1)}, s32[1024]{0:T(1024)}, u32[]{:S(2)}) copy-start(s32[1024]{0:T(1024)} %copy-done.2) | copy-start | bytes 12292
Sparse Core Ops, SparseCore 0:
  446.3 143.2 all-reduce.6
where the time goes:
time: 831 us; the launch traced here: 821 us
  local copies, waits for them, and re-layouts  372 us (45%)
  waiting for transfers between devices  194 us (23%)
  blocking collectives  147 us (18%)
  matrix products  44.6 us (5%)
  other arithmetic  44.1 us (5%)
  between operations  13.8 us (2%)
    psum x1, waiting for transfers between devices, per_device(): totals = lax.psum(partial_sums, ('ma', 'col'))  135 us
    unnamed x15, local copies, waits for them, and re-layouts  103 us
    all_to_all x1, blocking collectives, per_device(): lax.all_to_all(outgoing, 'ma', split_axis=0, concat_axis=5, tiled=True)  72.1 us
    all_to_all x3, local copies, waits for them, and re-layouts, per_device(): lax.all_to_all(outgoing, 'ma', split_axis=0, concat_axis=5, tiled=True)  61.8 us
    all_to_all x1, waiting for transfers between devices, per_device(): lax.all_to_all(lax.all_to_all(outgoing, 'ma', split_axis=0, concat_axis=5...  58.5 us
    all_to_all x1, blocking collectives, per_device(): lax.all_to_all(lax.all_to_all(going_home, 'col', split_axis=1, concat_axi...  42.2 us
    convert_element_type x1, local copies, waits for them, and re-layouts, per_device(): outgoing = jnp.einsum('fcsqkm,nm->nfcsqk', both_fields, permuter, preferr...  41.2 us
    all_to_all x1, blocking collectives, per_device(): lax.all_to_all(going_home, 'col', split_axis=1, concat_axis=0, tiled=True)  33.1 us
  transfers between devices with their start and end apart: 2, of which 2 were waited for; matrix products, arithmetic and copies ran while one was open for 1% of the time, Pallas kernels for 0%

commit v1 on v0

v1 whole, which is shorter than its diff:
```python
import functools

import jax
import jax.numpy as jnp
from jax import lax
from jax.experimental import pallas as pl
from jax.experimental.pallas import tpu as pltpu
from jax.sharding import PartitionSpec as P

DEGREES = 1024
HALF = DEGREES // 2
POWER_FLOOR = 0.5
LANES = 128
SLOTS = 8
AXES = ("ma", "col")
PARTS = (10,)
VMEM_LIMIT = 56 * 1024 * 1024


def round_up(value, multiple):
    return -(-value // multiple) * multiple


def dot_nt(left, right):
    return lax.dot_general(left, right, (((1,), (1,)), ((), ())), preferred_element_type=jnp.float32)


def dot_nn(left, right):
    return lax.dot_general(left, right, (((1,), (0,)), ((), ())), preferred_element_type=jnp.float32)


def swap_groups(blocks):
    lane = lax.broadcasted_iota(jnp.int32, blocks[0].shape, 1)
    low_half = lane < 64
    even = (lane & 32) == 0
    first = [None] * 4
    for i in (0, 1):
        upper, lower = blocks[i], blocks[i + 2]
        first[i] = jnp.where(low_half, upper, pltpu.roll(lower, 64, 1))
        first[i + 2] = jnp.where(low_half, pltpu.roll(upper, 64, 1), lower)
    result = []
    for i in (0, 2):
        upper, lower = first[i], first[i + 1]
        result.append(jnp.where(even, upper, pltpu.roll(lower, 32, 1)))
        result.append(jnp.where(even, pltpu.roll(upper, 96, 1), lower))
    return result


def pack_kernel(perm_ref, pred_ref, target_ref, out_ref):
    for f, field_ref in enumerate((pred_ref, target_ref)):
        field = field_ref[...].reshape(2 * LANES, DEGREES)
        by_slot = dot_nt(perm_ref[...], field)
        both = [
            by_slot[:, c * LANES : (c + 1) * LANES].reshape(DEGREES // SLOTS, SLOTS, LANES)
            for c in range(2)
        ]
        out_ref[:, f, 0] = jnp.concatenate(both, axis=1).astype(jnp.bfloat16)


def pack(perm, pred, target, first, count):
    devices = DEGREES // SLOTS
    field_spec = pl.BlockSpec((2, 2, 2, 32, DEGREES), lambda i: (first // 2 + i, 0, 0, 0, 0))
    return pl.pallas_call(
        pack_kernel,
        grid=(count // 2,),
        in_specs=[pl.BlockSpec((DEGREES, DEGREES), lambda i: (0, 0)), field_spec, field_spec],
        out_specs=pl.BlockSpec((devices, 2, 1, 16, LANES), lambda i: (0, 0, i, 0, 0)),
        out_shape=jax.ShapeDtypeStruct((devices, 2, count // 2, 16, LANES), jnp.bfloat16),
        compiler_params=pltpu.CompilerParams(vmem_limit_bytes=VMEM_LIMIT),
        cost_estimate=pl.CostEstimate(
            flops=2 * DEGREES * DEGREES * 2 * LANES * count,
            bytes_accessed=2 * DEGREES * DEGREES + 8 * LANES * DEGREES * count,
            transcendentals=0,
        ),
        name="pack",
    )(perm, pred, target)


def moments_of(values, rows):
    width = values.shape[-1]
    shaped = values.reshape(4, 2, rows, width)
    pieces = []
    for left, right in ((0, 0), (1, 1), (0, 1)):
        for s in range(2):
            real = shaped[2 * s, left] * shaped[2 * s, right]
            imag = shaped[2 * s + 1, left] * shaped[2 * s + 1, right]
            pieces.append(real + imag)
    return jnp.concatenate(pieces, axis=0)


def analysis_kernel(
    count, order_ref, arrived_ref, leg_ref, coef_ref, last_ref, moment_ref,
    wide_ref, field_ref, raw_ref, total_ref,
):
    p = pl.program_id(0)
    rows = 4 * count

    @pl.when(p == 0)
    def _():
        def widen(j, carry):
            for f in range(2):
                block = arrived_ref[j, :, f].reshape(rows * SLOTS, LANES)
                wide_ref[f, j] = block.astype(jnp.float32)
            return carry

        lax.fori_loop(0, 32, widen, 0)
        total_ref[...] = jnp.zeros_like(total_ref)

    for t in range(2):
        slot = 2 * p + t
        for tile in range(8):
            blocks = []
            for i in range(4):
                fields = [
                    wide_ref[f, 4 * tile + i, pl.ds(slot, rows, stride=SLOTS), :] for f in range(2)
                ]
                blocks.append(jnp.concatenate(fields, axis=0))
            for g, block in enumerate(swap_groups(blocks)):
                field_ref[t, g * 2 * rows : (g + 1) * 2 * rows, tile * LANES : (tile + 1) * LANES] = (
                    block.astype(jnp.bfloat16)
                )

    lower_order = order_ref[p]
    boundary = DEGREES - lower_order
    width = 256
    for tile in range(DEGREES // width):
        start = tile * width
        leg = leg_ref[0, start : start + width, :]
        values = dot_nt(field_ref[0], leg)
        if start >= HALF:
            upper = dot_nt(field_ref[1], leg)
            row = lax.broadcasted_iota(jnp.int32, values.shape, 1) + start
            values = jnp.where(row < boundary, values, upper)
        coef_ref[0, :, start : start + width] = values
        raw_ref[:, start : start + width] = moments_of(values, rows)
    last_leg = jnp.broadcast_to(leg_ref[0, DEGREES : DEGREES + 1, :].astype(jnp.float32), (LANES, DEGREES))
    last = dot_nt(field_ref[1], last_leg.astype(jnp.bfloat16))
    last_ref[0] = last
    last_moments = moments_of(last, rows)

    lower_weight = jnp.where(lower_order == 0, 1.0, 2.0)
    step = 2 * rows
    for k in range(3):
        raw = raw_ref[k * step : (k + 1) * step, :]
        tail = last_moments[k * step : (k + 1) * step]
        degree = lax.broadcasted_iota(jnp.int32, raw.shape, 1)
        lower = jnp.where(degree >= lower_order, pltpu.roll(raw, lower_order, 1), 0.0)
        upper = pltpu.roll(raw, DEGREES - 1, 1)
        upper = jnp.where(degree == DEGREES - 1, jnp.concatenate([tail] * 8, axis=1), upper)
        upper = jnp.where(degree >= DEGREES - 1 - lower_order, upper, 0.0)
        total_ref[k * step : (k + 1) * step, :] += lower_weight * lower + 2.0 * upper

    @pl.when(p == pl.num_programs(0) - 1)
    def _():
        moment_ref[...] = total_ref[...].T


def analysis(lower_order, arrived, legendre, count):
    pairs, leg_rows, _ = legendre.shape
    rows = 32 * count
    lanes = round_up(24 * count, LANES)
    grid_spec = pltpu.PrefetchScalarGridSpec(
        num_scalar_prefetch=1,
        grid=(pairs,),
        in_specs=[
            pl.BlockSpec((32, 4, 2, count * SLOTS, LANES), lambda p, o: (0, 0, 0, 0, 0)),
            pl.BlockSpec((1, leg_rows, DEGREES), lambda p, o: (p, 0, 0)),
        ],
        out_specs=[
            pl.BlockSpec((1, rows, DEGREES), lambda p, o: (p, 0, 0)),
            pl.BlockSpec((1, rows, LANES), lambda p, o: (p, 0, 0)),
            pl.BlockSpec((DEGREES, lanes), lambda p, o: (0, 0)),
        ],
        scratch_shapes=[
            pltpu.VMEM((2, 32, rows, LANES), jnp.float32),
            pltpu.VMEM((2, rows, DEGREES), jnp.bfloat16),
            pltpu.VMEM((24 * count, DEGREES), jnp.float32),
            pltpu.VMEM((lanes, DEGREES), jnp.float32),
        ],
    )
    return pl.pallas_call(
        functools.partial(analysis_kernel, count),
        grid_spec=grid_spec,
        out_shape=[
            jax.ShapeDtypeStruct((pairs, rows, DEGREES), jnp.float32),
            jax.ShapeDtypeStruct((pairs, rows, LANES), jnp.float32),
            jax.ShapeDtypeStruct((DEGREES, lanes), jnp.float32),
        ],
        compiler_params=pltpu.CompilerParams(vmem_limit_bytes=VMEM_LIMIT),
        cost_estimate=pl.CostEstimate(
            flops=3 * pairs * rows * DEGREES * DEGREES,
            bytes_accessed=2 * legendre.size + 4 * pairs * rows * DEGREES + 2 * arrived.size,
            transcendentals=0,
        ),
        name="analysis",
    )(lower_order, arrived.reshape(32, 4, 2, count * SLOTS, LANES), legendre)


def factor_kernel(count, parts_ref, out_ref):
    total = jnp.sum(parts_ref[...], axis=0)
    size = total.shape[1]
    span = 8 * count
    power_pred = total
    power_true = pltpu.roll(total, size - span, 1)
    cross = pltpu.roll(total, size - 2 * span, 1)
    pred = jnp.maximum(power_pred, POWER_FLOOR)
    true = jnp.maximum(power_true, POWER_FLOOR)
    root_pred = jnp.sqrt(pred)
    root_true = jnp.sqrt(true)
    both = pred + true
    upper_mean = (pred * pred + true * true) / both
    inverse = 1.0 / (root_pred * root_true)
    coherence = cross * inverse
    mean_slope = (2.0 * pred - upper_mean) / both
    slope = (
        (root_pred - root_true) / root_pred
        + 2.0 * mean_slope * (1.0 - coherence)
        + upper_mean * coherence / pred
    )
    binds = jnp.where(power_pred > POWER_FLOOR, 1.0, jnp.where(power_pred == POWER_FLOOR, 0.5, 0.0))
    dpower = 2.0 * slope * binds
    dcross = -2.0 * upper_mean * inverse
    lane = lax.broadcasted_iota(jnp.int32, total.shape, 1)
    factors = jnp.where(lane < span, dpower, pltpu.roll(dcross, span, 1))[:, : out_ref.shape[-1]]
    out_ref[...] = jnp.broadcast_to(factors[None], out_ref.shape)


def factors_of(parts, count):
    lanes = round_up(16 * count, LANES)
    return pl.pallas_call(
        functools.partial(factor_kernel, count),
        out_shape=jax.ShapeDtypeStruct(parts.shape[:2] + (lanes,), jnp.float32),
        compiler_params=pltpu.CompilerParams(vmem_limit_bytes=VMEM_LIMIT),
        cost_estimate=pl.CostEstimate(flops=parts.size, bytes_accessed=8 * parts.size, transcendentals=0),
        name="factors",
    )(parts)


def synthesis_kernel(
    count, order_ref, coef_ref, last_ref, factor_ref, leg_ref, out_ref,
    spread_ref, lower_ref, upper_ref, wide_ref,
):
    p = pl.program_id(0)
    rows = 4 * count

    @pl.when(p == 0)
    def _():
        spread_ref[...] = factor_ref[...].T

    lower_order = order_ref[p]
    boundary = DEGREES - lower_order
    lower_weight = jnp.where(lower_order == 0, 1.0, 2.0)
    back = lax.rem(DEGREES - lower_order, DEGREES)
    last_grads = []
    for s in range(2):
        row_factors, last_factors = [], []
        for k in range(2):
            at = (2 * k + s) * rows
            factor = spread_ref[at : at + rows, :]
            row = lax.broadcasted_iota(jnp.int32, factor.shape, 1)
            shifted = lower_weight * pltpu.roll(factor, back, 1)
            row_factors.append(jnp.where(row < boundary, shifted, 2.0 * pltpu.roll(factor, 1, 1)))
            last_factors.append(jnp.broadcast_to(2.0 * factor[:, DEGREES - 1 :], (rows, LANES)))
        for q in range(2):
            g = 2 * s + q
            at = 2 * g * rows
            predicted = coef_ref[0, at : at + rows, :]
            observed = coef_ref[0, at + rows : at + 2 * rows, :]
            grad = row_factors[0] * predicted + row_factors[1] * observed
            row = lax.broadcasted_iota(jnp.int32, grad.shape, 1)
            lower_ref[g * rows : (g + 1) * rows, :] = jnp.where(row < boundary, grad, 0.0)
            upper_ref[g * rows : (g + 1) * rows, :] = jnp.where(row < boundary, 0.0, grad)[:, HALF:]
            predicted = last_ref[0, at : at + rows, :]
            observed = last_ref[0, at + rows : at + 2 * rows, :]
            last_grad = last_factors[0] * predicted + last_factors[1] * observed
            last_grads.append(last_grad.astype(jnp.bfloat16).astype(jnp.float32))
    last_grad = jnp.concatenate(last_grads, axis=0)
    lower_grad = lower_ref[...].astype(jnp.bfloat16)
    upper_grad = upper_ref[...].astype(jnp.bfloat16)
    last_leg = leg_ref[0, DEGREES : DEGREES + 1, :].astype(jnp.float32)

    width = 256
    for tile in range(DEGREES // width):
        start = tile * width
        lower = dot_nn(lower_grad, leg_ref[0, :DEGREES, start : start + width])
        upper = dot_nn(upper_grad, leg_ref[0, HALF:DEGREES, start : start + width])
        for t, values in enumerate((lower, upper)):
            for sub in range(width // LANES):
                at = start + sub * LANES
                piece = values[:, sub * LANES : (sub + 1) * LANES]
                if t == 1:
                    piece = piece + last_grad * last_leg[:, at : at + LANES]
                blocks = [piece[g * rows : (g + 1) * rows] for g in range(4)]
                for i, block in enumerate(swap_groups(blocks)):
                    wide_ref[at // 32 + i, pl.ds(2 * p + t, rows, stride=SLOTS), :] = block

    @pl.when(p == pl.num_programs(0) - 1)
    def _():
        def narrow(j, carry):
            out_ref[j] = wide_ref[j].astype(jnp.bfloat16)
            return carry

        lax.fori_loop(0, 32, narrow, 0)


def synthesis(lower_order, coeffs, last, factors, legendre, count):
    pairs, leg_rows, _ = legendre.shape
    rows = 32 * count
    lanes = factors.shape[1]
    grid_spec = pltpu.PrefetchScalarGridSpec(
        num_scalar_prefetch=1,
        grid=(pairs,),
        in_specs=[
            pl.BlockSpec((1, rows, DEGREES), lambda p, o: (p, 0, 0)),
            pl.BlockSpec((1, rows, LANES), lambda p, o: (p, 0, 0)),
            pl.BlockSpec((DEGREES, lanes), lambda p, o: (0, 0)),
            pl.BlockSpec((1, leg_rows, DEGREES), lambda p, o: (p, 0, 0)),
        ],
        out_specs=pl.BlockSpec((32, rows, LANES), lambda p, o: (0, 0, 0)),
        scratch_shapes=[
            pltpu.VMEM((lanes, DEGREES), jnp.float32),
            pltpu.VMEM((rows // 2, DEGREES), jnp.float32),
            pltpu.VMEM((rows // 2, HALF), jnp.float32),
            pltpu.VMEM((32, rows, LANES), jnp.float32),
        ],
    )
    return pl.pallas_call(
        functools.partial(synthesis_kernel, count),
        grid_spec=grid_spec,
        out_shape=jax.ShapeDtypeStruct((32, rows, LANES), jnp.bfloat16),
        compiler_params=pltpu.CompilerParams(vmem_limit_bytes=VMEM_LIMIT),
        cost_estimate=pl.CostEstimate(
            flops=3 * pairs * rows // 2 * DEGREES * DEGREES,
            bytes_accessed=2 * legendre.size + 4 * pairs * rows * DEGREES + 64 * rows * LANES,
            transcendentals=0,
        ),
        name="synthesis",
    )(lower_order, coeffs, last, factors, legendre)


def unpack_kernel(perm_ref, returned_ref, *refs):
    out_ref = refs[-1]
    both = returned_ref[...].astype(jnp.float32)
    sides = [both[:, c * SLOTS : (c + 1) * SLOTS].reshape(DEGREES, LANES) for c in range(2)]
    by_slot = jnp.concatenate(sides, axis=1)
    field = dot_nn(by_slot.T.astype(jnp.bfloat16), perm_ref[...])
    out_ref[...] = field.astype(jnp.bfloat16).reshape(out_ref.shape)


def unpack(perm, returned, earlier, first, count, channels):
    devices = DEGREES // SLOTS
    block = (2, 2, 2, 32, DEGREES)
    in_specs = [
        pl.BlockSpec((DEGREES, DEGREES), lambda i: (0, 0)),
        pl.BlockSpec((devices, 16, LANES), lambda i: (0, i, 0)),
    ]
    args = [perm, returned]
    aliases = {}
    if earlier is not None:
        in_specs.append(pl.BlockSpec(memory_space=pl.ANY))
        args.append(earlier)
        aliases = {2: 0}
    return pl.pallas_call(
        unpack_kernel,
        grid=(count // 2,),
        in_specs=in_specs,
        out_specs=pl.BlockSpec(block, lambda i: (first // 2 + i, 0, 0, 0, 0)),
        out_shape=jax.ShapeDtypeStruct((channels, 2, 2, 32, DEGREES), jnp.bfloat16),
        input_output_aliases=aliases,
        compiler_params=pltpu.CompilerParams(vmem_limit_bytes=VMEM_LIMIT),
        cost_estimate=pl.CostEstimate(
            flops=2 * DEGREES * DEGREES * LANES * count,
            bytes_accessed=2 * DEGREES * DEGREES + 4 * LANES * DEGREES * count,
            transcendentals=0,
        ),
        name="unpack",
    )(*args)


def exchange(values):
    return lax.all_to_all(values, AXES, split_axis=0, concat_axis=0, tiled=True)


def per_device(pred_four, target_four, legendre, pair_order):
    channels = pred_four.shape[0]
    pairs = legendre.shape[0]
    devices = DEGREES // SLOTS
    slot_orders = jnp.stack([pair_order, DEGREES - 1 - pair_order], axis=1).reshape(DEGREES)
    order_index = jnp.arange(DEGREES, dtype=jnp.int32)
    perm = (slot_orders[:, None] == order_index[None, :]).astype(jnp.bfloat16)
    device = lax.axis_index(AXES)
    lower_order = lax.dynamic_slice_in_dim(pair_order, device * pairs, pairs)
    starts = [sum(PARTS[:i]) for i in range(len(PARTS))]

    arrived = []
    for first, count in zip(starts, PARTS):
        packed = pack(perm, pred_four, target_four, first, count)
        arrived.append(exchange(packed.reshape(devices, 2 * count * SLOTS, LANES)))
    kept, spectra = [], []
    for count, block in zip(PARTS, arrived):
        coeffs, last, moments = analysis(lower_order, block, legendre, count)
        kept.append((coeffs, last))
        spectra.append(exchange(moments.reshape(devices, SLOTS, -1)))
    factors = [
        exchange(factors_of(block, count)).reshape(DEGREES, -1)
        for count, block in zip(PARTS, spectra)
    ]
    returned = []
    for count, (coeffs, last), factor in zip(PARTS, kept, factors):
        going = synthesis(lower_order, coeffs, last, factor, legendre, count)
        returned.append(exchange(going.reshape(devices, count * SLOTS, LANES)))
    result = None
    for first, count, block in zip(starts, PARTS, returned):
        result = unpack(perm, block, result, first, count, channels)
    return result


def solution(mesh):
    placed = (
        P("col", None, None, "ma", None),
        P("col", None, None, "ma", None),
        P(AXES, None, None),
        P(),
    )
    return jax.shard_map(
        per_device,
        mesh=mesh,
        in_specs=placed,
        out_specs=P("col", None, None, "ma", None),
        check_vma=False,
    )
```

time: 831 us -> 223 us (0.27); the launches traced: 821 us -> 222 us
  local copies, waits for them, and re-layouts: 372 us -> 11.1 us
  waiting for transfers between devices: 194 us -> 53.2 us
  blocking collectives: 147 us -> 89.4 us
  Pallas kernels: 0 us -> 53.3 us
  matrix products: 44.6 us -> 0 us
  other arithmetic: 44.1 us -> 3.09 us
  between operations: 13.8 us -> 0.03 us
    psum x1 -> x0, waiting for transfers between devices: 135 us -> none  [per_device(): totals = lax.psum(partial_sums, ('ma', 'col'))]
    all_to_all x9 -> x0, local copies, waits for them, and re-layouts: 127 us -> none  [the longest x3 61.8 us: per_device(): lax.all_to_all(outgoing, 'ma', split_axis=0, concat_axis=5, tiled=True)]
    unnamed x15 -> x1, local copies, waits for them, and re-layouts: 103 us -> 9.49 us
    all_to_all x3, blocking collectives: 147 us -> 89.4 us  [exchange(): return lax.all_to_all(values, AXES, split_axis=0, concat_axis=0, tiled=True)]
    pallas_call x0 -> x5, Pallas kernels: none -> 53.3 us  [the longest x1 18.4 us: analysis(): pl.pallas_call(functools.partial(analysis_kernel, count), grid_spec=grid_...]
    dot_general x4 -> x0, matrix products: 44.6 us -> none  [the longest x1 18.6 us: per_device(): jnp.einsum('pjk,pork->pojr', legendre, by_pair, preferred_element_type=jn...]
    convert_element_type x1 -> x0, local copies, waits for them, and re-layouts: 41.2 us -> none  [per_device(): outgoing = jnp.einsum('fcsqkm,nm->nfcsqk', both_fields, permuter, preferr...]
    gather x32 -> x0, local copies, waits for them, and re-layouts: 31.5 us -> none
  transfers between devices with their start and end apart: 2 -> 1, of which waited for: 2 -> 1; matrix products, arithmetic and copies ran while one was open for 1% -> 5% of each run, Pallas kernels for 0% -> 0%
where the time goes in v1:
time: 223 us; the launch traced here: 222 us
  blocking collectives  89.4 us (40%)
  Pallas kernels  53.3 us (24%)
  waiting for transfers between devices  53.2 us (24%)
  starting transfers between devices  11.9 us (5%)
  local copies, waits for them, and re-layouts  11.1 us (5%)
  other arithmetic  3.09 us (1%)
    all_to_all x3, blocking collectives, exchange(): return lax.all_to_all(values, AXES, split_axis=0, concat_axis=0, tiled=True)  89.4 us
    all_to_all x1, waiting for transfers between devices, exchange(): return lax.all_to_all(values, AXES, split_axis=0, concat_axis=0, tiled=True)  53.2 us
    pallas_call x1, Pallas kernels, analysis(): pl.pallas_call(functools.partial(analysis_kernel, count), grid_spec=grid_...  18.4 us
    pallas_call x1, Pallas kernels, synthesis(): pl.pallas_call(functools.partial(synthesis_kernel, count), grid_spec=grid...  14.9 us
    all_to_all x1, starting transfers between devices, exchange(): return lax.all_to_all(values, AXES, split_axis=0, concat_axis=0, tiled=True)  11.9 us
    pallas_call x1, Pallas kernels, pack(): pl.pallas_call(pack_kernel, grid=(count // 2,), in_specs=[pl.BlockSpec((D...  10 us
    unnamed x1, local copies, waits for them, and re-layouts  9.49 us
    pallas_call x1, Pallas kernels, unpack(): pl.pallas_call(unpack_kernel, grid=(count // 2,), in_specs=in_specs, out_...  7.39 us
  transfers between devices with their start and end apart: 1, of which 1 were waited for; matrix products, arithmetic and copies ran while one was open for 5% of the time, Pallas kernels for 0%

profile of v1, /device:TPU:1, one launch (start us, length us, event | category | flops | bytes accessed | tf_op | source)
XLA Modules:
  0.0 222.0 jit_solution(10300849770417723151)
XLA Ops:
  0.0 0.7 broadcast_subtract_fusion
  0.7 0.7 pad_add_fusion
  1.4 0.1 copy.7
  1.5 0.2 eq.15
  1.7 1.7 fusion.perm_ref
  3.4 10.0 %pack.1 = bf16[128,2,5,16,128]{4,3,2,1,0:T(8,128)(2,1)} custom-call(bf16[1024,1024]{1,0:T(8,128)(2,1)} %fusion.perm_ref, bf16[10,2,2,32,1024]{4,3,2,1,0:T(8,128)(2,1)} %pred_ref.1, bf16[10,2,2,32,1024]{4,3,2,1,0:T(8,128)(2,1)} %target_ref.1), custom_call_target="tpu_custom_call" | custom-call | flops 5368709120 | bytes 12582912 | tf_op jit(solution)/shard_map/pack/pallas_call | solution.py:63
  13.4 11.9 %all-to-all-start = ((bf16[128,160,128]{2,1,0:T(8,128)(2,1)}), bf16[128,160,128]{2,1,0:T(8,128)(2,1)}, u32[]{:S(2)}, u32[]{:S(2)}) async-start(bf16[128,160,128]{2,1,0:T(8,128)(2,1)} %bitcast.8), calls=%async_computation | async-start | bytes 10485760 | tf_op jit(solution)/shard_map/all_to_all | solution.py:381
  25.3 1.3 dynamic_slice.3.order_ref
  26.6 9.5 %copy.8.leg_ref = bf16[4,1025,1024]{2,1,0:T(8,128)(2,1)} copy(bf16[4,1025,1024]{2,0,1:T(4,128)(2,1)} %param.6) | data formatting | bytes 16793600 | tf_op args[2]
  36.1 53.2 %all-to-all-done = bf16[128,160,128]{2,1,0:T(8,128)(2,1)} async-done(((bf16[128,160,128]{2,1,0:T(8,128)(2,1)}), bf16[128,160,128]{2,1,0:T(8,128)(2,1)}, u32[]{:S(2)}, u32[]{:S(2)}) %all-to-all-start) | async-done | bytes 5242912 | tf_op jit(solution)/shard_map/all_to_all | solution.py:381
  89.3 18.4 %analysis.1 = (f32[4,320,1024]{2,1,0:T(8,128)}, f32[4,320,128]{2,1,0:T(8,128)}, f32[1024,256]{1,0:T(8,128)}) custom-call(s32[4]{0:T(128)} %dynamic_slice.3.order_ref, bf16[32,4,2,80,128]{4,3,2,1,0:T(8,128)(2,1)} %bitcast.3.arrived_ref, bf16[4,1025,1024]{2,1,0:T(8,128)(2,1)} %copy.8.leg_ref), custom_call_target="tpu_custom_call" | custom-call | flops 4026531840 | bytes 18882560 | tf_op jit(solution)/shard_map/analysis/pallas_call | solution.py:181
  107.7 24.1 %all_to_all.20.parts_ref = f32[128,8,256]{2,1,0:T(8,128)} all-to-all(f32[128,8,256]{2,1,0:T(8,128)} %bitcast.10), channel_id=1, replica_groups=mesh['ma'=32,'col'=4] {'ma','col'}, dimensions={0} | all-to-all | bytes 2097152 | tf_op jit(solution)/shard_map/all_to_all | solution.py:381
  131.7 2.6 %factors.1 = f32[128,8,256]{2,1,0:T(8,128)} custom-call(f32[128,8,256]{2,1,0:T(8,128)} %all_to_all.20.parts_ref), custom_call_target="tpu_custom_call" | custom-call | flops 262144 | bytes 2097152 | tf_op jit(solution)/shard_map/factors/pallas_call | solution.py:230
  134.3 24.3 %all_to_all.21 = f32[128,8,256]{2,1,0:T(8,128)} all-to-all(f32[128,8,256]{2,1,0:T(8,128)} %factors.1), channel_id=1, replica_groups=mesh['ma'=32,'col'=4] {'ma','col'}, dimensions={0} | all-to-all | bytes 2097152 | tf_op jit(solution)/shard_map/all_to_all | solution.py:381
  158.6 14.9 %synthesis.1 = bf16[32,320,128]{2,1,0:T(8,128)(2,1)} custom-call(s32[4]{0:T(128)} %dynamic_slice.3.order_ref, f32[4,320,1024]{2,1,0:T(8,128)} %get-tuple-element.8.coef_ref, f32[4,320,128]{2,1,0:T(8,128)} %get-tuple-element.9.last_ref, f32[1024,256]{1,0:T(8,128)} %bitcast.9, bf16[4,1025,1024]{2,1,0:T(8,128)(2,1)} %copy.8.leg_ref), custom_call_target="tpu_custom_call" | custom-call | flops 2013265920 | bytes 16261120 | tf_op jit(solution)/shard_map/synthesis/pallas_call | solution.py:327
  173.5 41.1 %all_to_all.22.returned_ref = bf16[128,80,128]{2,1,0:T(8,128)(2,1)} all-to-all(bf16[128,80,128]{2,1,0:T(8,128)(2,1)} %bitcast.7), channel_id=1, replica_groups=mesh['ma'=32,'col'=4] {'ma','col'}, dimensions={0} | all-to-all | bytes 5242880 | tf_op jit(solution)/shard_map/all_to_all | solution.py:381
  214.6 7.4 %unpack.1 = bf16[10,2,2,32,1024]{4,3,2,1,0:T(8,128)(2,1)} custom-call(bf16[1024,1024]{1,0:T(8,128)(2,1)} %fusion.perm_ref, bf16[128,80,128]{2,1,0:T(8,128)(2,1)} %all_to_all.22.returned_ref), custom_call_target="tpu_custom_call" | custom-call | flops 2684354560 | bytes 7340032 | tf_op jit(solution)/shard_map/unpack/pallas_call | solution.py:363
Async XLA Ops:
  13.4 75.9 %all-to-all-start = ((bf16[128,160,128]{2,1,0:T(8,128)(2,1)}), bf16[128,160,128]{2,1,0:T(8,128)(2,1)}, u32[]{:S(2)}, u32[]{:S(2)}) async-start(bf16[128,160,128]{2,1,0:T(8,128)(2,1)} %bitcast.8), calls=%async_computation | async-start | bytes 10485760 | tf_op jit(solution)/shard_map/all_to_all | solution.py:381

commit v2 on v0

v2 whole, which is shorter than its diff:
```python
import functools

import jax
import jax.numpy as jnp
from jax import lax
from jax.experimental import pallas as pl
from jax.experimental.pallas import tpu as pltpu
from jax.sharding import PartitionSpec as P

DEGREES = 1024
HALF = DEGREES // 2
POWER_FLOOR = 0.5
LANES = 128
SLOTS = 8
AXES = ("ma", "col")
PACK_LIMIT = 24 * 1024 * 1024
KERNEL_LIMIT = 32 * 1024 * 1024


def round_up(value, multiple):
    return -(-value // multiple) * multiple


def dot_nt(left, right):
    return lax.dot_general(left, right, (((1,), (1,)), ((), ())), preferred_element_type=jnp.float32)


def dot_nn(left, right):
    return lax.dot_general(left, right, (((1,), (0,)), ((), ())), preferred_element_type=jnp.float32)


def by_position(blocks, shift):
    group = lax.broadcasted_iota(jnp.int32, blocks[0].shape, 1) >> 5
    result = blocks[-shift % 4]
    for z in range(1, 4):
        result = jnp.where(group == z, blocks[(z - shift) % 4], result)
    return result


def one_hots(pairs_ref, lower_ref, upper_ref):
    row = jnp.broadcast_to(pairs_ref[...], (8, HALF)).astype(jnp.float32)
    order = row.T[:, :1].astype(jnp.int32)
    lane = lax.broadcasted_iota(jnp.int32, (HALF, HALF), 1)
    lower_ref[...] = jnp.where(lane == order, 1.0, 0.0).astype(jnp.bfloat16)
    upper_ref[...] = jnp.where(lane == HALF - 1 - order, 1.0, 0.0).astype(jnp.bfloat16)


def trade_halves(first, second):
    top = lax.broadcasted_iota(jnp.int32, first.shape, 1) < 4
    return (
        jnp.where(top, first, pltpu.roll(second, 4, 1)),
        jnp.where(top, pltpu.roll(first, 4, 1), second),
    )


def pack_kernel(turn_ref, pairs_ref, pred_ref, target_ref, out_ref, lower_ref, upper_ref):
    @pl.when(pl.program_id(0) == 0)
    def _():
        one_hots(pairs_ref, lower_ref, upper_ref)

    turn = turn_ref[0]
    for f, field_ref in enumerate((pred_ref, target_ref)):
        field = jnp.concatenate(
            [field_ref[c, (z - turn) & 3] for c in range(2) for z in range(4)], axis=0
        )
        low = dot_nt(lower_ref[...], field[:, :HALF]).reshape(HALF // 8, 8, 2 * LANES)
        high = dot_nt(upper_ref[...], field[:, HALF:]).reshape(HALF // 8, 8, 2 * LANES)
        both = jnp.stack(trade_halves(low, high), axis=1).reshape(HALF // 4, 8, 2 * LANES)
        both = jnp.concatenate([both[:, :, :LANES], both[:, :, LANES:]], axis=1)
        out_ref[:, f, 0] = both.astype(jnp.bfloat16)


def pack(turn, pairs, pred, target, first, count):
    devices = DEGREES // SLOTS
    field_spec = pl.BlockSpec((2, 4, 32, DEGREES), lambda i, t: (first // 2 + i, 0, 0, 0))
    grid_spec = pltpu.PrefetchScalarGridSpec(
        num_scalar_prefetch=1,
        grid=(count // 2,),
        in_specs=[pl.BlockSpec((1, HALF), lambda i, t: (0, 0)), field_spec, field_spec],
        out_specs=pl.BlockSpec((devices, 2, 1, 16, LANES), lambda i, t: (0, 0, i, 0, 0)),
        scratch_shapes=[pltpu.VMEM((HALF, HALF), jnp.bfloat16)] * 2,
    )
    return pl.pallas_call(
        pack_kernel,
        grid_spec=grid_spec,
        out_shape=jax.ShapeDtypeStruct((devices, 2, count // 2, 16, LANES), jnp.bfloat16),
        compiler_params=pltpu.CompilerParams(vmem_limit_bytes=PACK_LIMIT),
        cost_estimate=pl.CostEstimate(
            flops=DEGREES * DEGREES * 2 * LANES * count,
            bytes_accessed=8 * LANES * DEGREES * count,
            transcendentals=0,
        ),
        name="pack",
    )(turn, pairs, pred, target)


def moments_of(values, rows):
    width = values.shape[-1]
    shaped = values.reshape(4, 2, rows, width)
    pieces = []
    for left, right in ((0, 0), (1, 1), (0, 1)):
        for s in range(2):
            real = shaped[2 * s, left] * shaped[2 * s, right]
            imag = shaped[2 * s + 1, left] * shaped[2 * s + 1, right]
            pieces.append(real + imag)
    return jnp.concatenate(pieces, axis=0)


def analysis_kernel(
    count, order_ref, arrived_ref, leg_ref, coef_ref, last_ref, moment_ref,
    wide_ref, field_ref, raw_ref, lower_ref, upper_ref, tail_ref,
):
    rows = 4 * count
    size = 24 * count

    def widen(j, carry):
        for f in range(2):
            block = arrived_ref[j, :, f].reshape(rows * SLOTS, LANES)
            wide_ref[f, j] = block.astype(jnp.float32)
        return carry

    lax.fori_loop(0, 32, widen, 0)
    lower_ref[...] = jnp.zeros_like(lower_ref)
    upper_ref[...] = jnp.zeros_like(upper_ref)
    tail_ref[...] = jnp.zeros_like(tail_ref)

    def one_pair(p, carry):
        for t in range(2):
            slot = 4 * t + p
            for tile in range(8):
                blocks = []
                for i in range(4):
                    fields = [
                        wide_ref[f, 4 * tile + i, pl.ds(slot, rows, stride=SLOTS), :] for f in range(2)
                    ]
                    blocks.append(jnp.concatenate(fields, axis=0))
                for g in range(4):
                    block = by_position(blocks, g)
                    if g > 0:
                        block = pltpu.roll(block, LANES - 32 * g, 1)
                    field_ref[
                        t, g * 2 * rows : (g + 1) * 2 * rows, tile * LANES : (tile + 1) * LANES
                    ] = block.astype(jnp.bfloat16)

        lower_order = order_ref[p]
        boundary = DEGREES - lower_order
        width = 256
        for tile in range(DEGREES // width):
            start = tile * width
            leg = leg_ref[p, start : start + width, :]
            values = dot_nt(field_ref[0], leg)
            if start >= HALF:
                upper = dot_nt(field_ref[1], leg)
                row = lax.broadcasted_iota(jnp.int32, values.shape, 1) + start
                values = jnp.where(row < boundary, values, upper)
            coef_ref[p, :, start : start + width] = values
            moments = moments_of(values, rows)
            raw_ref[:, start : start + width] = moments
            if start >= HALF:
                row = lax.broadcasted_iota(jnp.int32, moments.shape, 1) + start
                upper_ref[:, start - HALF : start - HALF + width] += jnp.where(
                    row < boundary, 0.0, moments
                )
        last_leg = jnp.broadcast_to(
            leg_ref[p, DEGREES : DEGREES + 1, :].astype(jnp.float32), (LANES, DEGREES)
        )
        last = dot_nt(field_ref[1], last_leg.astype(jnp.bfloat16))
        last_ref[p] = last
        tail_ref[...] += moments_of(last, rows)

        lower_weight = jnp.where(lower_order == 0, 1.0, 2.0)
        tiles_up = lower_order >> 7
        lanes_up = lower_order & (LANES - 1)
        lane = lax.broadcasted_iota(jnp.int32, (size, LANES), 1)
        before = jnp.zeros((size, LANES), jnp.float32)
        for tile in range(8):
            turned = pltpu.roll(raw_ref[:, tile * LANES : (tile + 1) * LANES], lanes_up, 1)
            at = pl.multiple_of((tile + tiles_up) * LANES, LANES)
            lower_ref[:, pl.ds(at, LANES)] += lower_weight * jnp.where(lane < lanes_up, before, turned)
            before = turned
        return carry

    lax.fori_loop(0, 4, one_pair, 0)

    lane = lax.broadcasted_iota(jnp.int32, (size, LANES), 1)
    after = tail_ref[...]
    for tile in reversed(range(8)):
        total = lower_ref[:, tile * LANES : (tile + 1) * LANES]
        if tile >= 4:
            turned = pltpu.roll(upper_ref[:, (tile - 4) * LANES : (tile - 3) * LANES], LANES - 1, 1)
            total = total + 2.0 * jnp.where(lane == LANES - 1, after, turned)
            after = turned
        pad = moment_ref.shape[1] - size
        if pad > 0:
            total = jnp.concatenate([total, jnp.zeros((pad, LANES), jnp.float32)], axis=0)
        moment_ref[tile * LANES : (tile + 1) * LANES, :] = total.T


def in_vmem(*values):
    return [pltpu.with_memory_space_constraint(value, pltpu.VMEM) for value in values]


def analysis(lower_order, arrived, legendre, count):
    pairs = legendre.shape[0]
    rows = 32 * count
    lanes = round_up(24 * count, LANES)
    arrived = arrived.reshape(32, 4, 2, count * SLOTS, LANES)
    whole = pl.BlockSpec(memory_space=pltpu.VMEM)
    return pl.pallas_call(
        functools.partial(analysis_kernel, count),
        in_specs=[pl.BlockSpec(memory_space=pltpu.SMEM), whole, whole],
        out_specs=[whole, whole, whole],
        out_shape=[
            pltpu.VMEM((pairs, rows, DEGREES), jnp.float32),
            pltpu.VMEM((pairs, rows, LANES), jnp.float32),
            pltpu.VMEM((DEGREES, lanes), jnp.float32),
        ],
        scratch_shapes=[
            pltpu.VMEM((2, 32, rows, LANES), jnp.float32),
            pltpu.VMEM((2, rows, DEGREES), jnp.bfloat16),
            pltpu.VMEM((24 * count, DEGREES), jnp.float32),
            pltpu.VMEM((24 * count, DEGREES + HALF), jnp.float32),
            pltpu.VMEM((24 * count, HALF), jnp.float32),
            pltpu.VMEM((24 * count, LANES), jnp.float32),
        ],
        compiler_params=pltpu.CompilerParams(vmem_limit_bytes=KERNEL_LIMIT),
        cost_estimate=pl.CostEstimate(
            flops=3 * pairs * rows * DEGREES * DEGREES,
            bytes_accessed=2 * legendre.size + 4 * pairs * rows * DEGREES + 2 * arrived.size,
            transcendentals=0,
        ),
        name="analysis",
    )(lower_order, *in_vmem(arrived, legendre))


def factor_kernel(count, parts_ref, out_ref):
    total = jnp.sum(parts_ref[...], axis=0)
    size = total.shape[1]
    span = 8 * count
    power_pred = total
    power_true = pltpu.roll(total, size - span, 1)
    cross = pltpu.roll(total, size - 2 * span, 1)
    pred = jnp.maximum(power_pred, POWER_FLOOR)
    true = jnp.maximum(power_true, POWER_FLOOR)
    root_pred = jnp.sqrt(pred)
    root_true = jnp.sqrt(true)
    both = pred + true
    upper_mean = (pred * pred + true * true) / both
    inverse = 1.0 / (root_pred * root_true)
    coherence = cross * inverse
    mean_slope = (2.0 * pred - upper_mean) / both
    slope = (
        (root_pred - root_true) / root_pred
        + 2.0 * mean_slope * (1.0 - coherence)
        + upper_mean * coherence / pred
    )
    binds = jnp.where(power_pred > POWER_FLOOR, 1.0, jnp.where(power_pred == POWER_FLOOR, 0.5, 0.0))
    dpower = 2.0 * slope * binds
    dcross = -2.0 * upper_mean * inverse
    lane = lax.broadcasted_iota(jnp.int32, total.shape, 1)
    factors = jnp.where(lane < span, dpower, pltpu.roll(dcross, span, 1))[:, : out_ref.shape[-1]]
    out_ref[...] = jnp.broadcast_to(factors[None], out_ref.shape)


def factors_of(parts, count):
    lanes = round_up(16 * count, LANES)
    whole = pl.BlockSpec(memory_space=pltpu.VMEM)
    return pl.pallas_call(
        functools.partial(factor_kernel, count),
        in_specs=[whole],
        out_specs=whole,
        out_shape=pltpu.VMEM(parts.shape[:2] + (lanes,), jnp.float32),
        compiler_params=pltpu.CompilerParams(vmem_limit_bytes=KERNEL_LIMIT),
        cost_estimate=pl.CostEstimate(flops=parts.size, bytes_accessed=8 * parts.size, transcendentals=0),
        name="factors",
    )(*in_vmem(parts))


def synthesis_kernel(
    count, order_ref, coef_ref, last_ref, factor_ref, leg_ref, out_ref,
    spread_ref, upspread_ref, lower_ref, upper_ref, wide_ref,
):
    rows = 4 * count
    size = 16 * count
    lane = lax.broadcasted_iota(jnp.int32, (size, LANES), 1)

    before = None
    for tile in range(8):
        turned = factor_ref[tile * LANES : (tile + 1) * LANES, :].T[:size]
        spread_ref[:, tile * LANES : (tile + 1) * LANES] = turned
        shifted = pltpu.roll(turned, 1, 1)
        if tile >= 4:
            upspread_ref[:, (tile - 4) * LANES : (tile - 3) * LANES] = 2.0 * jnp.where(
                lane == 0, before, shifted
            )
        before = shifted

    def one_pair(p, carry):
        lower_order = order_ref[p]
        boundary = DEGREES - lower_order
        lower_weight = jnp.where(lower_order == 0, 1.0, 2.0)
        tiles_up = lower_order >> 7
        lanes_up = lower_order & (LANES - 1)
        back = (LANES - lanes_up) & (LANES - 1)

        def turned_tile(tile):
            at = pl.multiple_of((tile + tiles_up) * LANES, LANES)
            return pltpu.roll(spread_ref[:, pl.ds(at, LANES)], back, 1)

        def graded(factors, observe):
            grads = []
            for g in range(4):
                s = g // 2
                predicted = observe(2 * g * rows)
                observed = observe((2 * g + 1) * rows)
                grads.append(
                    factors[s * rows : (s + 1) * rows] * predicted
                    + factors[(2 + s) * rows : (3 + s) * rows] * observed
                )
            return jnp.concatenate(grads, axis=0)

        now = turned_tile(0)
        for tile in range(8):
            start = tile * LANES
            then = turned_tile(tile + 1)
            factors = lower_weight * jnp.where(lane < LANES - lanes_up, now, then)
            now = then
            row = lane + start
            if tile >= 4:
                factors = jnp.where(
                    row < boundary, factors, upspread_ref[:, start - HALF : start - HALF + LANES]
                )
            grad = graded(factors, lambda at: coef_ref[p, at : at + rows, start : start + LANES])
            if tile >= 4:
                upper_ref[:, start - HALF : start - HALF + LANES] = jnp.where(
                    row < boundary, 0.0, grad
                ).astype(jnp.bfloat16)
                grad = jnp.where(row < boundary, grad, 0.0)
            lower_ref[:, start : start + LANES] = grad.astype(jnp.bfloat16)
        last_factors = jnp.broadcast_to(2.0 * spread_ref[:, DEGREES - 1 : DEGREES], (size, LANES))
        last_grad = graded(last_factors, lambda at: last_ref[p, at : at + rows, :])
        last_grad = last_grad.astype(jnp.bfloat16).astype(jnp.float32)
        last_leg = leg_ref[p, DEGREES : DEGREES + 1, :].astype(jnp.float32)

        width = 256
        for tile in range(DEGREES // width):
            start = tile * width
            lower = dot_nn(lower_ref[...], leg_ref[p, :DEGREES, start : start + width])
            upper = dot_nn(upper_ref[...], leg_ref[p, HALF:DEGREES, start : start + width])
            for t, values in enumerate((lower, upper)):
                for sub in range(width // LANES):
                    at = start + sub * LANES
                    piece = values[:, sub * LANES : (sub + 1) * LANES]
                    if t == 1:
                        piece = piece + last_grad * last_leg[:, at : at + LANES]
                    blocks = [piece[g * rows : (g + 1) * rows] for g in range(4)]
                    blocks = [
                        block if g == 0 else pltpu.roll(block, 32 * g, 1) for g, block in enumerate(blocks)
                    ]
                    for i in range(4):
                        wide_ref[at // 32 + i, pl.ds(4 * t + p, rows, stride=SLOTS), :] = by_position(
                            blocks, i
                        )
        return carry

    lax.fori_loop(0, 4, one_pair, 0)

    def narrow(j, carry):
        out_ref[j] = wide_ref[j].astype(jnp.bfloat16)
        return carry

    lax.fori_loop(0, 32, narrow, 0)


def synthesis(lower_order, coeffs, last, factors, legendre, count):
    pairs = legendre.shape[0]
    rows = 32 * count
    whole = pl.BlockSpec(memory_space=pltpu.VMEM)
    return pl.pallas_call(
        functools.partial(synthesis_kernel, count),
        in_specs=[pl.BlockSpec(memory_space=pltpu.SMEM), whole, whole, whole, whole],
        out_specs=whole,
        out_shape=pltpu.VMEM((32, rows, LANES), jnp.bfloat16),
        scratch_shapes=[
            pltpu.VMEM((rows // 2, DEGREES + HALF), jnp.float32),
            pltpu.VMEM((rows // 2, HALF), jnp.float32),
            pltpu.VMEM((rows // 2, DEGREES), jnp.bfloat16),
            pltpu.VMEM((rows // 2, HALF), jnp.bfloat16),
            pltpu.VMEM((32, rows, LANES), jnp.float32),
        ],
        compiler_params=pltpu.CompilerParams(vmem_limit_bytes=KERNEL_LIMIT),
        cost_estimate=pl.CostEstimate(
            flops=3 * pairs * rows // 2 * DEGREES * DEGREES,
            bytes_accessed=2 * legendre.size + 4 * pairs * rows * DEGREES + 64 * rows * LANES,
            transcendentals=0,
        ),
        name="synthesis",
    )(lower_order, *in_vmem(coeffs, last, factors, legendre))


def unpack_kernel(turn_ref, pairs_ref, returned_ref, out_ref, lower_ref, upper_ref):
    @pl.when(pl.program_id(0) == 0)
    def _():
        one_hots(pairs_ref, lower_ref, upper_ref)

    turn = turn_ref[0]
    both = returned_ref[...].astype(jnp.float32).reshape(HALF // 8, 2, 2 * SLOTS, LANES)
    sides = [
        trade_halves(both[:, 0, c * SLOTS : (c + 1) * SLOTS], both[:, 1, c * SLOTS : (c + 1) * SLOTS])
        for c in range(2)
    ]
    for o, one_hot_ref in enumerate((lower_ref, upper_ref)):
        by_slot = jnp.concatenate([side[o].reshape(HALF, LANES) for side in sides], axis=1)
        field = dot_nn(by_slot.T.astype(jnp.bfloat16), one_hot_ref[...]).astype(jnp.bfloat16)
        for c in range(2):
            for z in range(4):
                at = c * LANES + z * 32
                out_ref[c, (z - turn) & 3, :, o * HALF : (o + 1) * HALF] = field[at : at + 32]


def unpack(turn, pairs, returned, count):
    devices = DEGREES // SLOTS
    grid_spec = pltpu.PrefetchScalarGridSpec(
        num_scalar_prefetch=1,
        grid=(count // 2,),
        in_specs=[
            pl.BlockSpec((1, HALF), lambda i, t: (0, 0)),
            pl.BlockSpec((devices, 16, LANES), lambda i, t: (0, i, 0)),
        ],
        out_specs=pl.BlockSpec((2, 4, 32, DEGREES), lambda i, t: (i, 0, 0, 0)),
        scratch_shapes=[pltpu.VMEM((HALF, HALF), jnp.bfloat16)] * 2,
    )
    return pl.pallas_call(
        unpack_kernel,
        grid_spec=grid_spec,
        out_shape=jax.ShapeDtypeStruct((count, 4, 32, DEGREES), jnp.bfloat16),
        compiler_params=pltpu.CompilerParams(vmem_limit_bytes=PACK_LIMIT),
        cost_estimate=pl.CostEstimate(
            flops=DEGREES * DEGREES * LANES * count,
            bytes_accessed=4 * LANES * DEGREES * count,
            transcendentals=0,
        ),
        name="unpack",
    )(turn, pairs, returned)


def exchange(values):
    return lax.all_to_all(values, AXES, split_axis=0, concat_axis=0, tiled=True)


def per_device(pred_four, target_four, legendre, pair_order):
    channels = pred_four.shape[0]
    pairs = legendre.shape[0]
    devices = DEGREES // SLOTS
    device = lax.axis_index(AXES)
    turn = (lax.axis_index("ma") & 3).reshape(1)
    lower_order = lax.dynamic_slice_in_dim(pair_order, device * pairs, pairs)
    pair_row = pair_order.reshape(1, HALF)

    by_group = (channels, 4, 32, DEGREES)
    packed = pack(
        turn, pair_row, pred_four.reshape(by_group), target_four.reshape(by_group), 0, channels
    )
    arrived = exchange(packed.reshape(devices, 2 * channels * SLOTS, LANES))
    coeffs, last, moments = analysis(lower_order, arrived, legendre, channels)
    spectra = exchange(moments.reshape(devices, SLOTS, -1))
    factors = exchange(factors_of(spectra, channels)).reshape(DEGREES, -1)
    going = synthesis(lower_order, coeffs, last, factors, legendre, channels)
    returned = exchange(going.reshape(devices, channels * SLOTS, LANES))
    return unpack(turn, pair_row, returned, channels).reshape(pred_four.shape)


def solution(mesh):
    placed = (
        P("col", None, None, "ma", None),
        P("col", None, None, "ma", None),
        P(AXES, None, None),
        P(),
    )
    return jax.shard_map(
        per_device,
        mesh=mesh,
        in_specs=placed,
        out_specs=P("col", None, None, "ma", None),
        check_vma=False,
    )
```

time: 831 us -> 202 us (0.24); the launches traced: 821 us -> 202 us
  local copies, waits for them, and re-layouts: 372 us -> 19.4 us
  waiting for transfers between devices: 194 us -> 54.4 us
  blocking collectives: 147 us -> 86.6 us
  matrix products: 44.6 us -> 0 us
  other arithmetic: 44.1 us -> 0 us
  Pallas kernels: 0 us -> 29.6 us
  between operations: 13.8 us -> 0.07 us
    psum x1 -> x0, waiting for transfers between devices: 135 us -> none  [per_device(): totals = lax.psum(partial_sums, ('ma', 'col'))]
    all_to_all x9 -> x0, local copies, waits for them, and re-layouts: 127 us -> none  [the longest x3 61.8 us: per_device(): lax.all_to_all(outgoing, 'ma', split_axis=0, concat_axis=5, tiled=True)]
    unnamed x15, local copies, waits for them, and re-layouts: 103 us -> 19.3 us
    all_to_all x3, blocking collectives: 147 us -> 86.6 us  [exchange(): return lax.all_to_all(values, AXES, split_axis=0, concat_axis=0, tiled=True)]
    dot_general x4 -> x0, matrix products: 44.6 us -> none  [the longest x1 18.6 us: per_device(): jnp.einsum('pjk,pork->pojr', legendre, by_pair, preferred_element_type=jn...]
    convert_element_type x1 -> x0, local copies, waits for them, and re-layouts: 41.2 us -> none  [per_device(): outgoing = jnp.einsum('fcsqkm,nm->nfcsqk', both_fields, permuter, preferr...]
    gather x32 -> x0, local copies, waits for them, and re-layouts: 31.5 us -> none
    pallas_call x0 -> x5, Pallas kernels: none -> 29.6 us  [the longest x1 13.4 us: analysis(): pl.pallas_call(functools.partial(analysis_kernel, count), in_specs=[pl.Bl...]
  transfers between devices with their start and end apart: 2 -> 1, of which waited for: 2 -> 1; matrix products, arithmetic and copies ran while one was open for 1% -> 5% of each run, Pallas kernels for 0% -> 0%
where the time goes in v2:
time: 202 us
  blocking collectives  86.6 us (43%)
  waiting for transfers between devices  54.4 us (27%)
  Pallas kernels  29.6 us (15%)
  local copies, waits for them, and re-layouts  19.4 us (10%)
  starting transfers between devices  11.9 us (6%)
    all_to_all x3, blocking collectives, exchange(): return lax.all_to_all(values, AXES, split_axis=0, concat_axis=0, tiled=True)  86.6 us
    all_to_all x1, waiting for transfers between devices, exchange(): return lax.all_to_all(values, AXES, split_axis=0, concat_axis=0, tiled=True)  54.4 us
    unnamed x15, local copies, waits for them, and re-layouts  19.3 us
    pallas_call x1, Pallas kernels, analysis(): pl.pallas_call(functools.partial(analysis_kernel, count), in_specs=[pl.Bl...  13.4 us
    all_to_all x1, starting transfers between devices, exchange(): return lax.all_to_all(values, AXES, split_axis=0, concat_axis=0, tiled=True)  11.9 us
    pallas_call x1, Pallas kernels, synthesis(): pl.pallas_call(functools.partial(synthesis_kernel, count), in_specs=[pl.B...  6.79 us
    pallas_call x1, Pallas kernels, pack(): pl.pallas_call(pack_kernel, grid_spec=grid_spec, out_shape=jax.ShapeDtype...  4.55 us
    pallas_call x1, Pallas kernels, unpack(): pl.pallas_call(unpack_kernel, grid_spec=grid_spec, out_shape=jax.ShapeDty...  4.46 us
  transfers between devices with their start and end apart: 1, of which 1 were waited for; matrix products, arithmetic and copies ran while one was open for 5% of the time, Pallas kernels for 0%

profile of v2, /device:TPU:1, one launch (start us, length us, event | category | flops | bytes accessed | tf_op | source)
XLA Modules:
  0.0 201.9 jit_solution(5904238692932453662)
XLA Ops:
  0.0 0.0 copy-start.3
  0.0 1.7 copy-done.3
  1.7 0.0 copy-start.4
  1.7 1.7 copy-done.4
  3.5 0.0 copy-start.5
  3.5 0.7 copy-done.5
  4.2 4.5 %pack.1 = bf16[128,2,5,16,128]{4,3,2,1,0:T(8,128)(2,1)S(1)} custom-call(s32[1]{0:T(128)} %bitcast.turn_ref, s32[1,512]{1,0:T(1,128)S(1)} %bitcast.16, bf16[10,4,32,1024]{3,2,1,0:T(8,128)(2,1)S(1)} %bitcast.13, bf16[10,4,32,1024]{3,2,1,0:T(8,128)(2,1)S(1)} %bitcast.14), custom_call_target="tpu_custom_call" | custom-call | flops 2684354560 | bytes 10485760 | tf_op jit(solution)/shard_map/pack/pallas_call | solution.py:83
  8.7 0.0 copy-start.2
  8.7 2.3 %copy-done.2 = bf16[128,2,5,16,128]{4,3,2,1,0:T(8,128)(2,1)} copy-done((bf16[128,2,5,16,128]{4,3,2,1,0:T(8,128)(2,1)}, bf16[128,2,5,16,128]{4,3,2,1,0:T(8,128)(2,1)S(1)}, u32[]{:S(2)}) %copy-start.2) | copy-done | bytes 5242904
  11.0 0.0 copy-start.6
  11.0 11.9 %all-to-all-start = ((bf16[128,160,128]{2,1,0:T(8,128)(2,1)}), bf16[128,160,128]{2,1,0:T(8,128)(2,1)}, u32[]{:S(2)}, u32[]{:S(2)}) async-start(bf16[128,160,128]{2,1,0:T(8,128)(2,1)} %bitcast.10), calls=%async_computation | async-start | bytes 10485760 | tf_op jit(solution)/shard_map/all_to_all | solution.py:448
  22.9 0.0 copy-done.6
  22.9 0.1 dynamic_slice.3.order_ref
  23.0 9.5 %copy.5.leg_ref = bf16[4,1025,1024]{2,1,0:T(8,128)(2,1)} copy(bf16[4,1025,1024]{2,0,1:T(4,128)(2,1)} %param.6) | data formatting | bytes 16793600 | tf_op args[2]
  32.5 54.4 %all-to-all-done = bf16[128,160,128]{2,1,0:T(8,128)(2,1)} async-done(((bf16[128,160,128]{2,1,0:T(8,128)(2,1)}), bf16[128,160,128]{2,1,0:T(8,128)(2,1)}, u32[]{:S(2)}, u32[]{:S(2)}) %all-to-all-start) | async-done | bytes 5242912 | tf_op jit(solution)/shard_map/all_to_all | solution.py:448
  86.9 0.0 copy-start
  86.9 3.4 %copy-done = bf16[4,1025,1024]{2,1,0:T(8,128)(2,1)S(1)} copy-done((bf16[4,1025,1024]{2,1,0:T(8,128)(2,1)S(1)}, bf16[4,1025,1024]{2,1,0:T(8,128)(2,1)}, u32[]{:S(2)}) %copy-start) | copy-done | bytes 8396824
  90.3 0.0 copy-start.1
  90.3 13.4 %analysis.1 = (f32[4,320,1024]{2,1,0:T(8,128)S(1)}, f32[4,320,128]{2,1,0:T(8,128)S(1)}, f32[1024,256]{1,0:T(8,128)S(1)}) custom-call(s32[4]{0:T(128)S(1)} %dynamic_slice.3.order_ref, bf16[32,4,2,80,128]{4,3,2,1,0:T(8,128)(2,1)} %bitcast.5.arrived_ref, bf16[4,1025,1024]{2,1,0:T(8,128)(2,1)S(1)} %copy-done), custom_call_target="tpu_custom_call" | custom-call | flops 4026531840 | bytes 18882560 | tf_op jit(solution)/shard_map/analysis/pallas_call | solution.py:209
  103.7 23.8 %all_to_all.20.parts_ref = f32[128,8,256]{2,1,0:T(8,128)S(1)} all-to-all(f32[128,8,256]{2,1,0:T(8,128)S(1)} %bitcast.15), channel_id=1, replica_groups=mesh['ma'=32,'col'=4] {'ma','col'}, dimensions={0} | all-to-all | bytes 2097152 | tf_op jit(solution)/shard_map/all_to_all | solution.py:448
  127.5 0.4 factors.1
  127.8 23.0 %all_to_all.21 = f32[128,8,256]{2,1,0:T(8,128)S(1)} all-to-all(f32[128,8,256]{2,1,0:T(8,128)S(1)} %factors.1), channel_id=1, replica_groups=mesh['ma'=32,'col'=4] {'ma','col'}, dimensions={0} | all-to-all | bytes 2097152 | tf_op jit(solution)/shard_map/all_to_all | solution.py:448
  150.9 0.0 copy-done.1
  150.9 6.8 %synthesis.1 = bf16[32,320,128]{2,1,0:T(8,128)(2,1)S(1)} custom-call(s32[4]{0:T(128)S(1)} %dynamic_slice.3.order_ref, f32[4,320,1024]{2,1,0:T(8,128)S(1)} %get-tuple-element.8.coef_ref, f32[4,320,128]{2,1,0:T(8,128)S(1)} %get-tuple-element.9.last_ref, f32[1024,256]{1,0:T(8,128)S(1)} %bitcast.12, bf16[4,1025,1024]{2,1,0:T(8,128)(2,1)S(1)} %copy-done.1), custom_call_target="tpu_custom_call" | custom-call | flops 2013265920 | bytes 16261120 | tf_op jit(solution)/shard_map/synthesis/pallas_call | solution.py:379
  157.7 39.8 %all_to_all.22.returned_ref = bf16[128,80,128]{2,1,0:T(8,128)(2,1)S(1)} all-to-all(bf16[128,80,128]{2,1,0:T(8,128)(2,1)S(1)} %bitcast.11), channel_id=1, replica_groups=mesh['ma'=32,'col'=4] {'ma','col'}, dimensions={0} | all-to-all | bytes 5242880 | tf_op jit(solution)/shard_map/all_to_all | solution.py:448
  197.4 4.5 %unpack.1 = bf16[10,4,32,1024]{3,2,1,0:T(8,128)(2,1)} custom-call(s32[1]{0:T(128)} %bitcast.turn_ref, s32[1,512]{1,0:T(1,128)S(1)} %bitcast.17, bf16[128,80,128]{2,1,0:T(8,128)(2,1)S(1)} %all_to_all.22.returned_ref), custom_call_target="tpu_custom_call" | custom-call | flops 1342177280 | bytes 5242880 | tf_op jit(solution)/shard_map/unpack/pallas_call | solution.py:433
Async XLA Ops:
  0.0 1.7 copy-start.3
  1.7 1.7 copy-start.4
  3.5 0.7 copy-start.5
  8.7 2.3 %copy-start.2 = (bf16[128,2,5,16,128]{4,3,2,1,0:T(8,128)(2,1)}, bf16[128,2,5,16,128]{4,3,2,1,0:T(8,128)(2,1)S(1)}, u32[]{:S(2)}) copy-start(bf16[128,2,5,16,128]{4,3,2,1,0:T(8,128)(2,1)S(1)} %pack.1) | copy-start | bytes 15728644
  11.0 11.9 %copy-start.6 = (s32[512]{0:T(512)S(1)}, s32[512]{0:T(512)}, u32[]{:S(2)}) copy-start(s32[512]{0:T(512)} %param.7) | copy-start | bytes 6148
  11.0 75.9 %all-to-all-start = ((bf16[128,160,128]{2,1,0:T(8,128)(2,1)}), bf16[128,160,128]{2,1,0:T(8,128)(2,1)}, u32[]{:S(2)}, u32[]{:S(2)}) async-start(bf16[128,160,128]{2,1,0:T(8,128)(2,1)} %bitcast.10), calls=%async_computation | async-start | bytes 10485760 | tf_op jit(solution)/shard_map/all_to_all | solution.py:448
  86.9 3.4 %copy-start = (bf16[4,1025,1024]{2,1,0:T(8,128)(2,1)S(1)}, bf16[4,1025,1024]{2,1,0:T(8,128)(2,1)}, u32[]{:S(2)}) copy-start(bf16[4,1025,1024]{2,1,0:T(8,128)(2,1)} %copy.5.leg_ref) | copy-start | bytes 25190404
  90.3 60.6 %copy-start.1 = (bf16[4,1025,1024]{2,1,0:T(8,128)(2,1)S(1)}, bf16[4,1025,1024]{2,1,0:T(8,128)(2,1)}, u32[]{:S(2)}) copy-start(bf16[4,1025,1024]{2,1,0:T(8,128)(2,1)} %copy.5.leg_ref) | copy-start | bytes 25190404

commit v3 on v2

--- a/solution.py
+++ b/solution.py
@@ -14,7 +14,7 @@
 SLOTS = 8
 AXES = ("ma", "col")
 PACK_LIMIT = 24 * 1024 * 1024
-KERNEL_LIMIT = 32 * 1024 * 1024
+KERNEL_LIMIT = 40 * 1024 * 1024
 
 
 def round_up(value, multiple):
@@ -53,37 +53,70 @@
     )
 
 
-def pack_kernel(turn_ref, pairs_ref, pred_ref, target_ref, out_ref, lower_ref, upper_ref):
-    @pl.when(pl.program_id(0) == 0)
-    def _():
-        one_hots(pairs_ref, lower_ref, upper_ref)
+def pack_kernel(
+    count, turn_ref, pairs_hbm, pred_hbm, target_hbm, out_hbm,
+    pairs_ref, field_ref, out_ref, lower_ref, upper_ref, pair_sem, in_sems, out_sems,
+):
+    def fetch(i, f):
+        source = (pred_hbm, target_hbm)[f].at[pl.ds(2 * i, 2)]
+        return pltpu.make_async_copy(source, field_ref.at[f, pl.ds(2 * i, 2)], in_sems.at[f, i])
+
+    def send(i):
+        return pltpu.make_async_copy(out_ref.at[i], out_hbm.at[:, :, i], out_sems.at[i])
+
+    pair_copy = pltpu.make_async_copy(pairs_hbm, pairs_ref, pair_sem)
+    pair_copy.start()
+    for i in range(2):
+        for f in range(2):
+            fetch(i, f).start()
+    pair_copy.wait()
+    one_hots(pairs_ref, lower_ref, upper_ref)
 
     turn = turn_ref[0]
-    for f, field_ref in enumerate((pred_ref, target_ref)):
-        field = jnp.concatenate(
-            [field_ref[c, (z - turn) & 3] for c in range(2) for z in range(4)], axis=0
-        )
-        low = dot_nt(lower_ref[...], field[:, :HALF]).reshape(HALF // 8, 8, 2 * LANES)
-        high = dot_nt(upper_ref[...], field[:, HALF:]).reshape(HALF // 8, 8, 2 * LANES)
-        both = jnp.stack(trade_halves(low, high), axis=1).reshape(HALF // 4, 8, 2 * LANES)
-        both = jnp.concatenate([both[:, :, :LANES], both[:, :, LANES:]], axis=1)
-        out_ref[:, f, 0] = both.astype(jnp.bfloat16)
-
-
-def pack(turn, pairs, pred, target, first, count):
+
+    def step(i, carry):
+        @pl.when(i + 2 < count // 2)
+        def _():
+            for f in range(2):
+                fetch(i + 2, f).start()
+
+        for f in range(2):
+            fetch(i, f).wait()
+            field = jnp.concatenate(
+                [field_ref[f, 2 * i + c, (z - turn) & 3] for c in range(2) for z in range(4)], axis=0
+            )
+            low = dot_nt(lower_ref[...], field[:, :HALF]).reshape(HALF // 8, 8, 2 * LANES)
+            high = dot_nt(upper_ref[...], field[:, HALF:]).reshape(HALF // 8, 8, 2 * LANES)
+            both = jnp.stack(trade_halves(low, high), axis=1).reshape(HALF // 4, 8, 2 * LANES)
+            both = jnp.concatenate([both[:, :, :LANES], both[:, :, LANES:]], axis=1)
+            out_ref[i, :, f] = both.astype(jnp.bfloat16)
+        send(i).start()
+        return carry
+
+    lax.fori_loop(0, count // 2, step, 0)
+    for i in range(count // 2):
+        send(i).wait()
+
+
+def pack(turn, pairs, pred, target, count):
     devices = DEGREES // SLOTS
-    field_spec = pl.BlockSpec((2, 4, 32, DEGREES), lambda i, t: (first // 2 + i, 0, 0, 0))
-    grid_spec = pltpu.PrefetchScalarGridSpec(
-        num_scalar_prefetch=1,
-        grid=(count // 2,),
-        in_specs=[pl.BlockSpec((1, HALF), lambda i, t: (0, 0)), field_spec, field_spec],
-        out_specs=pl.BlockSpec((devices, 2, 1, 16, LANES), lambda i, t: (0, 0, i, 0, 0)),
-        scratch_shapes=[pltpu.VMEM((HALF, HALF), jnp.bfloat16)] * 2,
-    )
+    steps = count // 2
+    far = pl.BlockSpec(memory_space=pltpu.HBM)
     return pl.pallas_call(
-        pack_kernel,
-        grid_spec=grid_spec,
-        out_shape=jax.ShapeDtypeStruct((devices, 2, count // 2, 16, LANES), jnp.bfloat16),
+        functools.partial(pack_kernel, count),
+        in_specs=[pl.BlockSpec(memory_space=pltpu.SMEM), far, far, far],
+        out_specs=far,
+        out_shape=pltpu.HBM((devices, 2, steps, 16, LANES), jnp.bfloat16),
+        scratch_shapes=[
+            pltpu.VMEM((1, HALF), jnp.int32),
+            pltpu.VMEM((2, count, 4, 32, DEGREES), jnp.bfloat16),
+            pltpu.VMEM((steps, devices, 2, 16, LANES), jnp.bfloat16),
+            pltpu.VMEM((HALF, HALF), jnp.bfloat16),
+            pltpu.VMEM((HALF, HALF), jnp.bfloat16),
+            pltpu.SemaphoreType.DMA,
+            pltpu.SemaphoreType.DMA((2, steps)),
+            pltpu.SemaphoreType.DMA((steps,)),
+        ],
         compiler_params=pltpu.CompilerParams(vmem_limit_bytes=PACK_LIMIT),
         cost_estimate=pl.CostEstimate(
             flops=DEGREES * DEGREES * 2 * LANES * count,
@@ -91,7 +124,7 @@
             transcendentals=0,
         ),
         name="pack",
-    )(turn, pairs, pred, target)
+    )(turn, in_hbm(pairs), in_hbm(pred), in_hbm(target))
 
 
 def moments_of(values, rows):
@@ -107,52 +140,70 @@
 
 
 def analysis_kernel(
-    count, order_ref, arrived_ref, leg_ref, coef_ref, last_ref, moment_ref,
-    wide_ref, field_ref, raw_ref, lower_ref, upper_ref, tail_ref,
+    count, order_ref, arrived_ref, source_ref, coef_ref, last_ref, moment_ref,
+    narrow_ref, leg_ref, wide_ref, field_ref, raw_ref, lower_ref, upper_ref, tail_ref, sems, leg_sems,
 ):
     rows = 4 * count
     size = 24 * count
-
-    def widen(j, carry):
-        for f in range(2):
-            block = arrived_ref[j, :, f].reshape(rows * SLOTS, LANES)
-            wide_ref[f, j] = block.astype(jnp.float32)
-        return carry
-
-    lax.fori_loop(0, 32, widen, 0)
+    span = count * SLOTS
+
+    def chunk(k):
+        at = pl.ds(4 * k, 4)
+        return pltpu.make_async_copy(arrived_ref.at[at], narrow_ref.at[at], sems.at[k])
+
+    def leg_copy(p):
+        return pltpu.make_async_copy(source_ref.at[p], leg_ref.at[p], leg_sems.at[p])
+
+    for k in range(8):
+        chunk(k).start()
     lower_ref[...] = jnp.zeros_like(lower_ref)
     upper_ref[...] = jnp.zeros_like(upper_ref)
     tail_ref[...] = jnp.zeros_like(tail_ref)
 
-    def one_pair(p, carry):
-        for t in range(2):
-            slot = 4 * t + p
-            for tile in range(8):
-                blocks = []
-                for i in range(4):
-                    fields = [
-                        wide_ref[f, 4 * tile + i, pl.ds(slot, rows, stride=SLOTS), :] for f in range(2)
-                    ]
-                    blocks.append(jnp.concatenate(fields, axis=0))
-                for g in range(4):
-                    block = by_position(blocks, g)
+    def build(k, carry):
+        chunk(k).wait()
+
+        @pl.when((k == 1) | (k == 4))
+        def _():
+            leg_copy(k // 4).start()
+
+        for g in range(4):
+            for col in range(4):
+                for f in range(2):
+                    blocks = [narrow_ref[4 * k + i, col, f] for i in range(4)]
+                    block = by_position(blocks, g).astype(jnp.float32)
                     if g > 0:
                         block = pltpu.roll(block, LANES - 32 * g, 1)
-                    field_ref[
-                        t, g * 2 * rows : (g + 1) * 2 * rows, tile * LANES : (tile + 1) * LANES
-                    ] = block.astype(jnp.bfloat16)
-
+                    wide_ref[g, f, col * span : (col + 1) * span, :] = block
+            for slot in range(SLOTS):
+                fields = [wide_ref[g, f, pl.ds(slot, rows, stride=SLOTS), :] for f in range(2)]
+                at = pl.multiple_of(k * LANES, LANES)
+                field_ref[slot, g * 2 * rows : (g + 1) * 2 * rows, pl.ds(at, LANES)] = (
+                    jnp.concatenate(fields, axis=0).astype(jnp.bfloat16)
+                )
+        return carry
+
+    lax.fori_loop(0, 8, build, 0)
+
+    def one_pair(p, carry):
+        @pl.when(p < 2)
+        def _():
+            leg_copy(p + 2).start()
+
+        leg_copy(p).wait()
         lower_order = order_ref[p]
         boundary = DEGREES - lower_order
         width = 256
+        late = (lower_order <= width).astype(jnp.int32)
+        at = pl.multiple_of(HALF + width * late, width)
+        extra = dot_nt(field_ref[4 * (1 - late) + p], leg_ref[p, pl.ds(at, width), :])
         for tile in range(DEGREES // width):
             start = tile * width
-            leg = leg_ref[p, start : start + width, :]
-            values = dot_nt(field_ref[0], leg)
+            values = dot_nt(field_ref[4 * (tile // 3) + p], leg_ref[p, start : start + width, :])
             if start >= HALF:
-                upper = dot_nt(field_ref[1], leg)
                 row = lax.broadcasted_iota(jnp.int32, values.shape, 1) + start
-                values = jnp.where(row < boundary, values, upper)
+                first, second = (values, extra) if tile == 2 else (extra, values)
+                values = jnp.where(row < boundary, first, second)
             coef_ref[p, :, start : start + width] = values
             moments = moments_of(values, rows)
             raw_ref[:, start : start + width] = moments
@@ -164,7 +215,7 @@
         last_leg = jnp.broadcast_to(
             leg_ref[p, DEGREES : DEGREES + 1, :].astype(jnp.float32), (LANES, DEGREES)
         )
-        last = dot_nt(field_ref[1], last_leg.astype(jnp.bfloat16))
+        last = dot_nt(field_ref[4 + p], last_leg.astype(jnp.bfloat16))
         last_ref[p] = last
         tail_ref[...] += moments_of(last, rows)
 
@@ -196,8 +247,12 @@
         moment_ref[tile * LANES : (tile + 1) * LANES, :] = total.T
 
 
-def in_vmem(*values):
-    return [pltpu.with_memory_space_constraint(value, pltpu.VMEM) for value in values]
+def in_vmem(value):
+    return pltpu.with_memory_space_constraint(value, pltpu.VMEM)
+
+
+def in_hbm(value):
+    return pltpu.with_memory_space_constraint(value, pltpu.HBM)
 
 
 def analysis(lower_order, arrived, legendre, count):
@@ -208,7 +263,7 @@
     whole = pl.BlockSpec(memory_space=pltpu.VMEM)
     return pl.pallas_call(
         functools.partial(analysis_kernel, count),
-        in_specs=[pl.BlockSpec(memory_space=pltpu.SMEM), whole, whole],
+        in_specs=[pl.BlockSpec(memory_space=pltpu.SMEM)] + [pl.BlockSpec(memory_space=pltpu.HBM)] * 2,
         out_specs=[whole, whole, whole],
         out_shape=[
             pltpu.VMEM((pairs, rows, DEGREES), jnp.float32),
@@ -216,12 +271,16 @@
             pltpu.VMEM((DEGREES, lanes), jnp.float32),
         ],
         scratch_shapes=[
-            pltpu.VMEM((2, 32, rows, LANES), jnp.float32),
-            pltpu.VMEM((2, rows, DEGREES), jnp.bfloat16),
+            pltpu.VMEM((32, 4, 2, count * SLOTS, LANES), jnp.bfloat16),
+            pltpu.VMEM(legendre.shape, jnp.bfloat16),
+            pltpu.VMEM((4, 2, rows, LANES), jnp.float32),
+            pltpu.VMEM((SLOTS, rows, DEGREES), jnp.bfloat16),
             pltpu.VMEM((24 * count, DEGREES), jnp.float32),
             pltpu.VMEM((24 * count, DEGREES + HALF), jnp.float32),
             pltpu.VMEM((24 * count, HALF), jnp.float32),
             pltpu.VMEM((24 * count, LANES), jnp.float32),
+            pltpu.SemaphoreType.DMA((8,)),
+            pltpu.SemaphoreType.DMA((4,)),
         ],
         compiler_params=pltpu.CompilerParams(vmem_limit_bytes=KERNEL_LIMIT),
         cost_estimate=pl.CostEstimate(
@@ -230,7 +289,7 @@
             transcendentals=0,
         ),
         name="analysis",
-    )(lower_order, *in_vmem(arrived, legendre))
+    )(lower_order, in_hbm(arrived), in_hbm(legendre))
 
 
 def factor_kernel(count, parts_ref, out_ref):
@@ -273,7 +332,7 @@
         compiler_params=pltpu.CompilerParams(vmem_limit_bytes=KERNEL_LIMIT),
         cost_estimate=pl.CostEstimate(flops=parts.size, bytes_accessed=8 * parts.size, transcendentals=0),
         name="factors",
-    )(*in_vmem(parts))
+    )(in_vmem(parts))
 
 
 def synthesis_kernel(
@@ -395,7 +454,7 @@
             transcendentals=0,
         ),
         name="synthesis",
-    )(lower_order, *in_vmem(coeffs, last, factors, legendre))
+    )(lower_order, *(in_vmem(value) for value in (coeffs, last, factors, legendre)))
 
 
 def unpack_kernel(turn_ref, pairs_ref, returned_ref, out_ref, lower_ref, upper_ref):
@@ -459,7 +518,7 @@
 
     by_group = (channels, 4, 32, DEGREES)
     packed = pack(
-        turn, pair_row, pred_four.reshape(by_group), target_four.reshape(by_group), 0, channels
+        turn, pair_row, pred_four.reshape(by_group), target_four.reshape(by_group), channels
     )
     arrived = exchange(packed.reshape(devices, 2 * channels * SLOTS, LANES))
     coeffs, last, moments = analysis(lower_order, arrived, legendre, channels)

time: 202 us -> 198 us (0.980)
  local copies, waits for them, and re-layouts: 19.4 us -> 13 us
    unnamed x15 -> x7, local copies, waits for them, and re-layouts: 19.3 us -> 12.9 us
    pallas_call x1, Pallas kernels: 4.55 us -> 7.5 us  [pack(): pl.pallas_call(functools.partial(pack_kernel, count), in_specs=[pl.BlockS...]
where the time goes in v3:
time: 198 us; the launch traced here: 197 us
  blocking collectives  86.6 us (44%)
  waiting for transfers between devices  54.3 us (27%)
  Pallas kernels  31.4 us (16%)
  local copies, waits for them, and re-layouts  13 us (7%)
  starting transfers between devices  11.9 us (6%)
    all_to_all x3, blocking collectives, exchange(): return lax.all_to_all(values, AXES, split_axis=0, concat_axis=0, tiled=True)  86.6 us
    all_to_all x1, waiting for transfers between devices, exchange(): return lax.all_to_all(values, AXES, split_axis=0, concat_axis=0, tiled=True)  54.3 us
    unnamed x7, local copies, waits for them, and re-layouts  12.9 us
    pallas_call x1, Pallas kernels, analysis(): pl.pallas_call(functools.partial(analysis_kernel, count), in_specs=[pl.Bl...  12.1 us
    all_to_all x1, starting transfers between devices, exchange(): return lax.all_to_all(values, AXES, split_axis=0, concat_axis=0, tiled=True)  11.9 us
    pallas_call x1, Pallas kernels, pack(): pl.pallas_call(functools.partial(pack_kernel, count), in_specs=[pl.BlockS...  7.5 us
    pallas_call x1, Pallas kernels, synthesis(): pl.pallas_call(functools.partial(synthesis_kernel, count), in_specs=[pl.B...  6.9 us
    pallas_call x1, Pallas kernels, unpack(): pl.pallas_call(unpack_kernel, grid_spec=grid_spec, out_shape=jax.ShapeDty...  4.47 us
  transfers between devices with their start and end apart: 1, of which 1 were waited for; matrix products, arithmetic and copies ran while one was open for 5% of the time, Pallas kernels for 0%

profile of v3, /device:TPU:1, one launch (start us, length us, event | category | flops | bytes accessed | tf_op | source)
XLA Modules:
  0.0 197.3 jit_solution(16458890531227543330)
XLA Ops:
  0.0 7.5 %pack.1 = bf16[128,2,5,16,128]{4,3,2,1,0:T(8,128)(2,1)} custom-call(s32[1]{0:T(128)} %bitcast.turn_ref, s32[1,512]{1,0:T(1,128)} %bitcast.13, bf16[10,4,32,1024]{3,2,1,0:T(8,128)(2,1)} %bitcast.16, bf16[10,4,32,1024]{3,2,1,0:T(8,128)(2,1)} %bitcast.17), custom_call_target="tpu_custom_call" | custom-call | flops 2684354560 | bytes 10485760 | tf_op jit(solution)/shard_map/pack/pallas_call | solution.py:105
  7.5 0.0 copy-start.1
  7.5 11.9 %all-to-all-start = ((bf16[128,160,128]{2,1,0:T(8,128)(2,1)}), bf16[128,160,128]{2,1,0:T(8,128)(2,1)}, u32[]{:S(2)}, u32[]{:S(2)}) async-start(bf16[128,160,128]{2,1,0:T(8,128)(2,1)} %bitcast.15), calls=%async_computation | async-start | bytes 10485760 | tf_op jit(solution)/shard_map/all_to_all | solution.py:507
  19.4 0.0 copy-done.1
  19.4 0.1 dynamic_slice.3.order_ref
  19.5 0.0 copy-start.2
  19.5 9.5 %copy.5.source_ref.leg_ref = bf16[4,1025,1024]{2,1,0:T(8,128)(2,1)} copy(bf16[4,1025,1024]{2,0,1:T(4,128)(2,1)} %param.6) | data formatting | bytes 16793600 | tf_op args[2]
  29.0 54.3 %all-to-all-done = bf16[128,160,128]{2,1,0:T(8,128)(2,1)} async-done(((bf16[128,160,128]{2,1,0:T(8,128)(2,1)}), bf16[128,160,128]{2,1,0:T(8,128)(2,1)}, u32[]{:S(2)}, u32[]{:S(2)}) %all-to-all-start) | async-done | bytes 5242912 | tf_op jit(solution)/shard_map/all_to_all | solution.py:507
  83.4 0.0 copy-done.2
  83.4 12.1 %analysis.1 = (f32[4,320,1024]{2,1,0:T(8,128)S(1)}, f32[4,320,128]{2,1,0:T(8,128)S(1)}, f32[1024,256]{1,0:T(8,128)S(1)}) custom-call(s32[4]{0:T(128)S(1)} %dynamic_slice.3.order_ref, bf16[32,4,2,80,128]{4,3,2,1,0:T(8,128)(2,1)} %bitcast.5.arrived_ref, bf16[4,1025,1024]{2,1,0:T(8,128)(2,1)} %copy.5.source_ref.leg_ref), custom_call_target="tpu_custom_call" | custom-call | flops 4026531840 | bytes 18882560 | tf_op jit(solution)/shard_map/analysis/pallas_call | solution.py:264
  95.5 23.8 %all_to_all.20.parts_ref = f32[128,8,256]{2,1,0:T(8,128)S(1)} all-to-all(f32[128,8,256]{2,1,0:T(8,128)S(1)} %bitcast.12), channel_id=1, replica_groups=mesh['ma'=32,'col'=4] {'ma','col'}, dimensions={0} | all-to-all | bytes 2097152 | tf_op jit(solution)/shard_map/all_to_all | solution.py:507
  119.3 0.4 factors.1
  119.7 23.0 %all_to_all.21 = f32[128,8,256]{2,1,0:T(8,128)S(1)} all-to-all(f32[128,8,256]{2,1,0:T(8,128)S(1)} %factors.1), channel_id=1, replica_groups=mesh['ma'=32,'col'=4] {'ma','col'}, dimensions={0} | all-to-all | bytes 2097152 | tf_op jit(solution)/shard_map/all_to_all | solution.py:507
  142.7 0.0 copy-start
  142.7 3.4 %copy-done = bf16[4,1025,1024]{2,1,0:T(8,128)(2,1)S(1)} copy-done((bf16[4,1025,1024]{2,1,0:T(8,128)(2,1)S(1)}, bf16[4,1025,1024]{2,1,0:T(8,128)(2,1)}, u32[]{:S(2)}) %copy-start) | copy-done | bytes 8396824
  146.1 6.9 %synthesis.1 = bf16[32,320,128]{2,1,0:T(8,128)(2,1)S(1)} custom-call(s32[4]{0:T(128)} %copy-done.2, f32[4,320,1024]{2,1,0:T(8,128)S(1)} %get-tuple-element.8.coef_ref, f32[4,320,128]{2,1,0:T(8,128)S(1)} %get-tuple-element.9.last_ref, f32[1024,256]{1,0:T(8,128)S(1)} %bitcast.11, bf16[4,1025,1024]{2,1,0:T(8,128)(2,1)S(1)} %copy-done), custom_call_target="tpu_custom_call" | custom-call | flops 2013265920 | bytes 16261120 | tf_op jit(solution)/shard_map/synthesis/pallas_call | solution.py:438
  153.0 39.8 %all_to_all.22.returned_ref = bf16[128,80,128]{2,1,0:T(8,128)(2,1)S(1)} all-to-all(bf16[128,80,128]{2,1,0:T(8,128)(2,1)S(1)} %bitcast.10), channel_id=1, replica_groups=mesh['ma'=32,'col'=4] {'ma','col'}, dimensions={0} | all-to-all | bytes 5242880 | tf_op jit(solution)/shard_map/all_to_all | solution.py:507
  192.8 4.5 %unpack.1 = bf16[10,4,32,1024]{3,2,1,0:T(8,128)(2,1)} custom-call(s32[1]{0:T(128)} %bitcast.turn_ref, s32[1,512]{1,0:T(1,128)S(1)} %bitcast.14, bf16[128,80,128]{2,1,0:T(8,128)(2,1)S(1)} %all_to_all.22.returned_ref), custom_call_target="tpu_custom_call" | custom-call | flops 1342177280 | bytes 5242880 | tf_op jit(solution)/shard_map/unpack/pallas_call | solution.py:492
Async XLA Ops:
  7.5 11.9 %copy-start.1 = (s32[512]{0:T(512)S(1)}, s32[512]{0:T(512)}, u32[]{:S(2)}) copy-start(s32[512]{0:T(512)} %param.7) | copy-start | bytes 6148
  7.5 75.8 %all-to-all-start = ((bf16[128,160,128]{2,1,0:T(8,128)(2,1)}), bf16[128,160,128]{2,1,0:T(8,128)(2,1)}, u32[]{:S(2)}, u32[]{:S(2)}) async-start(bf16[128,160,128]{2,1,0:T(8,128)(2,1)} %bitcast.15), calls=%async_computation | async-start | bytes 10485760 | tf_op jit(solution)/shard_map/all_to_all | solution.py:507
  19.5 63.9 %copy-start.2 = (s32[4]{0:T(128)}, s32[4]{0:T(128)S(1)}, u32[]{:S(2)}) copy-start(s32[4]{0:T(128)S(1)} %dynamic_slice.3.order_ref) | copy-start | bytes 52
  142.7 3.4 %copy-start = (bf16[4,1025,1024]{2,1,0:T(8,128)(2,1)S(1)}, bf16[4,1025,1024]{2,1,0:T(8,128)(2,1)}, u32[]{:S(2)}) copy-start(bf16[4,1025,1024]{2,1,0:T(8,128)(2,1)} %copy.5.source_ref.leg_ref) | copy-start | bytes 25190404

commit v4 on v3

v4 whole, which is shorter than its diff:
```python
import functools

import jax
import jax.numpy as jnp
from jax import lax
from jax.experimental import pallas as pl
from jax.experimental.pallas import tpu as pltpu
from jax.sharding import Mesh
from jax.sharding import PartitionSpec as P

DEGREES = 1024
HALF = DEGREES // 2
POWER_FLOOR = 0.5
LANES = 128
SLOTS = 8
PAIRS = 4
DEVICES = ("zx", "core", "col")
SAME_CORE = ("zx", "col")
KERNEL_LIMIT = 36 * 1024 * 1024
SMALL_LIMIT = 16 * 1024 * 1024
TINY_LIMIT = 4 * 1024 * 1024


def dot_nt(left, right):
    return lax.dot_general(left, right, (((1,), (1,)), ((), ())), preferred_element_type=jnp.float32)


def dot_nn(left, right):
    return lax.dot_general(left, right, (((1,), (0,)), ((), ())), preferred_element_type=jnp.float32)


def by_position(blocks, shift):
    group = lax.broadcasted_iota(jnp.int32, blocks[0].shape, 1) >> 5
    result = blocks[-shift % 4]
    for z in range(1, 4):
        result = jnp.where(group == z, blocks[(z - shift) % 4], result)
    return result


def trade_halves(first, second):
    top = lax.broadcasted_iota(jnp.int32, first.shape, 1) < 4
    return (
        jnp.where(top, first, pltpu.roll(second, 4, 1)),
        jnp.where(top, pltpu.roll(first, 4, 1), second),
    )


def one_hots(pairs_ref, lower_ref, upper_ref):
    order = jnp.broadcast_to(pairs_ref[...].astype(jnp.float32), (LANES, HALF)).T
    by_core = order.reshape(16, 2, 2, 8, LANES)
    first, second = by_core[:, 0].reshape(32, 8, LANES), by_core[:, 1].reshape(32, 8, LANES)
    order = jnp.stack(trade_halves(first, second), axis=1).reshape(HALF, LANES)
    order = jnp.concatenate([order] * (HALF // LANES), axis=1).astype(jnp.int32)
    lane = lax.broadcasted_iota(jnp.int32, (HALF, HALF), 1)
    lower_ref[...] = jnp.where(lane == order, 1.0, 0.0).astype(jnp.bfloat16)
    upper_ref[...] = jnp.where(lane == HALF - 1 - order, 1.0, 0.0).astype(jnp.bfloat16)


def pack_kernel(
    channels, turn_ref, pairs_hbm, pred_hbm, target_hbm, out_hbm,
    pairs_ref, field_ref, out_ref, lower_ref, upper_ref, pair_sem, in_sems, out_sems,
):
    steps = channels // 2
    ahead = 2

    def fetch(i, f):
        source = (pred_hbm, target_hbm)[f].at[pl.ds(2 * i, 2)]
        return pltpu.make_async_copy(source, field_ref.at[f, pl.ds(2 * i, 2)], in_sems.at[f, i])

    def send(i):
        return pltpu.make_async_copy(
            out_ref.at[i], out_hbm.at[:, :, :, pl.ds(2 * i, 2)], out_sems.at[i]
        )

    pair_copy = pltpu.make_async_copy(pairs_hbm, pairs_ref, pair_sem)
    pair_copy.start()
    for i in range(ahead):
        for f in range(2):
            fetch(i, f).start()
    pair_copy.wait()
    one_hots(pairs_ref, lower_ref, upper_ref)

    turn = turn_ref[0]

    def step(i, carry):
        @pl.when(i + ahead < steps)
        def _():
            for f in range(2):
                fetch(i + ahead, f).start()

        for f in range(2):
            fetch(i, f).wait()
        for c in range(2):
            pieces = []
            for sample in range(2):
                for z in range(4):
                    group = (z - turn) & 3
                    pieces.append(field_ref[group >> 1, 2 * i + c, 2 * sample + (group & 1)])
            field = jnp.concatenate(pieces, axis=0)
            low = dot_nt(lower_ref[...], field[:, :HALF]).reshape(HALF // 8, 8, 2 * LANES)
            high = dot_nt(upper_ref[...], field[:, HALF:]).reshape(HALF // 8, 8, 2 * LANES)
            both = jnp.concatenate([low, high], axis=1).astype(jnp.bfloat16)
            for sample in range(2):
                block = both[:, :, sample * LANES : (sample + 1) * LANES]
                out_ref[i, :, sample, :, c] = block.reshape(16, 4, 16, LANES)
        send(i).start()
        return carry

    lax.fori_loop(0, steps, step, 0)
    for i in range(steps):
        send(i).wait()


def pack(turn, pairs, pred, target):
    channels = pred.shape[0]
    steps = channels // 2
    far = pl.BlockSpec(memory_space=pltpu.HBM)
    return pl.pallas_call(
        functools.partial(pack_kernel, channels),
        in_specs=[pl.BlockSpec(memory_space=pltpu.SMEM), far, far, far],
        out_specs=far,
        out_shape=pltpu.HBM((16, 2, 4, channels, 16, LANES), jnp.bfloat16),
        scratch_shapes=[
            pltpu.VMEM((1, HALF), jnp.int32),
            pltpu.VMEM((2, channels, 4, 32, DEGREES), jnp.bfloat16),
            pltpu.VMEM((steps, 16, 2, 4, 2, 16, LANES), jnp.bfloat16),
            pltpu.VMEM((HALF, HALF), jnp.bfloat16),
            pltpu.VMEM((HALF, HALF), jnp.bfloat16),
            pltpu.SemaphoreType.DMA,
            pltpu.SemaphoreType.DMA((2, steps)),
            pltpu.SemaphoreType.DMA((steps,)),
        ],
        compiler_params=pltpu.CompilerParams(vmem_limit_bytes=KERNEL_LIMIT),
        cost_estimate=pl.CostEstimate(
            flops=DEGREES * DEGREES * 2 * LANES * channels,
            bytes_accessed=8 * LANES * DEGREES * channels,
            transcendentals=0,
        ),
        name="pack",
    )(turn, in_hbm(pairs), in_hbm(pred), in_hbm(target))


def moments_of(values, rows):
    shaped = values.reshape(2, 2, rows, values.shape[-1])
    pieces = []
    for left, right in ((0, 0), (1, 1), (0, 1)):
        real = shaped[left, 0] * shaped[right, 0]
        imag = shaped[left, 1] * shaped[right, 1]
        pieces.append(real + imag)
    return jnp.concatenate(pieces, axis=0)


def leg_stream(own_hbm, other_hbm, leg_ref, sems):
    def start(p):
        for hbm, here in ((own_hbm, p < PAIRS), (other_hbm, p >= PAIRS)):

            @pl.when(here)
            def _(hbm=hbm):
                at = p & 3
                pltpu.make_async_copy(hbm.at[at], leg_ref.at[at], sems.at[at]).start()

    def wait(p):
        at = p & 3
        pltpu.make_async_copy(own_hbm.at[at], leg_ref.at[at], sems.at[at]).wait()

    return start, wait


def analysis_kernel(
    rows, scalar_ref, arrived_ref, own_hbm, other_hbm, coef_ref, last_ref, moment_ref,
    narrow_ref, leg_ref, wide_ref, field_ref, lower_ref, upper_ref, tail_ref, sems, leg_sems,
):
    size = 3 * rows
    span = arrived_ref.shape[2]
    slots = 2 * SLOTS

    def chunk(k):
        at = pl.ds(4 * k, 4)
        return pltpu.make_async_copy(arrived_ref.at[at], narrow_ref.at[at], sems.at[k])

    start_leg, wait_leg = leg_stream(own_hbm, other_hbm, leg_ref, leg_sems)
    for k in range(8):
        chunk(k).start()
    lower_ref[...] = jnp.zeros_like(lower_ref)
    upper_ref[...] = jnp.zeros_like(upper_ref)
    tail_ref[...] = jnp.zeros_like(tail_ref)

    def build(k, carry):
        chunk(k).wait()

        @pl.when((k == 1) | (k == 3) | (k == 5))
        def _():
            start_leg(k >> 1)

        at = pl.multiple_of(k * LANES, LANES)
        for f in range(2):
            for q in range(2):
                g = 2 * f + q
                for col in range(4):
                    blocks = [narrow_ref[4 * k + i, col] for i in range(4)]
                    block = by_position(blocks, g).astype(jnp.float32)
                    if g > 0:
                        block = pltpu.roll(block, LANES - 32 * g, 1)
                    wide_ref[g, col * span : (col + 1) * span, :] = block
            for slot in range(slots):
                parts = [wide_ref[2 * f + q, pl.ds(slot, rows, stride=slots), :] for q in range(2)]
                low = 4 * rows * (slot // SLOTS) + 2 * f * rows
                field_ref[slot % SLOTS, low : low + 2 * rows, pl.ds(at, LANES)] = jnp.concatenate(
                    parts, axis=0
                ).astype(jnp.bfloat16)
        return carry

    lax.fori_loop(0, 8, build, 0)
    core = scalar_ref[2 * PAIRS]

    def one_pair(p, carry):
        @pl.when(p + 3 < 2 * PAIRS)
        def _():
            start_leg(p + 3)

        wait_leg(p)
        ring = p & 3
        slot = p ^ (core * PAIRS)
        lower_order = scalar_ref[p]
        boundary = DEGREES - lower_order
        width = 256
        lower_weight = jnp.where(lower_order == 0, 1.0, 2.0)
        tiles_up = lower_order >> 7
        lanes_up = lower_order & (LANES - 1)
        lane = lax.broadcasted_iota(jnp.int32, (size, LANES), 1)
        before = jnp.zeros((size, LANES), jnp.float32)
        for tile in range(DEGREES // width):
            start = tile * width
            count = 4 * rows if start < HALF else 8 * rows
            values = dot_nt(field_ref[slot, :count], leg_ref[ring, start : start + width, :])
            if start >= HALF:
                lower, upper = values[: 4 * rows], values[4 * rows :]
                row = lax.broadcasted_iota(jnp.int32, lower.shape, 1) + start
                values = jnp.where(row < boundary, lower, upper)
            coef_ref[p, :, start : start + width] = values
            for sub in range(width // LANES):
                moments = moments_of(values[:, sub * LANES : (sub + 1) * LANES], rows)
                now = start + sub * LANES
                if start >= HALF:
                    upper_ref[:, now - HALF : now - HALF + LANES] += jnp.where(
                        lane + now < boundary, 0.0, moments
                    )
                turned = pltpu.roll(moments, lanes_up, 1)
                at = pl.multiple_of(now + tiles_up * LANES, LANES)
                lower_ref[:, pl.ds(at, LANES)] += lower_weight * jnp.where(
                    lane < lanes_up, before, turned
                )
                before = turned
        last_leg = jnp.broadcast_to(
            leg_ref[ring, DEGREES : DEGREES + 1, :].astype(jnp.float32), (LANES, DEGREES)
        )
        last = dot_nt(field_ref[slot, 4 * rows :], last_leg.astype(jnp.bfloat16))
        last_ref[p] = last
        tail_ref[...] += moments_of(last, rows)
        return carry

    lax.fori_loop(0, 2 * PAIRS, one_pair, 0)

    lane = lax.broadcasted_iota(jnp.int32, (size, LANES), 1)
    after = tail_ref[...]
    for tile in reversed(range(8)):
        total = lower_ref[:, tile * LANES : (tile + 1) * LANES]
        if tile >= 4:
            turned = pltpu.roll(upper_ref[:, (tile - 4) * LANES : (tile - 3) * LANES], LANES - 1, 1)
            total = total + 2.0 * jnp.where(lane == LANES - 1, after, turned)
            after = turned
        total = jnp.concatenate([total, jnp.zeros((LANES - size, LANES), jnp.float32)], axis=0)
        moment_ref[tile * LANES : (tile + 1) * LANES, :] = total.T


def in_vmem(value):
    return pltpu.with_memory_space_constraint(value, pltpu.VMEM)


def in_hbm(value):
    return pltpu.with_memory_space_constraint(value, pltpu.HBM)


def analysis(scalars, arrived, own, other, rows):
    leg_rows = own.shape[1]
    span = rows * 4
    arrived = arrived.reshape(32, 4, span, LANES)
    whole = pl.BlockSpec(memory_space=pltpu.VMEM)
    far = pl.BlockSpec(memory_space=pltpu.HBM)
    return pl.pallas_call(
        functools.partial(analysis_kernel, rows),
        in_specs=[pl.BlockSpec(memory_space=pltpu.SMEM), far, far, far],
        out_specs=[whole, whole, whole],
        out_shape=[
            pltpu.VMEM((2 * PAIRS, 4 * rows, DEGREES), jnp.float32),
            pltpu.VMEM((2 * PAIRS, 4 * rows, LANES), jnp.float32),
            pltpu.VMEM((DEGREES, LANES), jnp.float32),
        ],
        scratch_shapes=[
            pltpu.VMEM((32, 4, span, LANES), jnp.bfloat16),
            pltpu.VMEM((4, leg_rows, DEGREES), jnp.bfloat16),
            pltpu.VMEM((4, 4 * span, LANES), jnp.float32),
            pltpu.VMEM((SLOTS, 8 * rows, DEGREES), jnp.bfloat16),
            pltpu.VMEM((3 * rows, DEGREES + HALF), jnp.float32),
            pltpu.VMEM((3 * rows, HALF), jnp.float32),
            pltpu.VMEM((3 * rows, LANES), jnp.float32),
            pltpu.SemaphoreType.DMA((8,)),
            pltpu.SemaphoreType.DMA((4,)),
        ],
        compiler_params=pltpu.CompilerParams(vmem_limit_bytes=KERNEL_LIMIT),
        cost_estimate=pl.CostEstimate(
            flops=20 * rows * PAIRS * DEGREES * DEGREES,
            bytes_accessed=4 * own.size + 16 * rows * PAIRS * DEGREES + 2 * arrived.size,
            transcendentals=0,
        ),
        name="analysis",
    )(scalars, in_hbm(arrived), in_hbm(own), in_hbm(other))


def factor_kernel(span, parts_ref, out_ref):
    total = jnp.sum(parts_ref[...], axis=0)
    size = total.shape[1]
    power_pred = total
    power_true = pltpu.roll(total, size - span, 1)
    cross = pltpu.roll(total, size - 2 * span, 1)
    pred = jnp.maximum(power_pred, POWER_FLOOR)
    true = jnp.maximum(power_true, POWER_FLOOR)
    root_pred = jnp.sqrt(pred)
    root_true = jnp.sqrt(true)
    both = pred + true
    upper_mean = (pred * pred + true * true) / both
    inverse = 1.0 / (root_pred * root_true)
    coherence = cross * inverse
    mean_slope = (2.0 * pred - upper_mean) / both
    slope = (
        (root_pred - root_true) / root_pred
        + 2.0 * mean_slope * (1.0 - coherence)
        + upper_mean * coherence / pred
    )
    binds = jnp.where(power_pred > POWER_FLOOR, 1.0, jnp.where(power_pred == POWER_FLOOR, 0.5, 0.0))
    dpower = 2.0 * slope * binds
    dcross = -2.0 * upper_mean * inverse
    lane = lax.broadcasted_iota(jnp.int32, total.shape, 1)
    factors = jnp.where(lane < span, dpower, pltpu.roll(dcross, span, 1))
    out_ref[...] = jnp.broadcast_to(factors[None], out_ref.shape)


def factors_of(parts, rows):
    whole = pl.BlockSpec(memory_space=pltpu.VMEM)
    return pl.pallas_call(
        functools.partial(factor_kernel, rows),
        in_specs=[whole],
        out_specs=whole,
        out_shape=pltpu.VMEM(parts.shape, jnp.float32),
        compiler_params=pltpu.CompilerParams(vmem_limit_bytes=TINY_LIMIT),
        cost_estimate=pl.CostEstimate(flops=parts.size, bytes_accessed=8 * parts.size, transcendentals=0),
        name="factors",
    )(in_vmem(parts))


def synthesis_kernel(
    rows, scalar_ref, coef_ref, last_ref, factor_ref, own_ref, other_ref, out_ref,
    spread_ref, upspread_ref, early_ref, late_ref, wide_ref,
):
    size = 2 * rows
    lane = lax.broadcasted_iota(jnp.int32, (size, LANES), 1)
    before = None
    for tile in range(8):
        turned = factor_ref[tile * LANES : (tile + 1) * LANES, :].T[:size]
        spread_ref[:, tile * LANES : (tile + 1) * LANES] = turned
        shifted = pltpu.roll(turned, 1, 1)
        if tile >= 4:
            upspread_ref[:, (tile - 4) * LANES : (tile - 3) * LANES] = 2.0 * jnp.where(
                lane == 0, before, shifted
            )
        before = shifted
    core = scalar_ref[2 * PAIRS]

    def one_pair(leg_ref, first, ring, carry):
        p = first + ring
        slot = p ^ (core * PAIRS)
        lower_order = scalar_ref[p]
        boundary = DEGREES - lower_order
        lower_weight = jnp.where(lower_order == 0, 1.0, 2.0)
        tiles_up = lower_order >> 7
        lanes_up = lower_order & (LANES - 1)
        back = (LANES - lanes_up) & (LANES - 1)

        def turned_tile(tile):
            at = pl.multiple_of((tile + tiles_up) * LANES, LANES)
            return pltpu.roll(spread_ref[:, pl.ds(at, LANES)], back, 1)

        def graded(factors, observe):
            grads = []
            for q in range(2):
                predicted = observe(q * rows)
                observed = observe((2 + q) * rows)
                grads.append(factors[:rows] * predicted + factors[rows:] * observed)
            return jnp.concatenate(grads, axis=0)

        now = turned_tile(0)
        for tile in range(8):
            start = tile * LANES
            then = turned_tile(tile + 1)
            factors = lower_weight * jnp.where(lane < LANES - lanes_up, now, then)
            now = then
            row = lane + start
            if tile >= 4:
                factors = jnp.where(
                    row < boundary, factors, upspread_ref[:, start - HALF : start - HALF + LANES]
                )
            grad = graded(factors, lambda at: coef_ref[p, at : at + rows, start : start + LANES])
            if tile >= 4:
                at = start - HALF
                late_ref[:size, at : at + LANES] = jnp.where(row < boundary, grad, 0.0).astype(
                    jnp.bfloat16
                )
                late_ref[size:, at : at + LANES] = jnp.where(row < boundary, 0.0, grad).astype(
                    jnp.bfloat16
                )
            else:
                early_ref[:, start : start + LANES] = grad.astype(jnp.bfloat16)
        last_factors = jnp.broadcast_to(2.0 * spread_ref[:, DEGREES - 1 : DEGREES], (size, LANES))
        last_grad = graded(last_factors, lambda at: last_ref[p, at : at + rows, :])
        last_grad = last_grad.astype(jnp.bfloat16).astype(jnp.float32)
        last_leg = leg_ref[ring, DEGREES : DEGREES + 1, :].astype(jnp.float32)

        width = 256
        for tile in range(DEGREES // width):
            start = tile * width
            early = dot_nn(early_ref[...], leg_ref[ring, :HALF, start : start + width])
            late = dot_nn(late_ref[...], leg_ref[ring, HALF:DEGREES, start : start + width])
            lower, upper = early + late[:size], late[size:]
            for sub in range(width // LANES):
                at = start + sub * LANES
                inside = slice(sub * LANES, (sub + 1) * LANES)
                top = lower[:, inside]
                bottom = upper[:, inside] + last_grad * last_leg[:, at : at + LANES]
                blocks = [top[:rows], top[rows:], bottom[:rows], bottom[rows:]]
                blocks = [
                    block if g == 0 else pltpu.roll(block, 32 * g, 1) for g, block in enumerate(blocks)
                ]
                for i in range(4):
                    wide_ref[at // 32 + i, pl.ds(slot, rows, stride=SLOTS), :] = by_position(blocks, i)
        return carry

    lax.fori_loop(0, PAIRS, functools.partial(one_pair, own_ref, 0), 0)
    lax.fori_loop(0, PAIRS, functools.partial(one_pair, other_ref, PAIRS), 0)

    def narrow(j, carry):
        out_ref[j] = wide_ref[j].astype(jnp.bfloat16)
        return carry

    lax.fori_loop(0, 32, narrow, 0)


def synthesis(scalars, coeffs, last, factors, own, other, rows):
    whole = pl.BlockSpec(memory_space=pltpu.VMEM)
    return pl.pallas_call(
        functools.partial(synthesis_kernel, rows),
        in_specs=[pl.BlockSpec(memory_space=pltpu.SMEM)] + [whole] * 5,
        out_specs=whole,
        out_shape=pltpu.VMEM((32, rows * SLOTS, LANES), jnp.bfloat16),
        scratch_shapes=[
            pltpu.VMEM((2 * rows, DEGREES + HALF), jnp.float32),
            pltpu.VMEM((2 * rows, HALF), jnp.float32),
            pltpu.VMEM((2 * rows, HALF), jnp.bfloat16),
            pltpu.VMEM((4 * rows, HALF), jnp.bfloat16),
            pltpu.VMEM((32, rows * SLOTS, LANES), jnp.float32),
        ],
        compiler_params=pltpu.CompilerParams(vmem_limit_bytes=SMALL_LIMIT),
        cost_estimate=pl.CostEstimate(
            flops=12 * rows * PAIRS * DEGREES * DEGREES,
            bytes_accessed=4 * own.size + 16 * rows * PAIRS * DEGREES + 64 * rows * SLOTS * LANES,
            transcendentals=0,
        ),
        name="synthesis",
    )(scalars, *(in_vmem(value) for value in (coeffs, last, factors, own, other)))


def unpack_kernel(turn_ref, pairs_ref, returned_ref, out_ref, lower_ref, upper_ref):
    @pl.when(pl.program_id(0) == 0)
    def _():
        one_hots(pairs_ref, lower_ref, upper_ref)

    turn = turn_ref[0]
    both = returned_ref[...].astype(jnp.float32)
    sides = []
    for c in range(2):
        first, second = (
            both[:, sample, :, c * SLOTS : (c + 1) * SLOTS].reshape(HALF, LANES) for sample in range(2)
        )
        group = lax.broadcasted_iota(jnp.int32, first.shape, 1) >> 5
        keep = ((group - turn) & 3) < 2
        sides.append(
            (
                jnp.where(keep, first, pltpu.roll(second, 64, 1)),
                jnp.where(keep, pltpu.roll(first, 64, 1), second),
            )
        )
    for o, one_hot_ref in enumerate((lower_ref, upper_ref)):
        by_slot = jnp.concatenate([side[o] for side in sides], axis=1)
        field = dot_nn(by_slot.T.astype(jnp.bfloat16), one_hot_ref[...]).astype(jnp.bfloat16)
        for c in range(2):
            for z in range(4):
                at = c * LANES + z * 32
                out_ref[c, (z - turn) & 3, :, o * HALF : (o + 1) * HALF] = field[at : at + 32]


def unpack(turn, pairs, returned, channels):
    grid_spec = pltpu.PrefetchScalarGridSpec(
        num_scalar_prefetch=1,
        grid=(channels // 2,),
        in_specs=[
            pl.BlockSpec((1, HALF), lambda i, t: (0, 0)),
            pl.BlockSpec((16, 2, 4, 16, LANES), lambda i, t: (0, 0, 0, i, 0)),
        ],
        out_specs=pl.BlockSpec((2, 4, 32, DEGREES), lambda i, t: (i, 0, 0, 0)),
        scratch_shapes=[pltpu.VMEM((HALF, HALF), jnp.bfloat16)] * 2,
    )
    return pl.pallas_call(
        unpack_kernel,
        grid_spec=grid_spec,
        out_shape=jax.ShapeDtypeStruct((channels, 4, 32, DEGREES), jnp.bfloat16),
        compiler_params=pltpu.CompilerParams(vmem_limit_bytes=SMALL_LIMIT),
        cost_estimate=pl.CostEstimate(
            flops=DEGREES * DEGREES * LANES * channels,
            bytes_accessed=4 * LANES * DEGREES * channels,
            transcendentals=0,
        ),
        name="unpack",
    )(turn, pairs, returned)


def exchange(values, axes):
    return lax.all_to_all(values, axes, split_axis=0, concat_axis=0, tiled=True)


def per_device(pred_four, target_four, legendre, pair_order):
    channels = pred_four.shape[0]
    devices = DEGREES // SLOTS
    rows = 4 * channels
    core = lax.axis_index("core")
    device = lax.axis_index(DEVICES)
    turn = ((2 * lax.axis_index("zx") + core) & 3).reshape(1)
    pair_row = pair_order.reshape(1, HALF)
    other_legendre = lax.ppermute(legendre, "core", [(0, 1), (1, 0)])
    own_order = lax.dynamic_slice_in_dim(pair_order, device * PAIRS, PAIRS)
    other_order = lax.dynamic_slice_in_dim(pair_order, (device ^ 4) * PAIRS, PAIRS)
    scalars = jnp.concatenate([own_order, other_order, core.astype(jnp.int32).reshape(1)])

    by_group = (channels, 4, 32, DEGREES)
    packed = pack(turn, pair_row, pred_four.reshape(by_group), target_four.reshape(by_group))
    arrived = exchange(packed.reshape(devices, rows * 4, LANES), DEVICES)
    coeffs, last, moments = analysis(scalars, arrived, legendre, other_legendre, rows)
    spectra = exchange(moments.reshape(devices // 2, 2 * SLOTS, LANES), SAME_CORE)
    factors = exchange(factors_of(spectra, rows), SAME_CORE).reshape(DEGREES, LANES)
    going = synthesis(scalars, coeffs, last, factors, legendre, other_legendre, rows)
    returned = exchange(going.reshape(devices, rows * 2, LANES), DEVICES)
    returned = returned.reshape(16, 2, 4, rows * 2, LANES)
    return unpack(turn, pair_row, returned, channels).reshape(pred_four.shape)


def solution(mesh):
    by_core = Mesh(mesh.devices.reshape(16, 2, 4), DEVICES)
    field = P("col", None, None, ("zx", "core"), None)
    return jax.shard_map(
        per_device,
        mesh=by_core,
        in_specs=(field, field, P(DEVICES, None, None), P()),
        out_specs=field,
        check_vma=False,
    )
```

time: 198 us -> 187 us (0.944)
  blocking collectives: 86.6 us -> 74.7 us
  waiting for transfers between devices: 54.3 us -> 44.7 us
  local copies, waits for them, and re-layouts: 13 us -> 19.1 us
  Pallas kernels: 31.4 us -> 36.1 us
    all_to_all x3, blocking collectives: 86.6 us -> 74.7 us  [exchange(): return lax.all_to_all(values, axes, split_axis=0, concat_axis=0, tiled=True)]
    all_to_all x1, waiting for transfers between devices: 54.3 us -> 44.7 us  [exchange(): return lax.all_to_all(values, axes, split_axis=0, concat_axis=0, tiled=True)]
    ppermute x0 -> x1, local copies, waits for them, and re-layouts: none -> 9.5 us  [per_device(): other_legendre = lax.ppermute(legendre, 'core', [(0, 1), (1, 0)])]
    pallas_call x4, Pallas kernels: 26.9 us -> 31 us  [the longest x1 16.8 us: analysis(): pl.pallas_call(functools.partial(analysis_kernel, rows), in_specs=[pl.Blo...]
    unnamed x7 -> x15, local copies, waits for them, and re-layouts: 12.9 us -> 9.55 us
  transfers between devices with their start and end apart: 1 -> 2, of which waited for: 1 -> 1; matrix products, arithmetic and copies ran while one was open for 5% -> 10% of each run, Pallas kernels for 0% -> 4%
where the time goes in v4:
time: 187 us
  blocking collectives  74.7 us (40%)
  waiting for transfers between devices  44.7 us (24%)
  Pallas kernels  36.1 us (19%)
  local copies, waits for them, and re-layouts  19.1 us (10%)
  starting transfers between devices  12 us (6%)
    all_to_all x3, blocking collectives, exchange(): return lax.all_to_all(values, axes, split_axis=0, concat_axis=0, tiled=True)  74.7 us
    all_to_all x1, waiting for transfers between devices, exchange(): return lax.all_to_all(values, axes, split_axis=0, concat_axis=0, tiled=True)  44.7 us
    pallas_call x1, Pallas kernels, analysis(): pl.pallas_call(functools.partial(analysis_kernel, rows), in_specs=[pl.Blo...  16.8 us
    all_to_all x1, starting transfers between devices, exchange(): return lax.all_to_all(values, axes, split_axis=0, concat_axis=0, tiled=True)  10.6 us
    unnamed x15, local copies, waits for them, and re-layouts  9.55 us
    ppermute x1, local copies, waits for them, and re-layouts, per_device(): other_legendre = lax.ppermute(legendre, 'core', [(0, 1), (1, 0)])  9.5 us
    pallas_call x1, Pallas kernels, synthesis(): pl.pallas_call(functools.partial(synthesis_kernel, rows), in_specs=[pl.Bl...  7.38 us
    pallas_call x1, Pallas kernels, pack(): pl.pallas_call(functools.partial(pack_kernel, channels), in_specs=[pl.Blo...  6.6 us
  transfers between devices with their start and end apart: 2, of which 1 were waited for; matrix products, arithmetic and copies ran while one was open for 10% of the time, Pallas kernels for 4%

profile of v4, /device:TPU:1, one launch (start us, length us, event | category | flops | bytes accessed | tf_op | source)
XLA Modules:
  0.0 186.9 jit_solution(17565829945337480303)
XLA Ops:
  0.0 1.4 collective-permute-start
  1.4 6.6 %pack.1 = bf16[16,2,4,10,16,128]{5,4,3,2,1,0:T(8,128)(2,1)} custom-call(s32[1]{0:T(128)} %bitcast.turn_ref, s32[1,512]{1,0:T(1,128)} %bitcast.20, bf16[10,4,32,1024]{3,2,1,0:T(8,128)(2,1)} %bitcast.23, bf16[10,4,32,1024]{3,2,1,0:T(8,128)(2,1)} %bitcast.24), custom_call_target="tpu_custom_call" | custom-call | flops 2684354560 | bytes 10485760 | tf_op jit(solution)/shard_map/pack/pallas_call | solution.py:118
  8.0 10.6 %all-to-all-start = ((bf16[128,160,128]{2,1,0:T(8,128)(2,1)}), bf16[128,160,128]{2,1,0:T(8,128)(2,1)}, u32[]{:S(2)}, u32[]{:S(2)}) async-start(bf16[128,160,128]{2,1,0:T(8,128)(2,1)} %bitcast.22), calls=%async_computation | async-start | bytes 10485760 | tf_op jit(solution)/shard_map/all_to_all | solution.py:536
  18.7 0.0 copy-start
  18.7 9.5 %copy.8.own_hbm.own_ref = bf16[4,1025,1024]{2,1,0:T(8,128)(2,1)} copy(bf16[4,1025,1024]{2,0,1:T(4,128)(2,1)} %param.6) | data formatting | bytes 16793600 | tf_op args[2]
  28.2 0.0 copy-done
  28.2 0.1 fusion
  28.3 0.1 pad_add_fusion.scalar_ref
  28.4 0.0 collective-permute-done
  28.4 9.5 %copy.9.other_hbm.other_ref = bf16[4,1025,1024]{2,1,0:T(8,128)(2,1)} copy(bf16[4,1025,1024]{2,0,1:T(4,128)(2,1)} %collective-permute-done) | data formatting | bytes 16793600 | tf_op jit(solution)/shard_map/ppermute | solution.py:547
  37.9 44.7 %all-to-all-done = bf16[128,160,128]{2,1,0:T(8,128)(2,1)} async-done(((bf16[128,160,128]{2,1,0:T(8,128)(2,1)}), bf16[128,160,128]{2,1,0:T(8,128)(2,1)}, u32[]{:S(2)}, u32[]{:S(2)}) %all-to-all-start) | async-done | bytes 5242912 | tf_op jit(solution)/shard_map/all_to_all | solution.py:536
  82.6 0.0 slice-start
  82.6 0.0 slice-start.3
  82.6 0.0 slice-start.1
  82.6 0.0 slice-start.2
  82.6 0.0 slice-start.4
  82.6 0.0 slice-start.5
  82.6 16.8 %analysis.1 = (f32[8,160,1024]{2,1,0:T(8,128)S(1)}, f32[8,160,128]{2,1,0:T(8,128)S(1)}, f32[1024,128]{1,0:T(8,128)S(1)}) custom-call(s32[9]{0:T(128)S(1)} %pad_add_fusion.scalar_ref, bf16[32,4,160,128]{3,2,1,0:T(8,128)(2,1)} %bitcast.6.arrived_ref, bf16[4,1025,1024]{2,1,0:T(8,128)(2,1)} %copy.8.own_hbm.own_ref, bf16[4,1025,1024]{2,1,0:T(8,128)(2,1)} %copy.9.other_hbm.other_ref), custom_call_target="tpu_custom_call" | custom-call | flops 3355443200 | bytes 24657920 | tf_op jit(solution)/shard_map/analysis/pallas_call | solution.py:290
  99.4 16.6 %all_to_all.20.parts_ref = f32[64,16,128]{2,1,0:T(8,128)S(1)} all-to-all(f32[64,16,128]{2,1,0:T(8,128)S(1)} %bitcast.19), channel_id=1, replica_groups=mesh['zx'=16,'core'=2,'col'=4] {'zx','col'}, dimensions={0} | all-to-all | bytes 1048576 | tf_op jit(solution)/shard_map/all_to_all | solution.py:536
  116.0 0.2 factors.1
  116.2 15.2 %all_to_all.21 = f32[64,16,128]{2,1,0:T(8,128)S(1)} all-to-all(f32[64,16,128]{2,1,0:T(8,128)S(1)} %factors.1), channel_id=1, replica_groups=mesh['zx'=16,'core'=2,'col'=4] {'zx','col'}, dimensions={0} | all-to-all | bytes 1048576 | tf_op jit(solution)/shard_map/all_to_all | solution.py:536
  131.5 0.0 slice-done
  131.5 0.0 slice-done.3
  131.5 0.0 slice-done.1
  131.5 0.0 slice-done.2
  131.5 0.0 slice-done.4
  131.5 0.0 slice-done.5
  131.5 7.4 %synthesis.1 = bf16[32,320,128]{2,1,0:T(8,128)(2,1)S(1)} custom-call(s32[9]{0:T(128)S(1)} %pad_add_fusion.scalar_ref, f32[8,160,1024]{2,1,0:T(8,128)S(1)} %get-tuple-element.8.coef_ref, f32[8,160,128]{2,1,0:T(8,128)S(1)} %get-tuple-element.9.last_ref, f32[1024,128]{1,0:T(8,128)S(1)} %bitcast.18, bf16[4,1025,1024]{2,1,0:T(8,128)(2,1)S(1)} %bitcast.13, ...), custom_call_target="tpu_custom_call" | custom-call | flops 2013265920 | bytes 22036480 | tf_op jit(solution)/shard_map/synthesis/pallas_call | solution.py:459
  138.9 42.9 %all_to_all.22 = bf16[128,80,128]{2,1,0:T(8,128)(2,1)S(1)} all-to-all(bf16[128,80,128]{2,1,0:T(8,128)(2,1)S(1)} %bitcast.17), channel_id=1, replica_groups=mesh['zx'=16,'core'=2,'col'=4] {'zx','core','col'}, dimensions={0} | all-to-all | bytes 5242880 | tf_op jit(solution)/shard_map/all_to_all | solution.py:536
  181.8 5.1 %unpack.1 = bf16[10,4,32,1024]{3,2,1,0:T(8,128)(2,1)} custom-call(s32[1]{0:T(128)} %bitcast.turn_ref, s32[1,512]{1,0:T(1,128)S(1)} %bitcast.21, bf16[16,2,4,80,128]{4,3,2,1,0:T(8,128)(2,1)S(1)} %bitcast.16), custom_call_target="tpu_custom_call" | custom-call | flops 1342177280 | bytes 5242880 | tf_op jit(solution)/shard_map/unpack/pallas_call | solution.py:521
  (2 shorter events, 0.0 us)
Async XLA Ops:
  0.0 28.4 %collective-permute-start = (bf16[4,1025,1024]{2,0,1:T(4,128)(2,1)}, bf16[4,1025,1024]{2,0,1:T(4,128)(2,1)}, u32[]{:S(2)}, u32[]{:S(2)}) collective-permute-start(bf16[4,1025,1024]{2,0,1:T(4,128)(2,1)} %param.6), channel_id=1, source_target_pairs={{0,4},{4,0},{1,5},{5,1},{2,6},{6,2},{3,7},{7,3},{8,12},{12,8},{9,1... | collective-permute-start | bytes 25190408 | tf_op jit(solution)/shard_map/ppermute | solution.py:547
  8.0 74.6 %all-to-all-start = ((bf16[128,160,128]{2,1,0:T(8,128)(2,1)}), bf16[128,160,128]{2,1,0:T(8,128)(2,1)}, u32[]{:S(2)}, u32[]{:S(2)}) async-start(bf16[128,160,128]{2,1,0:T(8,128)(2,1)} %bitcast.22), calls=%async_computation | async-start | bytes 10485760 | tf_op jit(solution)/shard_map/all_to_all | solution.py:536
  18.7 9.5 %copy-start = (s32[512]{0:T(512)S(1)}, s32[512]{0:T(512)}, u32[]{:S(2)}) copy-start(s32[512]{0:T(512)} %param.7) | copy-start | bytes 6148
  82.6 48.9 %slice-start = ((s8[8454144]{0:T(1024)(128)(4,1)}), s8[4194304]{0:T(1024)(128)(4,1)S(1)}, s32[]{:S(2)}) async-start(s8[8454144]{0:T(1024)(128)(4,1)} %bitcast.12), calls=%async_computation.4 | async-start | bytes 8388608
  82.6 48.9 %slice-start.3 = ((s8[8454144]{0:T(1024)(128)(4,1)}), s8[4194304]{0:T(1024)(128)(4,1)S(1)}, s32[]{:S(2)}) async-start(s8[8454144]{0:T(1024)(128)(4,1)} %bitcast.14), calls=%async_computation.7 | async-start | bytes 8388608
  82.6 48.9 %slice-start.1 = ((s8[8454144]{0:T(1024)(128)(4,1)}), s8[4194304]{0:T(1024)(128)(4,1)S(1)}, s32[]{:S(2)}) async-start(s8[8454144]{0:T(1024)(128)(4,1)} %bitcast.12), calls=%async_computation.5 | async-start | bytes 8388608
  82.6 48.9 %slice-start.2 = ((s8[8454144]{0:T(1024)(128)(4,1)}), s8[65536]{0:T(1024)(128)(4,1)S(1)}, s32[]{:S(2)}) async-start(s8[8454144]{0:T(1024)(128)(4,1)} %bitcast.12), calls=%async_computation.6 | async-start | bytes 131072
  82.6 48.9 %slice-start.4 = ((s8[8454144]{0:T(1024)(128)(4,1)}), s8[4194304]{0:T(1024)(128)(4,1)S(1)}, s32[]{:S(2)}) async-start(s8[8454144]{0:T(1024)(128)(4,1)} %bitcast.14), calls=%async_computation.8 | async-start | bytes 8388608
  82.6 48.9 %slice-start.5 = ((s8[8454144]{0:T(1024)(128)(4,1)}), s8[65536]{0:T(1024)(128)(4,1)S(1)}, s32[]{:S(2)}) async-start(s8[8454144]{0:T(1024)(128)(4,1)} %bitcast.14), calls=%async_computation.9 | async-start | bytes 131072

commit v5 on v4

--- a/solution.py
+++ b/solution.py
@@ -27,6 +27,10 @@
 
 def dot_nn(left, right):
     return lax.dot_general(left, right, (((1,), (0,)), ((), ())), preferred_element_type=jnp.float32)
+
+
+def dot_tn(left, right):
+    return lax.dot_general(left, right, (((0,), (0,)), ((), ())), preferred_element_type=jnp.float32)
 
 
 def by_position(blocks, shift):
@@ -167,8 +171,8 @@
 
 
 def analysis_kernel(
-    rows, scalar_ref, arrived_ref, own_hbm, other_hbm, coef_ref, last_ref, moment_ref,
-    narrow_ref, leg_ref, wide_ref, field_ref, lower_ref, upper_ref, tail_ref, sems, leg_sems,
+    rows, scalar_ref, arrived_ref, edge_ref, own_hbm, other_hbm, coef_ref, last_ref, moment_ref,
+    narrow_ref, leg_ref, sort_ref, turned_edge_ref, field_ref, lower_ref, upper_ref, tail_ref, sems, leg_sems,
 ):
     size = 3 * rows
     span = arrived_ref.shape[2]
@@ -184,6 +188,12 @@
     lower_ref[...] = jnp.zeros_like(lower_ref)
     upper_ref[...] = jnp.zeros_like(upper_ref)
     tail_ref[...] = jnp.zeros_like(tail_ref)
+    edges = jnp.concatenate([edge_ref[...], jnp.zeros((LANES - SLOTS, DEGREES), jnp.float32)], axis=0)
+    turned_edge_ref[...] = edges.T.astype(jnp.bfloat16)
+    row = lax.broadcasted_iota(jnp.int32, (LANES, LANES), 0)
+    column = lax.broadcasted_iota(jnp.int32, (LANES, LANES), 1)
+    takes = column == (row & (SLOTS - 1)) * slots + (row >> 3)
+    sort_ref[...] = jnp.where(takes, 1.0, 0.0).astype(jnp.bfloat16)
 
     def build(k, carry):
         chunk(k).wait()
@@ -194,16 +204,27 @@
 
         at = pl.multiple_of(k * LANES, LANES)
         for f in range(2):
-            for q in range(2):
-                g = 2 * f + q
-                for col in range(4):
-                    blocks = [narrow_ref[4 * k + i, col] for i in range(4)]
-                    block = by_position(blocks, g).astype(jnp.float32)
+            tiles = []
+            for col in range(4):
+                both = []
+                for q in range(2):
+                    g = 2 * f + q
+                    block = by_position([narrow_ref[4 * k + i, col] for i in range(4)], g)
                     if g > 0:
                         block = pltpu.roll(block, LANES - 32 * g, 1)
-                    wide_ref[g, col * span : (col + 1) * span, :] = block
+                    both.append(block)
+                both = jnp.concatenate(both, axis=1)
+                tiles += [both[c * slots : (c + 1) * slots] for c in range(span // slots)]
+            sorted_rows = []
+            for u in range(rows // SLOTS):
+                group = jnp.concatenate(tiles[u * SLOTS : (u + 1) * SLOTS], axis=0)
+                sorted_rows.append(dot_nn(sort_ref[...], group))
             for slot in range(slots):
-                parts = [wide_ref[2 * f + q, pl.ds(slot, rows, stride=slots), :] for q in range(2)]
+                parts = [
+                    block[slot * SLOTS : (slot + 1) * SLOTS, q * LANES : (q + 1) * LANES]
+                    for q in range(2)
+                    for block in sorted_rows
+                ]
                 low = 4 * rows * (slot // SLOTS) + 2 * f * rows
                 field_ref[slot % SLOTS, low : low + 2 * rows, pl.ds(at, LANES)] = jnp.concatenate(
                     parts, axis=0
@@ -228,15 +249,19 @@
         tiles_up = lower_order >> 7
         lanes_up = lower_order & (LANES - 1)
         lane = lax.broadcasted_iota(jnp.int32, (size, LANES), 1)
+        late = (lower_order <= width).astype(jnp.int32)
+        at = pl.multiple_of(HALF + width * late, width)
+        low = pl.multiple_of(4 * rows * (1 - late), 4 * rows)
+        extra = dot_nn(field_ref[slot, pl.ds(low, 4 * rows)], leg_ref[ring, :, pl.ds(at, width)])
         before = jnp.zeros((size, LANES), jnp.float32)
         for tile in range(DEGREES // width):
             start = tile * width
-            count = 4 * rows if start < HALF else 8 * rows
-            values = dot_nt(field_ref[slot, :count], leg_ref[ring, start : start + width, :])
+            low = 4 * rows * (tile // 3)
+            values = dot_nn(field_ref[slot, low : low + 4 * rows], leg_ref[ring, :, start : start + width])
             if start >= HALF:
-                lower, upper = values[: 4 * rows], values[4 * rows :]
-                row = lax.broadcasted_iota(jnp.int32, lower.shape, 1) + start
-                values = jnp.where(row < boundary, lower, upper)
+                row = lax.broadcasted_iota(jnp.int32, values.shape, 1) + start
+                first, second = (values, extra) if tile == 2 else (extra, values)
+                values = jnp.where(row < boundary, first, second)
             coef_ref[p, :, start : start + width] = values
             for sub in range(width // LANES):
                 moments = moments_of(values[:, sub * LANES : (sub + 1) * LANES], rows)
@@ -251,18 +276,15 @@
                     lane < lanes_up, before, turned
                 )
                 before = turned
-        last_leg = jnp.broadcast_to(
-            leg_ref[ring, DEGREES : DEGREES + 1, :].astype(jnp.float32), (LANES, DEGREES)
-        )
-        last = dot_nt(field_ref[slot, 4 * rows :], last_leg.astype(jnp.bfloat16))
+        last = dot_nn(field_ref[slot, 4 * rows :], turned_edge_ref[...])
         last_ref[p] = last
-        tail_ref[...] += moments_of(last, rows)
+        tail_ref[...] += jnp.where(lane == p, moments_of(last, rows), 0.0)
         return carry
 
     lax.fori_loop(0, 2 * PAIRS, one_pair, 0)
 
     lane = lax.broadcasted_iota(jnp.int32, (size, LANES), 1)
-    after = tail_ref[...]
+    after = jnp.broadcast_to(jnp.sum(tail_ref[...], axis=1, keepdims=True), (size, LANES))
     for tile in reversed(range(8)):
         total = lower_ref[:, tile * LANES : (tile + 1) * LANES]
         if tile >= 4:
@@ -281,15 +303,33 @@
     return pltpu.with_memory_space_constraint(value, pltpu.HBM)
 
 
-def analysis(scalars, arrived, own, other, rows):
-    leg_rows = own.shape[1]
+def turn_kernel(leg_ref, out_ref):
+    out_ref[0] = leg_ref[0].T
+
+
+def turned(legendre):
+    pairs, _, size = legendre.shape
+    width = 256
+    return pl.pallas_call(
+        turn_kernel,
+        grid=(pairs, DEGREES // width),
+        in_specs=[pl.BlockSpec((1, width, size), lambda p, i: (p, i, 0))],
+        out_specs=pl.BlockSpec((1, size, width), lambda p, i: (p, 0, i)),
+        out_shape=pltpu.HBM((pairs, size, DEGREES), legendre.dtype),
+        compiler_params=pltpu.CompilerParams(vmem_limit_bytes=SMALL_LIMIT),
+        cost_estimate=pl.CostEstimate(flops=0, bytes_accessed=4 * legendre.size, transcendentals=0),
+        name="turned",
+    )(in_hbm(legendre))
+
+
+def analysis(scalars, arrived, edges, own, other, rows):
     span = rows * 4
     arrived = arrived.reshape(32, 4, span, LANES)
     whole = pl.BlockSpec(memory_space=pltpu.VMEM)
     far = pl.BlockSpec(memory_space=pltpu.HBM)
     return pl.pallas_call(
         functools.partial(analysis_kernel, rows),
-        in_specs=[pl.BlockSpec(memory_space=pltpu.SMEM), far, far, far],
+        in_specs=[pl.BlockSpec(memory_space=pltpu.SMEM), far, whole, far, far],
         out_specs=[whole, whole, whole],
         out_shape=[
             pltpu.VMEM((2 * PAIRS, 4 * rows, DEGREES), jnp.float32),
@@ -298,8 +338,9 @@
         ],
         scratch_shapes=[
             pltpu.VMEM((32, 4, span, LANES), jnp.bfloat16),
-            pltpu.VMEM((4, leg_rows, DEGREES), jnp.bfloat16),
-            pltpu.VMEM((4, 4 * span, LANES), jnp.float32),
+            pltpu.VMEM((4, DEGREES, DEGREES), jnp.bfloat16),
+            pltpu.VMEM((LANES, LANES), jnp.bfloat16),
+            pltpu.VMEM((DEGREES, LANES), jnp.bfloat16),
             pltpu.VMEM((SLOTS, 8 * rows, DEGREES), jnp.bfloat16),
             pltpu.VMEM((3 * rows, DEGREES + HALF), jnp.float32),
             pltpu.VMEM((3 * rows, HALF), jnp.float32),
@@ -314,7 +355,7 @@
             transcendentals=0,
         ),
         name="analysis",
-    )(scalars, in_hbm(arrived), in_hbm(own), in_hbm(other))
+    )(scalars, in_hbm(arrived), edges, in_hbm(own), in_hbm(other))
 
 
 def factor_kernel(span, parts_ref, out_ref):
@@ -421,7 +462,10 @@
             else:
                 early_ref[:, start : start + LANES] = grad.astype(jnp.bfloat16)
         last_factors = jnp.broadcast_to(2.0 * spread_ref[:, DEGREES - 1 : DEGREES], (size, LANES))
-        last_grad = graded(last_factors, lambda at: last_ref[p, at : at + rows, :])
+        edge_lane = lax.broadcasted_iota(jnp.int32, (4 * rows, LANES), 1)
+        last = jnp.sum(jnp.where(edge_lane == p, last_ref[p], 0.0), axis=1, keepdims=True)
+        last = jnp.broadcast_to(last, (4 * rows, LANES))
+        last_grad = graded(last_factors, lambda at: last[at : at + rows])
         last_grad = last_grad.astype(jnp.bfloat16).astype(jnp.float32)
         last_leg = leg_ref[ring, DEGREES : DEGREES + 1, :].astype(jnp.float32)
 
@@ -444,14 +488,14 @@
                     wide_ref[at // 32 + i, pl.ds(slot, rows, stride=SLOTS), :] = by_position(blocks, i)
         return carry
 
-    lax.fori_loop(0, PAIRS, functools.partial(one_pair, own_ref, 0), 0)
-    lax.fori_loop(0, PAIRS, functools.partial(one_pair, other_ref, PAIRS), 0)
+    lax.fori_loop(0, PAIRS, functools.partial(one_pair, own_ref, 0), 0, unroll=2)
+    lax.fori_loop(0, PAIRS, functools.partial(one_pair, other_ref, PAIRS), 0, unroll=2)
 
     def narrow(j, carry):
         out_ref[j] = wide_ref[j].astype(jnp.bfloat16)
         return carry
 
-    lax.fori_loop(0, 32, narrow, 0)
+    lax.fori_loop(0, 32, narrow, 0, unroll=8)
 
 
 def synthesis(scalars, coeffs, last, factors, own, other, rows):
@@ -500,7 +544,7 @@
         )
     for o, one_hot_ref in enumerate((lower_ref, upper_ref)):
         by_slot = jnp.concatenate([side[o] for side in sides], axis=1)
-        field = dot_nn(by_slot.T.astype(jnp.bfloat16), one_hot_ref[...]).astype(jnp.bfloat16)
+        field = dot_tn(by_slot.astype(jnp.bfloat16), one_hot_ref[...]).astype(jnp.bfloat16)
         for c in range(2):
             for z in range(4):
                 at = c * LANES + z * 32
@@ -552,7 +596,10 @@
     by_group = (channels, 4, 32, DEGREES)
     packed = pack(turn, pair_row, pred_four.reshape(by_group), target_four.reshape(by_group))
     arrived = exchange(packed.reshape(devices, rows * 4, LANES), DEVICES)
-    coeffs, last, moments = analysis(scalars, arrived, legendre, other_legendre, rows)
+    edges = jnp.concatenate([legendre[:, DEGREES], other_legendre[:, DEGREES]]).astype(jnp.float32)
+    coeffs, last, moments = analysis(
+        scalars, arrived, edges, turned(legendre), turned(other_legendre), rows
+    )
     spectra = exchange(moments.reshape(devices // 2, 2 * SLOTS, LANES), SAME_CORE)
     factors = exchange(factors_of(spectra, rows), SAME_CORE).reshape(DEGREES, LANES)
     going = synthesis(scalars, coeffs, last, factors, legendre, other_legendre, rows)

time: 187 us -> 183 us (0.979)
  waiting for transfers between devices: 44.7 us -> 16.9 us
  Pallas kernels: 36.1 us -> 57.4 us
    all_to_all x1, waiting for transfers between devices: 44.7 us -> 16.9 us  [exchange(): return lax.all_to_all(values, axes, split_axis=0, concat_axis=0, tiled=True)]
    pallas_call x0 -> x2, Pallas kernels: none -> 26.4 us  [turned(): pl.pallas_call(turn_kernel, grid=(pairs, DEGREES // width), in_specs=[pl....]
    pallas_call x1, Pallas kernels: 16.8 us -> 12.7 us  [analysis(): pl.pallas_call(functools.partial(analysis_kernel, rows), in_specs=[pl.Blo...]
  transfers between devices with their start and end apart: 2 -> 2, of which waited for: 1 -> 1; matrix products, arithmetic and copies ran while one was open for 10% -> 11% of each run, Pallas kernels for 4% -> 18%
where the time goes in v5:
time: 183 us; the launch traced here: 182 us
  blocking collectives  74.8 us (41%)
  Pallas kernels  57.4 us (31%)
  local copies, waits for them, and re-layouts  20.5 us (11%)
  waiting for transfers between devices  16.9 us (9%)
  starting transfers between devices  12 us (7%)
    all_to_all x3, blocking collectives, exchange(): return lax.all_to_all(values, axes, split_axis=0, concat_axis=0, tiled=True)  74.8 us
    pallas_call x2, Pallas kernels, turned(): pl.pallas_call(turn_kernel, grid=(pairs, DEGREES // width), in_specs=[pl....  26.4 us
    all_to_all x1, waiting for transfers between devices, exchange(): return lax.all_to_all(values, axes, split_axis=0, concat_axis=0, tiled=True)  16.9 us
    pallas_call x1, Pallas kernels, analysis(): pl.pallas_call(functools.partial(analysis_kernel, rows), in_specs=[pl.Blo...  12.7 us
    all_to_all x1, starting transfers between devices, exchange(): return lax.all_to_all(values, axes, split_axis=0, concat_axis=0, tiled=True)  10.6 us
    unnamed x15, local copies, waits for them, and re-layouts  9.55 us
    ppermute x1, local copies, waits for them, and re-layouts, per_device(): other_legendre = lax.ppermute(legendre, 'core', [(0, 1), (1, 0)])  9.5 us
    pallas_call x1, Pallas kernels, synthesis(): pl.pallas_call(functools.partial(synthesis_kernel, rows), in_specs=[pl.Bl...  6.59 us
  transfers between devices with their start and end apart: 2, of which 1 were waited for; matrix products, arithmetic and copies ran while one was open for 11% of the time, Pallas kernels for 18%

profile of v5, /device:TPU:1, one launch (start us, length us, event | category | flops | bytes accessed | tf_op | source)
XLA Modules:
  0.0 181.9 jit_solution(4554690246005157181)
XLA Ops:
  0.0 1.4 collective-permute-start
  1.4 6.5 %pack.1 = bf16[16,2,4,10,16,128]{5,4,3,2,1,0:T(8,128)(2,1)} custom-call(s32[1]{0:T(128)} %bitcast.turn_ref, s32[1,512]{1,0:T(1,128)} %bitcast.24, bf16[10,4,32,1024]{3,2,1,0:T(8,128)(2,1)} %bitcast.27, bf16[10,4,32,1024]{3,2,1,0:T(8,128)(2,1)} %bitcast.28), custom_call_target="tpu_custom_call" | custom-call | flops 2684354560 | bytes 10485760 | tf_op jit(solution)/shard_map/pack/pallas_call | solution.py:122
  8.0 10.6 %all-to-all-start = ((bf16[128,160,128]{2,1,0:T(8,128)(2,1)}), bf16[128,160,128]{2,1,0:T(8,128)(2,1)}, u32[]{:S(2)}, u32[]{:S(2)}) async-start(bf16[128,160,128]{2,1,0:T(8,128)(2,1)} %bitcast.26), calls=%async_computation | async-start | bytes 10485760 | tf_op jit(solution)/shard_map/all_to_all | solution.py:580
  18.6 9.5 %copy.11.leg_ref.own_ref = bf16[4,1025,1024]{2,1,0:T(8,128)(2,1)} copy(bf16[4,1025,1024]{2,0,1:T(4,128)(2,1)} %param.6) | data formatting | bytes 16793600 | tf_op args[2]
  28.1 0.0 copy-start
  28.1 13.2 %turned.2.own_hbm = bf16[4,1024,1024]{2,1,0:T(8,128)(2,1)} custom-call(bf16[4,1025,1024]{2,1,0:T(8,128)(2,1)} %copy.11.leg_ref.own_ref), custom_call_target="tpu_custom_call" | custom-call | bytes 16793600 | tf_op jit(solution)/shard_map/turned/pallas_call | solution.py:313
  41.3 0.0 copy-done
  41.3 0.1 fusion
  41.4 0.1 pad_add_fusion.scalar_ref
  41.5 0.7 slice_bitcast_fusion.1
  42.2 0.0 collective-permute-done
  42.2 9.5 %copy.12.leg_ref.other_ref = bf16[4,1025,1024]{2,1,0:T(8,128)(2,1)} copy(bf16[4,1025,1024]{2,0,1:T(4,128)(2,1)} %collective-permute-done) | data formatting | bytes 16793600 | tf_op jit(solution)/shard_map/ppermute | solution.py:591
  51.7 13.2 %turned.3.other_hbm = bf16[4,1024,1024]{2,1,0:T(8,128)(2,1)} custom-call(bf16[4,1025,1024]{2,1,0:T(8,128)(2,1)} %copy.12.leg_ref.other_ref), custom_call_target="tpu_custom_call" | custom-call | bytes 16793600 | tf_op jit(solution)/shard_map/turned/pallas_call | solution.py:313
  64.9 0.7 slice_bitcast_fusion
  65.6 16.9 %all-to-all-done = bf16[128,160,128]{2,1,0:T(8,128)(2,1)} async-done(((bf16[128,160,128]{2,1,0:T(8,128)(2,1)}), bf16[128,160,128]{2,1,0:T(8,128)(2,1)}, u32[]{:S(2)}, u32[]{:S(2)}) %all-to-all-start) | async-done | bytes 5242912 | tf_op jit(solution)/shard_map/all_to_all | solution.py:580
  82.5 0.0 slice-start
  82.5 0.0 slice-start.3
  82.5 0.0 slice-start.4
  82.5 0.0 slice-start.5
  82.6 12.7 %analysis.1 = (f32[8,160,1024]{2,1,0:T(8,128)S(1)}, f32[8,160,128]{2,1,0:T(8,128)S(1)}, f32[1024,128]{1,0:T(8,128)S(1)}) custom-call(s32[9]{0:T(128)S(1)} %pad_add_fusion.scalar_ref, bf16[32,4,160,128]{3,2,1,0:T(8,128)(2,1)} %bitcast.6.arrived_ref, f32[8,1024]{1,0:T(8,128)S(1)} %maximum_convert_fusion.edge_ref, bf16[4,1024,1024]{2,1,0:T(8,128)(2,1)} %turned.2.own_hbm, ...), custom_call_target="tpu_custom_call" | custom-call | flops 3355443200 | bytes 24641536 | tf_op jit(solution)/shard_map/analysis/pallas_call | solution.py:330
  95.2 16.7 %all_to_all.20.parts_ref = f32[64,16,128]{2,1,0:T(8,128)S(1)} all-to-all(f32[64,16,128]{2,1,0:T(8,128)S(1)} %bitcast.23), channel_id=1, replica_groups=mesh['zx'=16,'core'=2,'col'=4] {'zx','col'}, dimensions={0} | all-to-all | bytes 1048576 | tf_op jit(solution)/shard_map/all_to_all | solution.py:580
  111.9 0.2 factors.1
  112.1 15.3 %all_to_all.21 = f32[64,16,128]{2,1,0:T(8,128)S(1)} all-to-all(f32[64,16,128]{2,1,0:T(8,128)S(1)} %factors.1), channel_id=1, replica_groups=mesh['zx'=16,'core'=2,'col'=4] {'zx','col'}, dimensions={0} | all-to-all | bytes 1048576 | tf_op jit(solution)/shard_map/all_to_all | solution.py:580
  127.4 0.0 slice-done
  127.4 0.0 slice-done.3
  127.4 0.0 slice-done.1
  127.4 0.0 slice-done.2
  127.4 0.0 slice-done.4
  127.5 0.0 slice-done.5
  127.5 6.6 %synthesis.1 = bf16[32,320,128]{2,1,0:T(8,128)(2,1)S(1)} custom-call(s32[9]{0:T(128)S(1)} %pad_add_fusion.scalar_ref, f32[8,160,1024]{2,1,0:T(8,128)S(1)} %get-tuple-element.8.coef_ref, f32[8,160,128]{2,1,0:T(8,128)S(1)} %get-tuple-element.9.last_ref, f32[1024,128]{1,0:T(8,128)S(1)} %bitcast.22, bf16[4,1025,1024]{2,1,0:T(8,128)(2,1)S(1)} %bitcast.17, ...), custom_call_target="tpu_custom_call" | custom-call | flops 2013265920 | bytes 22036480 | tf_op jit(solution)/shard_map/synthesis/pallas_call | solution.py:503
  134.1 42.9 %all_to_all.22 = bf16[128,80,128]{2,1,0:T(8,128)(2,1)S(1)} all-to-all(bf16[128,80,128]{2,1,0:T(8,128)(2,1)S(1)} %bitcast.21), channel_id=1, replica_groups=mesh['zx'=16,'core'=2,'col'=4] {'zx','core','col'}, dimensions={0} | all-to-all | bytes 5242880 | tf_op jit(solution)/shard_map/all_to_all | solution.py:580
  176.9 5.0 %unpack.1 = bf16[10,4,32,1024]{3,2,1,0:T(8,128)(2,1)} custom-call(s32[1]{0:T(128)} %bitcast.turn_ref, s32[1,512]{1,0:T(1,128)S(1)} %bitcast.25, bf16[16,2,4,80,128]{4,3,2,1,0:T(8,128)(2,1)S(1)} %bitcast.20), custom_call_target="tpu_custom_call" | custom-call | flops 1342177280 | bytes 5242880 | tf_op jit(solution)/shard_map/unpack/pallas_call | solution.py:565
  (5 shorter events, 0.0 us)
Async XLA Ops:
  0.0 42.2 %collective-permute-start = (bf16[4,1025,1024]{2,0,1:T(4,128)(2,1)}, bf16[4,1025,1024]{2,0,1:T(4,128)(2,1)}, u32[]{:S(2)}, u32[]{:S(2)}) collective-permute-start(bf16[4,1025,1024]{2,0,1:T(4,128)(2,1)} %param.6), channel_id=1, source_target_pairs={{0,4},{4,0},{1,5},{5,1},{2,6},{6,2},{3,7},{7,3},{8,12},{12,8},{9,1... | collective-permute-start | bytes 25190408 | tf_op jit(solution)/shard_map/ppermute | solution.py:591
  8.0 74.6 %all-to-all-start = ((bf16[128,160,128]{2,1,0:T(8,128)(2,1)}), bf16[128,160,128]{2,1,0:T(8,128)(2,1)}, u32[]{:S(2)}, u32[]{:S(2)}) async-start(bf16[128,160,128]{2,1,0:T(8,128)(2,1)} %bitcast.26), calls=%async_computation | async-start | bytes 10485760 | tf_op jit(solution)/shard_map/all_to_all | solution.py:580
  28.1 13.2 %copy-start = (s32[512]{0:T(512)S(1)}, s32[512]{0:T(512)}, u32[]{:S(2)}) copy-start(s32[512]{0:T(512)} %param.7) | copy-start | bytes 6148
  82.5 44.9 %slice-start = ((s8[8454144]{0:T(1024)(128)(4,1)}), s8[4194304]{0:T(1024)(128)(4,1)S(1)}, s32[]{:S(2)}) async-start(s8[8454144]{0:T(1024)(128)(4,1)} %bitcast.16), calls=%async_computation.4 | async-start | bytes 8388608
  82.5 44.9 %slice-start.3 = ((s8[8454144]{0:T(1024)(128)(4,1)}), s8[4194304]{0:T(1024)(128)(4,1)S(1)}, s32[]{:S(2)}) async-start(s8[8454144]{0:T(1024)(128)(4,1)} %bitcast.18), calls=%async_computation.7 | async-start | bytes 8388608
  82.5 44.9 %slice-start.1 = ((s8[8454144]{0:T(1024)(128)(4,1)}), s8[4194304]{0:T(1024)(128)(4,1)S(1)}, s32[]{:S(2)}) async-start(s8[8454144]{0:T(1024)(128)(4,1)} %bitcast.16), calls=%async_computation.5 | async-start | bytes 8388608
  82.5 44.9 %slice-start.2 = ((s8[8454144]{0:T(1024)(128)(4,1)}), s8[65536]{0:T(1024)(128)(4,1)S(1)}, s32[]{:S(2)}) async-start(s8[8454144]{0:T(1024)(128)(4,1)} %bitcast.16), calls=%async_computation.6 | async-start | bytes 131072
  82.5 44.9 %slice-start.4 = ((s8[8454144]{0:T(1024)(128)(4,1)}), s8[4194304]{0:T(1024)(128)(4,1)S(1)}, s32[]{:S(2)}) async-start(s8[8454144]{0:T(1024)(128)(4,1)} %bitcast.18), calls=%async_computation.8 | async-start | bytes 8388608
  82.5 44.9 %slice-start.5 = ((s8[8454144]{0:T(1024)(128)(4,1)}), s8[65536]{0:T(1024)(128)(4,1)S(1)}, s32[]{:S(2)}) async-start(s8[8454144]{0:T(1024)(128)(4,1)} %bitcast.18), calls=%async_computation.9 | async-start | bytes 131072

commit v6 on v5

--- a/solution.py
+++ b/solution.py
@@ -110,7 +110,7 @@
         send(i).start()
         return carry
 
-    lax.fori_loop(0, steps, step, 0)
+    lax.fori_loop(0, steps, step, 0, unroll=True)
     for i in range(steps):
         send(i).wait()
 
@@ -488,8 +488,8 @@
                     wide_ref[at // 32 + i, pl.ds(slot, rows, stride=SLOTS), :] = by_position(blocks, i)
         return carry
 
-    lax.fori_loop(0, PAIRS, functools.partial(one_pair, own_ref, 0), 0, unroll=2)
-    lax.fori_loop(0, PAIRS, functools.partial(one_pair, other_ref, PAIRS), 0, unroll=2)
+    lax.fori_loop(0, PAIRS, functools.partial(one_pair, own_ref, 0), 0, unroll=4)
+    lax.fori_loop(0, PAIRS, functools.partial(one_pair, other_ref, PAIRS), 0, unroll=4)
 
     def narrow(j, carry):
         out_ref[j] = wide_ref[j].astype(jnp.bfloat16)
@@ -522,58 +522,67 @@
     )(scalars, *(in_vmem(value) for value in (coeffs, last, factors, own, other)))
 
 
-def unpack_kernel(turn_ref, pairs_ref, returned_ref, out_ref, lower_ref, upper_ref):
-    @pl.when(pl.program_id(0) == 0)
-    def _():
-        one_hots(pairs_ref, lower_ref, upper_ref)
-
+def unpack_kernel(
+    channels, turn_ref, pairs_ref, returned_ref, out_hbm, out_ref, lower_ref, upper_ref, sems
+):
+    one_hots(pairs_ref, lower_ref, upper_ref)
     turn = turn_ref[0]
-    both = returned_ref[...].astype(jnp.float32)
-    sides = []
-    for c in range(2):
-        first, second = (
-            both[:, sample, :, c * SLOTS : (c + 1) * SLOTS].reshape(HALF, LANES) for sample in range(2)
-        )
-        group = lax.broadcasted_iota(jnp.int32, first.shape, 1) >> 5
-        keep = ((group - turn) & 3) < 2
-        sides.append(
-            (
-                jnp.where(keep, first, pltpu.roll(second, 64, 1)),
-                jnp.where(keep, pltpu.roll(first, 64, 1), second),
+
+    def send(i):
+        at = pl.ds(2 * i, 2)
+        return pltpu.make_async_copy(out_ref.at[at], out_hbm.at[at], sems.at[i])
+
+    steps = channels // 2
+    for i in range(steps):
+        sides = []
+        for c in range(2 * i, 2 * i + 2):
+            first, second = (
+                returned_ref[:, sample, :, (c // 2) * 16 : (c // 2) * 16 + 16]
+                .astype(jnp.float32)[:, :, (c % 2) * SLOTS : (c % 2 + 1) * SLOTS]
+                .reshape(HALF, LANES)
+                for sample in range(2)
             )
-        )
-    for o, one_hot_ref in enumerate((lower_ref, upper_ref)):
-        by_slot = jnp.concatenate([side[o] for side in sides], axis=1)
-        field = dot_tn(by_slot.astype(jnp.bfloat16), one_hot_ref[...]).astype(jnp.bfloat16)
-        for c in range(2):
-            for z in range(4):
-                at = c * LANES + z * 32
-                out_ref[c, (z - turn) & 3, :, o * HALF : (o + 1) * HALF] = field[at : at + 32]
+            group = lax.broadcasted_iota(jnp.int32, first.shape, 1) >> 5
+            keep = ((group - turn) & 3) < 2
+            sides.append(
+                (
+                    jnp.where(keep, first, pltpu.roll(second, 64, 1)),
+                    jnp.where(keep, pltpu.roll(first, 64, 1), second),
+                )
+            )
+        for o, one_hot_ref in enumerate((lower_ref, upper_ref)):
+            by_slot = jnp.concatenate([side[o] for side in sides], axis=1)
+            field = dot_tn(by_slot.astype(jnp.bfloat16), one_hot_ref[...]).astype(jnp.bfloat16)
+            for c in range(2):
+                for z in range(4):
+                    at = c * LANES + z * 32
+                    out_ref[2 * i + c, (z - turn) & 3, :, o * HALF : (o + 1) * HALF] = field[at : at + 32]
+        send(i).start()
+    for i in range(steps):
+        send(i).wait()
 
 
 def unpack(turn, pairs, returned, channels):
-    grid_spec = pltpu.PrefetchScalarGridSpec(
-        num_scalar_prefetch=1,
-        grid=(channels // 2,),
-        in_specs=[
-            pl.BlockSpec((1, HALF), lambda i, t: (0, 0)),
-            pl.BlockSpec((16, 2, 4, 16, LANES), lambda i, t: (0, 0, 0, i, 0)),
+    whole = pl.BlockSpec(memory_space=pltpu.VMEM)
+    return pl.pallas_call(
+        functools.partial(unpack_kernel, channels),
+        in_specs=[pl.BlockSpec(memory_space=pltpu.SMEM), whole, whole],
+        out_specs=pl.BlockSpec(memory_space=pltpu.HBM),
+        out_shape=pltpu.HBM((channels, 4, 32, DEGREES), jnp.bfloat16),
+        scratch_shapes=[
+            pltpu.VMEM((channels, 4, 32, DEGREES), jnp.bfloat16),
+            pltpu.VMEM((HALF, HALF), jnp.bfloat16),
+            pltpu.VMEM((HALF, HALF), jnp.bfloat16),
+            pltpu.SemaphoreType.DMA((channels // 2,)),
         ],
-        out_specs=pl.BlockSpec((2, 4, 32, DEGREES), lambda i, t: (i, 0, 0, 0)),
-        scratch_shapes=[pltpu.VMEM((HALF, HALF), jnp.bfloat16)] * 2,
-    )
-    return pl.pallas_call(
-        unpack_kernel,
-        grid_spec=grid_spec,
-        out_shape=jax.ShapeDtypeStruct((channels, 4, 32, DEGREES), jnp.bfloat16),
-        compiler_params=pltpu.CompilerParams(vmem_limit_bytes=SMALL_LIMIT),
+        compiler_params=pltpu.CompilerParams(vmem_limit_bytes=KERNEL_LIMIT),
         cost_estimate=pl.CostEstimate(
             flops=DEGREES * DEGREES * LANES * channels,
             bytes_accessed=4 * LANES * DEGREES * channels,
             transcendentals=0,
         ),
         name="unpack",
-    )(turn, pairs, returned)
+    )(turn, pairs, in_vmem(returned))
 
 
 def exchange(values, axes):

time: 183 us -> 181 us (0.989)
  no operation moved by 1% of the time
where the time goes in v6:
time: 181 us; the launch traced here: 180 us
  blocking collectives  74.8 us (41%)
  Pallas kernels  55.6 us (31%)
  local copies, waits for them, and re-layouts  20.5 us (11%)
  waiting for transfers between devices  16.9 us (9%)
  starting transfers between devices  12 us (7%)
    all_to_all x3, blocking collectives, exchange(): return lax.all_to_all(values, axes, split_axis=0, concat_axis=0, tiled=True)  74.8 us
    pallas_call x2, Pallas kernels, turned(): pl.pallas_call(turn_kernel, grid=(pairs, DEGREES // width), in_specs=[pl....  26.4 us
    all_to_all x1, waiting for transfers between devices, exchange(): return lax.all_to_all(values, axes, split_axis=0, concat_axis=0, tiled=True)  16.9 us
    pallas_call x1, Pallas kernels, analysis(): pl.pallas_call(functools.partial(analysis_kernel, rows), in_specs=[pl.Blo...  12.7 us
    all_to_all x1, starting transfers between devices, exchange(): return lax.all_to_all(values, axes, split_axis=0, concat_axis=0, tiled=True)  10.6 us
    unnamed x15, local copies, waits for them, and re-layouts  9.55 us
    ppermute x1, local copies, waits for them, and re-layouts, per_device(): other_legendre = lax.ppermute(legendre, 'core', [(0, 1), (1, 0)])  9.5 us
    pallas_call x1, Pallas kernels, pack(): pl.pallas_call(functools.partial(pack_kernel, channels), in_specs=[pl.Blo...  6.39 us
  transfers between devices with their start and end apart: 2, of which 1 were waited for; matrix products, arithmetic and copies ran while one was open for 11% of the time, Pallas kernels for 18%

profile of v6, /device:TPU:1, one launch (start us, length us, event | category | flops | bytes accessed | tf_op | source)
XLA Modules:
  0.0 180.3 jit_solution(16165218103343752487)
XLA Ops:
  0.0 1.4 collective-permute-start
  1.4 6.4 %pack.1 = bf16[16,2,4,10,16,128]{5,4,3,2,1,0:T(8,128)(2,1)} custom-call(s32[1]{0:T(128)} %bitcast.turn_ref, s32[1,512]{1,0:T(1,128)} %bitcast.24, bf16[10,4,32,1024]{3,2,1,0:T(8,128)(2,1)} %bitcast.27, bf16[10,4,32,1024]{3,2,1,0:T(8,128)(2,1)} %bitcast.28), custom_call_target="tpu_custom_call" | custom-call | flops 2684354560 | bytes 10485760 | tf_op jit(solution)/shard_map/pack/pallas_call | solution.py:122
  7.8 10.6 %all-to-all-start = ((bf16[128,160,128]{2,1,0:T(8,128)(2,1)}), bf16[128,160,128]{2,1,0:T(8,128)(2,1)}, u32[]{:S(2)}, u32[]{:S(2)}) async-start(bf16[128,160,128]{2,1,0:T(8,128)(2,1)} %bitcast.26), calls=%async_computation | async-start | bytes 10485760 | tf_op jit(solution)/shard_map/all_to_all | solution.py:589
  18.5 9.5 %copy.11.leg_ref.own_ref = bf16[4,1025,1024]{2,1,0:T(8,128)(2,1)} copy(bf16[4,1025,1024]{2,0,1:T(4,128)(2,1)} %param.6) | data formatting | bytes 16793600 | tf_op args[2]
  28.0 0.0 copy-start
  28.0 13.2 %turned.2.own_hbm = bf16[4,1024,1024]{2,1,0:T(8,128)(2,1)} custom-call(bf16[4,1025,1024]{2,1,0:T(8,128)(2,1)} %copy.11.leg_ref.own_ref), custom_call_target="tpu_custom_call" | custom-call | bytes 16793600 | tf_op jit(solution)/shard_map/turned/pallas_call | solution.py:313
  41.2 0.0 copy-done
  41.2 0.1 fusion
  41.2 0.1 pad_add_fusion.scalar_ref
  41.3 0.7 slice_bitcast_fusion.1
  42.0 0.0 collective-permute-done
  42.0 9.5 %copy.12.leg_ref.other_ref = bf16[4,1025,1024]{2,1,0:T(8,128)(2,1)} copy(bf16[4,1025,1024]{2,0,1:T(4,128)(2,1)} %collective-permute-done) | data formatting | bytes 16793600 | tf_op jit(solution)/shard_map/ppermute | solution.py:600
  51.5 13.2 %turned.3.other_hbm = bf16[4,1024,1024]{2,1,0:T(8,128)(2,1)} custom-call(bf16[4,1025,1024]{2,1,0:T(8,128)(2,1)} %copy.12.leg_ref.other_ref), custom_call_target="tpu_custom_call" | custom-call | bytes 16793600 | tf_op jit(solution)/shard_map/turned/pallas_call | solution.py:313
  64.7 0.7 slice_bitcast_fusion
  65.4 16.9 %all-to-all-done = bf16[128,160,128]{2,1,0:T(8,128)(2,1)} async-done(((bf16[128,160,128]{2,1,0:T(8,128)(2,1)}), bf16[128,160,128]{2,1,0:T(8,128)(2,1)}, u32[]{:S(2)}, u32[]{:S(2)}) %all-to-all-start) | async-done | bytes 5242912 | tf_op jit(solution)/shard_map/all_to_all | solution.py:589
  82.4 0.0 slice-start
  82.4 0.0 slice-start.3
  82.4 0.0 slice-start.4
  82.4 0.0 slice-start.5
  82.4 12.7 %analysis.1 = (f32[8,160,1024]{2,1,0:T(8,128)S(1)}, f32[8,160,128]{2,1,0:T(8,128)S(1)}, f32[1024,128]{1,0:T(8,128)S(1)}) custom-call(s32[9]{0:T(128)S(1)} %pad_add_fusion.scalar_ref, bf16[32,4,160,128]{3,2,1,0:T(8,128)(2,1)} %bitcast.6.arrived_ref, f32[8,1024]{1,0:T(8,128)S(1)} %maximum_convert_fusion.edge_ref, bf16[4,1024,1024]{2,1,0:T(8,128)(2,1)} %turned.2.own_hbm, ...), custom_call_target="tpu_custom_call" | custom-call | flops 3355443200 | bytes 24641536 | tf_op jit(solution)/shard_map/analysis/pallas_call | solution.py:330
  95.1 16.7 %all_to_all.20.parts_ref = f32[64,16,128]{2,1,0:T(8,128)S(1)} all-to-all(f32[64,16,128]{2,1,0:T(8,128)S(1)} %bitcast.23), channel_id=1, replica_groups=mesh['zx'=16,'core'=2,'col'=4] {'zx','col'}, dimensions={0} | all-to-all | bytes 1048576 | tf_op jit(solution)/shard_map/all_to_all | solution.py:589
  111.9 0.2 factors.1
  112.1 15.2 %all_to_all.21 = f32[64,16,128]{2,1,0:T(8,128)S(1)} all-to-all(f32[64,16,128]{2,1,0:T(8,128)S(1)} %factors.1), channel_id=1, replica_groups=mesh['zx'=16,'core'=2,'col'=4] {'zx','col'}, dimensions={0} | all-to-all | bytes 1048576 | tf_op jit(solution)/shard_map/all_to_all | solution.py:589
  127.4 0.0 slice-done
  127.4 0.0 slice-done.3
  127.4 0.0 slice-done.1
  127.4 0.0 slice-done.2
  127.4 0.0 slice-done.4
  127.4 0.0 slice-done.5
  127.4 6.1 %synthesis.1 = bf16[32,320,128]{2,1,0:T(8,128)(2,1)S(1)} custom-call(s32[9]{0:T(128)S(1)} %pad_add_fusion.scalar_ref, f32[8,160,1024]{2,1,0:T(8,128)S(1)} %get-tuple-element.8.coef_ref, f32[8,160,128]{2,1,0:T(8,128)S(1)} %get-tuple-element.9.last_ref, f32[1024,128]{1,0:T(8,128)S(1)} %bitcast.22, bf16[4,1025,1024]{2,1,0:T(8,128)(2,1)S(1)} %bitcast.17, ...), custom_call_target="tpu_custom_call" | custom-call | flops 2013265920 | bytes 22036480 | tf_op jit(solution)/shard_map/synthesis/pallas_call | solution.py:503
  133.6 42.9 %all_to_all.22 = bf16[128,80,128]{2,1,0:T(8,128)(2,1)S(1)} all-to-all(bf16[128,80,128]{2,1,0:T(8,128)(2,1)S(1)} %bitcast.21), channel_id=1, replica_groups=mesh['zx'=16,'core'=2,'col'=4] {'zx','core','col'}, dimensions={0} | all-to-all | bytes 5242880 | tf_op jit(solution)/shard_map/all_to_all | solution.py:589
  176.4 3.7 %unpack.1 = bf16[10,4,32,1024]{3,2,1,0:T(8,128)(2,1)} custom-call(s32[1]{0:T(128)} %bitcast.turn_ref, s32[1,512]{1,0:T(1,128)S(1)} %bitcast.25, bf16[16,2,4,80,128]{4,3,2,1,0:T(8,128)(2,1)S(1)} %bitcast.20), custom_call_target="tpu_custom_call" | custom-call | flops 1342177280 | bytes 5242880 | tf_op jit(solution)/shard_map/unpack/pallas_call | solution.py:567
  (5 shorter events, 0.0 us)
Async XLA Ops:
  0.0 42.0 %collective-permute-start = (bf16[4,1025,1024]{2,0,1:T(4,128)(2,1)}, bf16[4,1025,1024]{2,0,1:T(4,128)(2,1)}, u32[]{:S(2)}, u32[]{:S(2)}) collective-permute-start(bf16[4,1025,1024]{2,0,1:T(4,128)(2,1)} %param.6), channel_id=1, source_target_pairs={{0,4},{4,0},{1,5},{5,1},{2,6},{6,2},{3,7},{7,3},{8,12},{12,8},{9,1... | collective-permute-start | bytes 25190408 | tf_op jit(solution)/shard_map/ppermute | solution.py:600
  7.8 74.6 %all-to-all-start = ((bf16[128,160,128]{2,1,0:T(8,128)(2,1)}), bf16[128,160,128]{2,1,0:T(8,128)(2,1)}, u32[]{:S(2)}, u32[]{:S(2)}) async-start(bf16[128,160,128]{2,1,0:T(8,128)(2,1)} %bitcast.26), calls=%async_computation | async-start | bytes 10485760 | tf_op jit(solution)/shard_map/all_to_all | solution.py:589
  28.0 13.2 %copy-start = (s32[512]{0:T(512)S(1)}, s32[512]{0:T(512)}, u32[]{:S(2)}) copy-start(s32[512]{0:T(512)} %param.7) | copy-start | bytes 6148
  82.4 45.0 %slice-start = ((s8[8454144]{0:T(1024)(128)(4,1)}), s8[4194304]{0:T(1024)(128)(4,1)S(1)}, s32[]{:S(2)}) async-start(s8[8454144]{0:T(1024)(128)(4,1)} %bitcast.16), calls=%async_computation.4 | async-start | bytes 8388608
  82.4 45.0 %slice-start.3 = ((s8[8454144]{0:T(1024)(128)(4,1)}), s8[4194304]{0:T(1024)(128)(4,1)S(1)}, s32[]{:S(2)}) async-start(s8[8454144]{0:T(1024)(128)(4,1)} %bitcast.18), calls=%async_computation.7 | async-start | bytes 8388608
  82.4 45.0 %slice-start.1 = ((s8[8454144]{0:T(1024)(128)(4,1)}), s8[4194304]{0:T(1024)(128)(4,1)S(1)}, s32[]{:S(2)}) async-start(s8[8454144]{0:T(1024)(128)(4,1)} %bitcast.16), calls=%async_computation.5 | async-start | bytes 8388608
  82.4 45.0 %slice-start.2 = ((s8[8454144]{0:T(1024)(128)(4,1)}), s8[65536]{0:T(1024)(128)(4,1)S(1)}, s32[]{:S(2)}) async-start(s8[8454144]{0:T(1024)(128)(4,1)} %bitcast.16), calls=%async_computation.6 | async-start | bytes 131072
  82.4 45.0 %slice-start.4 = ((s8[8454144]{0:T(1024)(128)(4,1)}), s8[4194304]{0:T(1024)(128)(4,1)S(1)}, s32[]{:S(2)}) async-start(s8[8454144]{0:T(1024)(128)(4,1)} %bitcast.18), calls=%async_computation.8 | async-start | bytes 8388608
  82.4 45.0 %slice-start.5 = ((s8[8454144]{0:T(1024)(128)(4,1)}), s8[65536]{0:T(1024)(128)(4,1)S(1)}, s32[]{:S(2)}) async-start(s8[8454144]{0:T(1024)(128)(4,1)} %bitcast.18), calls=%async_computation.9 | async-start | bytes 131072

commit v7 on v6

--- a/solution.py
+++ b/solution.py
@@ -17,6 +17,7 @@
 DEVICES = ("zx", "core", "col")
 SAME_CORE = ("zx", "col")
 KERNEL_LIMIT = 36 * 1024 * 1024
+MIDDLE_LIMIT = 26 * 1024 * 1024
 SMALL_LIMIT = 16 * 1024 * 1024
 TINY_LIMIT = 4 * 1024 * 1024
 
@@ -292,7 +293,9 @@
             total = total + 2.0 * jnp.where(lane == LANES - 1, after, turned)
             after = turned
         total = jnp.concatenate([total, jnp.zeros((LANES - size, LANES), jnp.float32)], axis=0)
-        moment_ref[tile * LANES : (tile + 1) * LANES, :] = total.T
+        by_degree = total.T
+        for h in range(2):
+            moment_ref[pl.ds(2 * tile + h, 64, stride=16), :] = by_degree[64 * h : 64 * (h + 1)]
 
 
 def in_vmem(value):
@@ -383,7 +386,11 @@
     dcross = -2.0 * upper_mean * inverse
     lane = lax.broadcasted_iota(jnp.int32, total.shape, 1)
     factors = jnp.where(lane < span, dpower, pltpu.roll(dcross, span, 1))
-    out_ref[...] = jnp.broadcast_to(factors[None], out_ref.shape)
+    by_half = [
+        jnp.concatenate([factors[2 * k + h : 2 * k + h + 1, : 2 * span] for k in range(8)], axis=1)
+        for h in range(2)
+    ]
+    out_ref[...] = jnp.broadcast_to(jnp.concatenate(by_half, axis=0)[None], out_ref.shape)
 
 
 def factors_of(parts, rows):
@@ -392,7 +399,7 @@
         functools.partial(factor_kernel, rows),
         in_specs=[whole],
         out_specs=whole,
-        out_shape=pltpu.VMEM(parts.shape, jnp.float32),
+        out_shape=pltpu.VMEM((parts.shape[0], 2, 16 * rows), jnp.float32),
         compiler_params=pltpu.CompilerParams(vmem_limit_bytes=TINY_LIMIT),
         cost_estimate=pl.CostEstimate(flops=parts.size, bytes_accessed=8 * parts.size, transcendentals=0),
         name="factors",
@@ -400,14 +407,21 @@
 
 
 def synthesis_kernel(
-    rows, scalar_ref, coef_ref, last_ref, factor_ref, own_ref, other_ref, out_ref,
-    spread_ref, upspread_ref, early_ref, late_ref, wide_ref,
+    rows, scalar_ref, coef_ref, last_ref, factor_ref, own_hbm, other_ref, out_ref,
+    own_ref, spread_ref, upspread_ref, early_ref, late_ref, wide_ref, sems,
 ):
     size = 2 * rows
     lane = lax.broadcasted_iota(jnp.int32, (size, LANES), 1)
+    def own_copy(p):
+        return pltpu.make_async_copy(own_hbm.at[p], own_ref.at[p], sems.at[p])
+
+    for p in range(PAIRS):
+        own_copy(p).start()
+
     before = None
+    by_degree = jnp.concatenate([factor_ref[:, h, :] for h in range(2)], axis=0).T
     for tile in range(8):
-        turned = factor_ref[tile * LANES : (tile + 1) * LANES, :].T[:size]
+        turned = by_degree[tile * size : (tile + 1) * size]
         spread_ref[:, tile * LANES : (tile + 1) * LANES] = turned
         shifted = pltpu.roll(turned, 1, 1)
         if tile >= 4:
@@ -488,8 +502,12 @@
                     wide_ref[at // 32 + i, pl.ds(slot, rows, stride=SLOTS), :] = by_position(blocks, i)
         return carry
 
-    lax.fori_loop(0, PAIRS, functools.partial(one_pair, own_ref, 0), 0, unroll=4)
+    def own_pair(p, carry):
+        own_copy(p).wait()
+        return one_pair(own_ref, 0, p, carry)
+
     lax.fori_loop(0, PAIRS, functools.partial(one_pair, other_ref, PAIRS), 0, unroll=4)
+    lax.fori_loop(0, PAIRS, own_pair, 0, unroll=4)
 
     def narrow(j, carry):
         out_ref[j] = wide_ref[j].astype(jnp.bfloat16)
@@ -502,24 +520,28 @@
     whole = pl.BlockSpec(memory_space=pltpu.VMEM)
     return pl.pallas_call(
         functools.partial(synthesis_kernel, rows),
-        in_specs=[pl.BlockSpec(memory_space=pltpu.SMEM)] + [whole] * 5,
+        in_specs=[pl.BlockSpec(memory_space=pltpu.SMEM)]
+        + [whole] * 3
+        + [pl.BlockSpec(memory_space=pltpu.HBM), whole],
         out_specs=whole,
         out_shape=pltpu.VMEM((32, rows * SLOTS, LANES), jnp.bfloat16),
         scratch_shapes=[
+            pltpu.VMEM(own.shape, jnp.bfloat16),
             pltpu.VMEM((2 * rows, DEGREES + HALF), jnp.float32),
             pltpu.VMEM((2 * rows, HALF), jnp.float32),
             pltpu.VMEM((2 * rows, HALF), jnp.bfloat16),
             pltpu.VMEM((4 * rows, HALF), jnp.bfloat16),
             pltpu.VMEM((32, rows * SLOTS, LANES), jnp.float32),
+            pltpu.SemaphoreType.DMA((PAIRS,)),
         ],
-        compiler_params=pltpu.CompilerParams(vmem_limit_bytes=SMALL_LIMIT),
+        compiler_params=pltpu.CompilerParams(vmem_limit_bytes=MIDDLE_LIMIT),
         cost_estimate=pl.CostEstimate(
             flops=12 * rows * PAIRS * DEGREES * DEGREES,
             bytes_accessed=4 * own.size + 16 * rows * PAIRS * DEGREES + 64 * rows * SLOTS * LANES,
             transcendentals=0,
         ),
         name="synthesis",
-    )(scalars, *(in_vmem(value) for value in (coeffs, last, factors, own, other)))
+    )(scalars, *(in_vmem(value) for value in (coeffs, last, factors)), in_hbm(own), in_vmem(other))
 
 
 def unpack_kernel(
@@ -610,7 +632,7 @@
         scalars, arrived, edges, turned(legendre), turned(other_legendre), rows
     )
     spectra = exchange(moments.reshape(devices // 2, 2 * SLOTS, LANES), SAME_CORE)
-    factors = exchange(factors_of(spectra, rows), SAME_CORE).reshape(DEGREES, LANES)
+    factors = exchange(factors_of(spectra, rows), SAME_CORE)
     going = synthesis(scalars, coeffs, last, factors, legendre, other_legendre, rows)
     returned = exchange(going.reshape(devices, rows * 2, LANES), DEVICES)
     returned = returned.reshape(16, 2, 4, rows * 2, LANES)

time: 181 us -> 182 us (level)
    unnamed x15 -> x5, local copies, waits for them, and re-layouts: 9.55 us -> 9.5 us
where the time goes in v7:
time: 182 us; the launch traced here: 180 us
  blocking collectives  74 us (41%)
  Pallas kernels  56.7 us (31%)
  local copies, waits for them, and re-layouts  20.5 us (11%)
  waiting for transfers between devices  16.9 us (9%)
  starting transfers between devices  12 us (7%)
    all_to_all x3, blocking collectives, exchange(): return lax.all_to_all(values, axes, split_axis=0, concat_axis=0, tiled=True)  74 us
    pallas_call x2, Pallas kernels, turned(): pl.pallas_call(turn_kernel, grid=(pairs, DEGREES // width), in_specs=[pl....  26.4 us
    all_to_all x1, waiting for transfers between devices, exchange(): return lax.all_to_all(values, axes, split_axis=0, concat_axis=0, tiled=True)  16.9 us
    pallas_call x1, Pallas kernels, analysis(): pl.pallas_call(functools.partial(analysis_kernel, rows), in_specs=[pl.Blo...  12.4 us
    all_to_all x1, starting transfers between devices, exchange(): return lax.all_to_all(values, axes, split_axis=0, concat_axis=0, tiled=True)  10.6 us
    ppermute x1, local copies, waits for them, and re-layouts, per_device(): other_legendre = lax.ppermute(legendre, 'core', [(0, 1), (1, 0)])  9.51 us
    unnamed x5, local copies, waits for them, and re-layouts  9.5 us
    pallas_call x1, Pallas kernels, synthesis(): pl.pallas_call(functools.partial(synthesis_kernel, rows), in_specs=[pl.Bl...  7.5 us
  transfers between devices with their start and end apart: 2, of which 1 were waited for; matrix products, arithmetic and copies ran while one was open for 11% of the time, Pallas kernels for 18%

profile of v7, /device:TPU:1, one launch (start us, length us, event | category | flops | bytes accessed | tf_op | source)
XLA Modules:
  0.0 180.4 jit_solution(11490152718996941725)
XLA Ops:
  0.0 1.4 collective-permute-start
  1.4 6.4 %pack.1 = bf16[16,2,4,10,16,128]{5,4,3,2,1,0:T(8,128)(2,1)} custom-call(s32[1]{0:T(128)} %bitcast.turn_ref, s32[1,512]{1,0:T(1,128)} %bitcast.18, bf16[10,4,32,1024]{3,2,1,0:T(8,128)(2,1)} %bitcast.21, bf16[10,4,32,1024]{3,2,1,0:T(8,128)(2,1)} %bitcast.22), custom_call_target="tpu_custom_call" | custom-call | flops 2684354560 | bytes 10485760 | tf_op jit(solution)/shard_map/pack/pallas_call | solution.py:123
  7.8 10.6 %all-to-all-start = ((bf16[128,160,128]{2,1,0:T(8,128)(2,1)}), bf16[128,160,128]{2,1,0:T(8,128)(2,1)}, u32[]{:S(2)}, u32[]{:S(2)}) async-start(bf16[128,160,128]{2,1,0:T(8,128)(2,1)} %bitcast.20), calls=%async_computation | async-start | bytes 10485760 | tf_op jit(solution)/shard_map/all_to_all | solution.py:611
  18.4 9.5 %copy.11.leg_ref.own_hbm = bf16[4,1025,1024]{2,1,0:T(8,128)(2,1)} copy(bf16[4,1025,1024]{2,0,1:T(4,128)(2,1)} %param.6) | data formatting | bytes 16793600 | tf_op args[2]
  27.9 0.0 copy-start.1
  27.9 13.2 %turned.2.own_hbm = bf16[4,1024,1024]{2,1,0:T(8,128)(2,1)} custom-call(bf16[4,1025,1024]{2,1,0:T(8,128)(2,1)} %copy.11.leg_ref.own_hbm), custom_call_target="tpu_custom_call" | custom-call | bytes 16793600 | tf_op jit(solution)/shard_map/turned/pallas_call | solution.py:316
  41.1 0.0 copy-done.1
  41.1 0.1 fusion
  41.2 0.1 pad_add_fusion.scalar_ref
  41.3 0.7 slice_bitcast_fusion.1
  42.0 0.0 collective-permute-done
  42.0 9.5 %copy.12.leg_ref.other_ref = bf16[4,1025,1024]{2,1,0:T(8,128)(2,1)} copy(bf16[4,1025,1024]{2,0,1:T(4,128)(2,1)} %collective-permute-done) | data formatting | bytes 16793600 | tf_op jit(solution)/shard_map/ppermute | solution.py:622
  51.5 13.2 %turned.3.other_hbm = bf16[4,1024,1024]{2,1,0:T(8,128)(2,1)} custom-call(bf16[4,1025,1024]{2,1,0:T(8,128)(2,1)} %copy.12.leg_ref.other_ref), custom_call_target="tpu_custom_call" | custom-call | bytes 16793600 | tf_op jit(solution)/shard_map/turned/pallas_call | solution.py:316
  64.7 0.7 slice_bitcast_fusion
  65.4 16.9 %all-to-all-done = bf16[128,160,128]{2,1,0:T(8,128)(2,1)} async-done(((bf16[128,160,128]{2,1,0:T(8,128)(2,1)}), bf16[128,160,128]{2,1,0:T(8,128)(2,1)}, u32[]{:S(2)}, u32[]{:S(2)}) %all-to-all-start) | async-done | bytes 5242912 | tf_op jit(solution)/shard_map/all_to_all | solution.py:611
  82.4 0.0 copy-start
  82.4 12.4 %analysis.1 = (f32[8,160,1024]{2,1,0:T(8,128)S(1)}, f32[8,160,128]{2,1,0:T(8,128)S(1)}, f32[1024,128]{1,0:T(8,128)S(1)}) custom-call(s32[9]{0:T(128)S(1)} %pad_add_fusion.scalar_ref, bf16[32,4,160,128]{3,2,1,0:T(8,128)(2,1)} %bitcast.6.arrived_ref, f32[8,1024]{1,0:T(8,128)S(1)} %maximum_convert_fusion.edge_ref, bf16[4,1024,1024]{2,1,0:T(8,128)(2,1)} %turned.2.own_hbm, ...), custom_call_target="tpu_custom_call" | custom-call | flops 3355443200 | bytes 24641536 | tf_op jit(solution)/shard_map/analysis/pallas_call | solution.py:333
  94.8 16.7 %all_to_all.20.parts_ref = f32[64,16,128]{2,1,0:T(8,128)S(1)} all-to-all(f32[64,16,128]{2,1,0:T(8,128)S(1)} %bitcast.17), channel_id=1, replica_groups=mesh['zx'=16,'core'=2,'col'=4] {'zx','col'}, dimensions={0} | all-to-all | bytes 1048576 | tf_op jit(solution)/shard_map/all_to_all | solution.py:611
  111.5 0.3 factors.1
  111.8 14.2 %all_to_all.21.factor_ref = f32[64,2,640]{2,1,0:T(2,128)S(1)} all-to-all(f32[64,2,640]{2,1,0:T(2,128)S(1)} %factors.1), channel_id=1, replica_groups=mesh['zx'=16,'core'=2,'col'=4] {'zx','col'}, dimensions={0} | all-to-all | bytes 655360 | tf_op jit(solution)/shard_map/all_to_all | solution.py:611
  126.0 0.0 copy-done
  126.0 7.5 %synthesis.1 = bf16[32,320,128]{2,1,0:T(8,128)(2,1)S(1)} custom-call(s32[9]{0:T(128)S(1)} %pad_add_fusion.scalar_ref, f32[8,160,1024]{2,1,0:T(8,128)S(1)} %get-tuple-element.8.coef_ref, f32[8,160,128]{2,1,0:T(8,128)S(1)} %get-tuple-element.9.last_ref, f32[64,2,640]{2,1,0:T(2,128)S(1)} %all_to_all.21.factor_ref, bf16[4,1025,1024]{2,1,0:T(8,128)(2,1)} %copy.11.leg_ref.own_hbm, ...), custom_call_target="tpu_custom_call" | custom-call | flops 2013265920 | bytes 22036480 | tf_op jit(solution)/shard_map/synthesis/pallas_call | solution.py:521
  133.5 43.0 %all_to_all.22 = bf16[128,80,128]{2,1,0:T(8,128)(2,1)S(1)} all-to-all(bf16[128,80,128]{2,1,0:T(8,128)(2,1)S(1)} %bitcast.16), channel_id=1, replica_groups=mesh['zx'=16,'core'=2,'col'=4] {'zx','core','col'}, dimensions={0} | all-to-all | bytes 5242880 | tf_op jit(solution)/shard_map/all_to_all | solution.py:611
  176.6 3.7 %unpack.1 = bf16[10,4,32,1024]{3,2,1,0:T(8,128)(2,1)} custom-call(s32[1]{0:T(128)} %bitcast.turn_ref, s32[1,512]{1,0:T(1,128)S(1)} %bitcast.19, bf16[16,2,4,80,128]{4,3,2,1,0:T(8,128)(2,1)S(1)} %bitcast.15), custom_call_target="tpu_custom_call" | custom-call | flops 1342177280 | bytes 5242880 | tf_op jit(solution)/shard_map/unpack/pallas_call | solution.py:589
  (1 shorter events, 0.0 us)
Async XLA Ops:
  0.0 42.0 %collective-permute-start = (bf16[4,1025,1024]{2,0,1:T(4,128)(2,1)}, bf16[4,1025,1024]{2,0,1:T(4,128)(2,1)}, u32[]{:S(2)}, u32[]{:S(2)}) collective-permute-start(bf16[4,1025,1024]{2,0,1:T(4,128)(2,1)} %param.6), channel_id=1, source_target_pairs={{0,4},{4,0},{1,5},{5,1},{2,6},{6,2},{3,7},{7,3},{8,12},{12,8},{9,1... | collective-permute-start | bytes 25190408 | tf_op jit(solution)/shard_map/ppermute | solution.py:622
  7.8 74.6 %all-to-all-start = ((bf16[128,160,128]{2,1,0:T(8,128)(2,1)}), bf16[128,160,128]{2,1,0:T(8,128)(2,1)}, u32[]{:S(2)}, u32[]{:S(2)}) async-start(bf16[128,160,128]{2,1,0:T(8,128)(2,1)} %bitcast.20), calls=%async_computation | async-start | bytes 10485760 | tf_op jit(solution)/shard_map/all_to_all | solution.py:611
  27.9 13.2 %copy-start.1 = (s32[512]{0:T(512)S(1)}, s32[512]{0:T(512)}, u32[]{:S(2)}) copy-start(s32[512]{0:T(512)} %param.7) | copy-start | bytes 6148
  82.4 43.7 %copy-start = (bf16[4,1025,1024]{2,1,0:T(8,128)(2,1)S(1)}, bf16[4,1025,1024]{2,1,0:T(8,128)(2,1)}, u32[]{:S(2)}) copy-start(bf16[4,1025,1024]{2,1,0:T(8,128)(2,1)} %copy.12.leg_ref.other_ref) | copy-start | bytes 25190404

commit v8 on v6

--- a/solution.py
+++ b/solution.py
@@ -523,9 +523,8 @@
 
 
 def unpack_kernel(
-    channels, turn_ref, pairs_ref, returned_ref, out_hbm, out_ref, lower_ref, upper_ref, sems
+    channels, turn_ref, lower_ref, upper_ref, returned_ref, out_hbm, out_ref, sems
 ):
-    one_hots(pairs_ref, lower_ref, upper_ref)
     turn = turn_ref[0]
 
     def send(i):
@@ -562,17 +561,25 @@
         send(i).wait()
 
 
-def unpack(turn, pairs, returned, channels):
+def both_one_hots(pairs):
+    return pl.pallas_call(
+        one_hots,
+        out_shape=[pltpu.HBM((HALF, HALF), jnp.bfloat16)] * 2,
+        compiler_params=pltpu.CompilerParams(vmem_limit_bytes=SMALL_LIMIT),
+        cost_estimate=pl.CostEstimate(flops=0, bytes_accessed=4 * HALF * HALF, transcendentals=0),
+        name="one_hots",
+    )(pairs)
+
+
+def unpack(turn, lower, upper, returned, channels):
     whole = pl.BlockSpec(memory_space=pltpu.VMEM)
     return pl.pallas_call(
         functools.partial(unpack_kernel, channels),
-        in_specs=[pl.BlockSpec(memory_space=pltpu.SMEM), whole, whole],
+        in_specs=[pl.BlockSpec(memory_space=pltpu.SMEM), whole, whole, whole],
         out_specs=pl.BlockSpec(memory_space=pltpu.HBM),
         out_shape=pltpu.HBM((channels, 4, 32, DEGREES), jnp.bfloat16),
         scratch_shapes=[
             pltpu.VMEM((channels, 4, 32, DEGREES), jnp.bfloat16),
-            pltpu.VMEM((HALF, HALF), jnp.bfloat16),
-            pltpu.VMEM((HALF, HALF), jnp.bfloat16),
             pltpu.SemaphoreType.DMA((channels // 2,)),
         ],
         compiler_params=pltpu.CompilerParams(vmem_limit_bytes=KERNEL_LIMIT),
@@ -582,7 +589,7 @@
             transcendentals=0,
         ),
         name="unpack",
-    )(turn, pairs, in_vmem(returned))
+    )(turn, in_vmem(lower), in_vmem(upper), in_vmem(returned))
 
 
 def exchange(values, axes):
@@ -606,15 +613,18 @@
     packed = pack(turn, pair_row, pred_four.reshape(by_group), target_four.reshape(by_group))
     arrived = exchange(packed.reshape(devices, rows * 4, LANES), DEVICES)
     edges = jnp.concatenate([legendre[:, DEGREES], other_legendre[:, DEGREES]]).astype(jnp.float32)
+    own_turned = turned(legendre)
+    late_row, own_turned = lax.optimization_barrier((pair_row, own_turned))
+    lower_hot, upper_hot = both_one_hots(late_row)
     coeffs, last, moments = analysis(
-        scalars, arrived, edges, turned(legendre), turned(other_legendre), rows
+        scalars, arrived, edges, own_turned, turned(other_legendre), rows
     )
     spectra = exchange(moments.reshape(devices // 2, 2 * SLOTS, LANES), SAME_CORE)
     factors = exchange(factors_of(spectra, rows), SAME_CORE).reshape(DEGREES, LANES)
     going = synthesis(scalars, coeffs, last, factors, legendre, other_legendre, rows)
     returned = exchange(going.reshape(devices, rows * 2, LANES), DEVICES)
     returned = returned.reshape(16, 2, 4, rows * 2, LANES)
-    return unpack(turn, pair_row, returned, channels).reshape(pred_four.shape)
+    return unpack(turn, lower_hot, upper_hot, returned, channels).reshape(pred_four.shape)
 
 
 def solution(mesh):

time: 181 us -> 185 us (1.022)
  blocking collectives: 74.8 us -> 32 us
  waiting for transfers between devices: 16.9 us -> 51.9 us
  starting transfers between devices: 12 us -> 19.1 us
  local copies, waits for them, and re-layouts: 20.5 us -> 24.1 us
    all_to_all x3 -> x2, blocking collectives: 74.8 us -> 32 us  [exchange(): return lax.all_to_all(values, axes, split_axis=0, concat_axis=0, tiled=True)]
    all_to_all x1 -> x2, waiting for transfers between devices: 16.9 us -> 51.9 us  [exchange(): return lax.all_to_all(values, axes, split_axis=0, concat_axis=0, tiled=True)]
    all_to_all x1 -> x2, starting transfers between devices: 10.6 us -> 17.7 us  [exchange(): return lax.all_to_all(values, axes, split_axis=0, concat_axis=0, tiled=True)]
    unnamed x15 -> x21, local copies, waits for them, and re-layouts: 9.55 us -> 13.1 us
  transfers between devices with their start and end apart: 2 -> 3, of which waited for: 1 -> 2; matrix products, arithmetic and copies ran while one was open for 11% -> 11% of each run, Pallas kernels for 18% -> 19%
where the time goes in v8:
time: 185 us; the launch traced here: 184 us
  Pallas kernels  56.4 us (30%)
  waiting for transfers between devices  51.9 us (28%)
  blocking collectives  32 us (17%)
  local copies, waits for them, and re-layouts  24.1 us (13%)
  starting transfers between devices  19.1 us (10%)
    all_to_all x2, waiting for transfers between devices, exchange(): return lax.all_to_all(values, axes, split_axis=0, concat_axis=0, tiled=True)  51.9 us
    all_to_all x2, blocking collectives, exchange(): return lax.all_to_all(values, axes, split_axis=0, concat_axis=0, tiled=True)  32 us
    pallas_call x2, Pallas kernels, turned(): pl.pallas_call(turn_kernel, grid=(pairs, DEGREES // width), in_specs=[pl....  26.4 us
    all_to_all x2, starting transfers between devices, exchange(): return lax.all_to_all(values, axes, split_axis=0, concat_axis=0, tiled=True)  17.7 us
    unnamed x21, local copies, waits for them, and re-layouts  13.1 us
    pallas_call x1, Pallas kernels, analysis(): pl.pallas_call(functools.partial(analysis_kernel, rows), in_specs=[pl.Blo...  12.6 us
    ppermute x1, local copies, waits for them, and re-layouts, per_device(): other_legendre = lax.ppermute(legendre, 'core', [(0, 1), (1, 0)])  9.5 us
    pallas_call x1, Pallas kernels, pack(): pl.pallas_call(functools.partial(pack_kernel, channels), in_specs=[pl.Blo...  6.4 us
  transfers between devices with their start and end apart: 3, of which 2 were waited for; matrix products, arithmetic and copies ran while one was open for 11% of the time, Pallas kernels for 19%

profile of v8, /device:TPU:1, one launch (start us, length us, event | category | flops | bytes accessed | tf_op | source)
XLA Modules:
  0.0 183.9 jit_solution(16479252761154386025)
XLA Ops:
  0.0 1.4 collective-permute-start
  1.4 6.4 %pack.1 = bf16[16,2,4,10,16,128]{5,4,3,2,1,0:T(8,128)(2,1)} custom-call(s32[1]{0:T(128)} %bitcast.turn_ref, s32[1,512]{1,0:T(1,128)} %bitcast.24, bf16[10,4,32,1024]{3,2,1,0:T(8,128)(2,1)} %bitcast.27, bf16[10,4,32,1024]{3,2,1,0:T(8,128)(2,1)} %bitcast.28), custom_call_target="tpu_custom_call" | custom-call | flops 2684354560 | bytes 10485760 | tf_op jit(solution)/shard_map/pack/pallas_call | solution.py:122
  7.8 10.6 %all-to-all-start = ((bf16[128,160,128]{2,1,0:T(8,128)(2,1)}), bf16[128,160,128]{2,1,0:T(8,128)(2,1)}, u32[]{:S(2)}, u32[]{:S(2)}) async-start(bf16[128,160,128]{2,1,0:T(8,128)(2,1)} %bitcast.26), calls=%async_computation | async-start | bytes 10485760 | tf_op jit(solution)/shard_map/all_to_all | solution.py:596
  18.5 9.5 %copy.11.leg_ref.own_ref = bf16[4,1025,1024]{2,1,0:T(8,128)(2,1)} copy(bf16[4,1025,1024]{2,0,1:T(4,128)(2,1)} %param.6) | data formatting | bytes 16793600 | tf_op args[2]
  28.0 13.2 %turned.2.own_hbm = bf16[4,1024,1024]{2,1,0:T(8,128)(2,1)} custom-call(bf16[4,1025,1024]{2,1,0:T(8,128)(2,1)} %copy.11.leg_ref.own_ref), custom_call_target="tpu_custom_call" | custom-call | bytes 16793600 | tf_op jit(solution)/shard_map/turned/pallas_call | solution.py:313
  41.2 0.0 copy-done.3
  41.2 0.1 fusion
  41.3 0.1 pad_add_fusion.scalar_ref
  41.4 0.7 slice_bitcast_fusion.1
  42.1 0.0 collective-permute-done
  42.1 9.5 %copy.12.leg_ref.other_ref = bf16[4,1025,1024]{2,1,0:T(8,128)(2,1)} copy(bf16[4,1025,1024]{2,0,1:T(4,128)(2,1)} %collective-permute-done) | data formatting | bytes 16793600 | tf_op jit(solution)/shard_map/ppermute | solution.py:607
  51.6 13.2 %turned.3.other_hbm = bf16[4,1024,1024]{2,1,0:T(8,128)(2,1)} custom-call(bf16[4,1025,1024]{2,1,0:T(8,128)(2,1)} %copy.12.leg_ref.other_ref), custom_call_target="tpu_custom_call" | custom-call | bytes 16793600 | tf_op jit(solution)/shard_map/turned/pallas_call | solution.py:313
  64.8 0.7 slice_bitcast_fusion
  65.5 16.9 %all-to-all-done = bf16[128,160,128]{2,1,0:T(8,128)(2,1)} async-done(((bf16[128,160,128]{2,1,0:T(8,128)(2,1)}), bf16[128,160,128]{2,1,0:T(8,128)(2,1)}, u32[]{:S(2)}, u32[]{:S(2)}) %all-to-all-start) | async-done | bytes 5242912 | tf_op jit(solution)/shard_map/all_to_all | solution.py:596
  82.4 0.0 slice-start.4
  82.4 0.0 slice-start.5
  82.4 12.6 %analysis.1 = (f32[8,160,1024]{2,1,0:T(8,128)S(1)}, f32[8,160,128]{2,1,0:T(8,128)S(1)}, f32[1024,128]{1,0:T(8,128)S(1)}) custom-call(s32[9]{0:T(128)S(1)} %pad_add_fusion.scalar_ref, bf16[32,4,160,128]{3,2,1,0:T(8,128)(2,1)} %bitcast.6.arrived_ref, f32[8,1024]{1,0:T(8,128)S(1)} %maximum_convert_fusion.edge_ref, bf16[4,1024,1024]{2,1,0:T(8,128)(2,1)} %turned.2.own_hbm, ...), custom_call_target="tpu_custom_call" | custom-call | flops 3355443200 | bytes 24641536 | tf_op jit(solution)/shard_map/analysis/pallas_call | solution.py:330
  95.1 16.8 %all_to_all.20.parts_ref = f32[64,16,128]{2,1,0:T(8,128)S(1)} all-to-all(f32[64,16,128]{2,1,0:T(8,128)S(1)} %bitcast.23), channel_id=1, replica_groups=mesh['zx'=16,'core'=2,'col'=4] {'zx','col'}, dimensions={0} | all-to-all | bytes 1048576 | tf_op jit(solution)/shard_map/all_to_all | solution.py:596
  111.8 0.2 factors.1
  112.1 15.2 %all_to_all.21 = f32[64,16,128]{2,1,0:T(8,128)S(1)} all-to-all(f32[64,16,128]{2,1,0:T(8,128)S(1)} %factors.1), channel_id=1, replica_groups=mesh['zx'=16,'core'=2,'col'=4] {'zx','col'}, dimensions={0} | all-to-all | bytes 1048576 | tf_op jit(solution)/shard_map/all_to_all | solution.py:596
  127.4 0.0 slice-done.1
  127.4 0.0 slice-done.2
  127.4 0.0 slice-done.4
  127.4 6.1 %synthesis.1 = bf16[32,320,128]{2,1,0:T(8,128)(2,1)S(1)} custom-call(s32[9]{0:T(128)S(1)} %pad_add_fusion.scalar_ref, f32[8,160,1024]{2,1,0:T(8,128)S(1)} %get-tuple-element.16.coef_ref, f32[8,160,128]{2,1,0:T(8,128)S(1)} %get-tuple-element.17.last_ref, f32[1024,128]{1,0:T(8,128)S(1)} %bitcast.22, bf16[4,1025,1024]{2,1,0:T(8,128)(2,1)S(1)} %bitcast.17, ...), custom_call_target="tpu_custom_call" | custom-call | flops 2013265920 | bytes 22036480 | tf_op jit(solution)/shard_map/synthesis/pallas_call | solution.py:503
  133.6 0.0 copy-start
  133.6 1.5 copy-done
  135.0 7.0 %all-to-all-start.3 = ((bf16[128,80,128]{2,1,0:T(8,128)(2,1)}), bf16[128,80,128]{2,1,0:T(8,128)(2,1)S(1)}, u32[]{:S(2)}, u32[]{:S(2)}) async-start(bf16[128,80,128]{2,1,0:T(8,128)(2,1)} %bitcast.21), calls=%async_computation.3 | async-start | bytes 5242880 | tf_op jit(solution)/shard_map/all_to_all | solution.py:596
  142.1 1.3 one_hots.1
  143.4 35.0 %all-to-all-done.3 = bf16[128,80,128]{2,1,0:T(8,128)(2,1)S(1)} async-done(((bf16[128,80,128]{2,1,0:T(8,128)(2,1)}), bf16[128,80,128]{2,1,0:T(8,128)(2,1)S(1)}, u32[]{:S(2)}, u32[]{:S(2)}) %all-to-all-start.3) | async-done | bytes 2621472 | tf_op jit(solution)/shard_map/all_to_all | solution.py:596
  178.4 1.0 copy-done.1
  179.4 1.0 copy-done.2
  180.5 3.3 %unpack.1 = bf16[10,4,32,1024]{3,2,1,0:T(8,128)(2,1)} custom-call(s32[1]{0:T(128)} %bitcast.turn_ref, bf16[512,512]{1,0:T(8,128)(2,1)S(1)} %copy-done.1, bf16[512,512]{1,0:T(8,128)(2,1)S(1)} %copy-done.2, bf16[16,2,4,80,128]{4,3,2,1,0:T(8,128)(2,1)S(1)} %bitcast.20), custom_call_target="tpu_custom_call" | custom-call | flops 1342177280 | bytes 5242880 | tf_op jit(solution)/shard_map/unpack/pallas_call | solution.py:576
  (13 shorter events, 0.0 us)
Async XLA Ops:
  0.0 42.1 %collective-permute-start = (bf16[4,1025,1024]{2,0,1:T(4,128)(2,1)}, bf16[4,1025,1024]{2,0,1:T(4,128)(2,1)}, u32[]{:S(2)}, u32[]{:S(2)}) collective-permute-start(bf16[4,1025,1024]{2,0,1:T(4,128)(2,1)} %param.6), channel_id=1, source_target_pairs={{0,4},{4,0},{1,5},{5,1},{2,6},{6,2},{3,7},{7,3},{8,12},{12,8},{9,1... | collective-permute-start | bytes 25190408 | tf_op jit(solution)/shard_map/ppermute | solution.py:607
  7.8 74.6 %all-to-all-start = ((bf16[128,160,128]{2,1,0:T(8,128)(2,1)}), bf16[128,160,128]{2,1,0:T(8,128)(2,1)}, u32[]{:S(2)}, u32[]{:S(2)}) async-start(bf16[128,160,128]{2,1,0:T(8,128)(2,1)} %bitcast.26), calls=%async_computation | async-start | bytes 10485760 | tf_op jit(solution)/shard_map/all_to_all | solution.py:596
  28.0 13.2 %copy-start.3 = (s32[512]{0:T(512)S(1)}, s32[512]{0:T(512)}, u32[]{:S(2)}) copy-start(s32[512]{0:T(512)} %param.7) | copy-start | bytes 6148
  82.4 45.0 %slice-start = ((s8[8454144]{0:T(1024)(128)(4,1)}), s8[4194304]{0:T(1024)(128)(4,1)S(1)}, s32[]{:S(2)}) async-start(s8[8454144]{0:T(1024)(128)(4,1)} %bitcast.16), calls=%async_computation.4 | async-start | bytes 8388608
  82.4 45.0 %slice-start.3 = ((s8[8454144]{0:T(1024)(128)(4,1)}), s8[4194304]{0:T(1024)(128)(4,1)S(1)}, s32[]{:S(2)}) async-start(s8[8454144]{0:T(1024)(128)(4,1)} %bitcast.18), calls=%async_computation.7 | async-start | bytes 8388608
  82.4 45.0 %slice-start.1 = ((s8[8454144]{0:T(1024)(128)(4,1)}), s8[4194304]{0:T(1024)(128)(4,1)S(1)}, s32[]{:S(2)}) async-start(s8[8454144]{0:T(1024)(128)(4,1)} %bitcast.16), calls=%async_computation.5 | async-start | bytes 8388608
  82.4 45.0 %slice-start.2 = ((s8[8454144]{0:T(1024)(128)(4,1)}), s8[65536]{0:T(1024)(128)(4,1)S(1)}, s32[]{:S(2)}) async-start(s8[8454144]{0:T(1024)(128)(4,1)} %bitcast.16), calls=%async_computation.6 | async-start | bytes 131072
  82.4 45.0 %slice-start.4 = ((s8[8454144]{0:T(1024)(128)(4,1)}), s8[4194304]{0:T(1024)(128)(4,1)S(1)}, s32[]{:S(2)}) async-start(s8[8454144]{0:T(1024)(128)(4,1)} %bitcast.18), calls=%async_computation.8 | async-start | bytes 8388608
  82.4 45.0 %slice-start.5 = ((s8[8454144]{0:T(1024)(128)(4,1)}), s8[65536]{0:T(1024)(128)(4,1)S(1)}, s32[]{:S(2)}) async-start(s8[8454144]{0:T(1024)(128)(4,1)} %bitcast.18), calls=%async_computation.9 | async-start | bytes 131072
  133.6 1.5 copy-start
  135.0 43.3 %all-to-all-start.3 = ((bf16[128,80,128]{2,1,0:T(8,128)(2,1)}), bf16[128,80,128]{2,1,0:T(8,128)(2,1)S(1)}, u32[]{:S(2)}, u32[]{:S(2)}) async-start(bf16[128,80,128]{2,1,0:T(8,128)(2,1)} %bitcast.21), calls=%async_computation.3 | async-start | bytes 5242880 | tf_op jit(solution)/shard_map/all_to_all | solution.py:596
  178.4 1.0 copy-start.1
  179.4 1.0 copy-start.2
